TPU v7x, 32 devices: a whole 2x2x4 slice. The times are simulated.
32 devices in a mesh: ka: 16 (over z, x, core), ga: 2 (over y).
Axes of the slice: x: 2, y: 2, z: 4, core: 2. Of those that a mesh axis runs over, the one named last changes fastest.
Arguments:
- row_orbitals: bfloat16 [4, 32, 4096], replicated, may hold values from -6 to 6
- orbitals: bfloat16 [64, 32, 4096], P('ka'), may hold values from -6 to 6
- screening: bfloat16 [1152, 304, 304], P('ka', None, 'ga'), may hold values from -0.3125 to 0.3125
- pair_blocks: int32 [64, 4], replicated, may hold values from 0 to 1151, as said below
- row_vectors: bfloat16 [4, 4, 256], replicated, may hold values from -6 to 6
- vectors: bfloat16 [4, 64, 256], P(None, 'ka'), may hold values from -6 to 6
Outputs:
- row_image: float32 [4, 4, 256], replicated
- column_image: float32 [4, 64, 256], P(None, 'ka')
Inputs may be any that keep to these rules, and one draw needn't show every extreme that they name: `pair_blocks`: block q lies on index q // 72 of ka. In each aligned block of 4 rows (all 4 columns), at most 2 entries share one value of q // 72, and exactly 2 do for some value.
All inputs are finite; a program needn't handle non-finite values.
Results may differ from a plain program's by a relative error of at most 0.0081.
Values may be sent and summed in bfloat16 or wider, within the bound.
No kernel may reach another device: no remote copies, remote signals or barrier semaphores. Data moves between devices by JAX's collectives and lax.ppermute only.
A program may use at most 128 MiB of HBM per device.

v0:
```python
import math

import jax
import jax.numpy as jnp
from jax import lax
from jax.sharding import PartitionSpec as P

NV = 16
NC = 16
CAP = 2


def plane_rows(first, count, grid):
    wave = (first + lax.iota(jnp.int32, count))[:, None]
    point = lax.iota(jnp.int32, grid)[None, :]
    phase = (wave * point % grid).astype(jnp.float32) * (2.0 * math.pi / grid)
    return math.sqrt(2.0 / grid) * jnp.cos(phase)


def densities_one(plane, row_bands, orbitals, lower, upper):
    grid = orbitals.shape[2]
    band_count = upper - lower
    weighted = (plane[:, None, :] * row_bands[lower:upper].astype(jnp.float32)[None]).astype(
        jnp.bfloat16
    )
    product = lax.dot_general(
        weighted.reshape(-1, grid),
        orbitals[:, lower:upper].reshape(-1, grid),
        (((1,), (1,)), ((), ())),
        preferred_element_type=jnp.float32,
    )
    product = product.reshape(plane.shape[0], band_count, orbitals.shape[0], band_count)
    return product.transpose(2, 0, 1, 3).astype(jnp.bfloat16)


def on_device(row_orbitals, orbitals, screening, pair_blocks, row_vectors, vectors):
    ka_count = lax.axis_size("ka")
    my_point = lax.axis_index("ka")
    my_slice = lax.axis_index("ga")
    row_count = row_orbitals.shape[0]
    point_local = orbitals.shape[0]
    block_local, wave_count, slice_width = screening.shape
    pair_count = point_local * row_count
    vec_count = vectors.shape[0]
    table = pair_blocks.reshape(ka_count, pair_count)
    owner = table // block_local
    block_index = table % block_local
    pair_iota = lax.iota(jnp.int32, pair_count)
    earlier = pair_iota[None, :] < pair_iota[:, None]
    same_owner = (owner[:, :, None] == owner[:, None, :]) & earlier[None]
    slot_rank = jnp.sum(same_owner.astype(jnp.int32), axis=2)
    mine = owner == my_point
    slot_hot = mine[:, :, None] & (slot_rank[:, :, None] == lax.iota(jnp.int32, CAP)[None, None, :])
    block_hot = block_index[:, :, None] == lax.iota(jnp.int32, block_local)[None, None, :]
    select = jnp.einsum(
        "dps,dpq->dsq",
        slot_hot.astype(jnp.bfloat16),
        block_hot.astype(jnp.bfloat16),
        preferred_element_type=jnp.float32,
    )
    outgoing = jnp.dot(
        select.reshape(ka_count * CAP, block_local).astype(jnp.bfloat16),
        screening.reshape(block_local, wave_count * slice_width),
        preferred_element_type=jnp.float32,
    ).astype(jnp.bfloat16)
    outgoing = outgoing.reshape(ka_count, CAP, wave_count, slice_width)
    my_owner = lax.dynamic_index_in_dim(owner, my_point, 0, keepdims=False)
    my_rank = lax.dynamic_index_in_dim(slot_rank, my_point, 0, keepdims=False)
    position = my_owner * CAP + my_rank
    plane = plane_rows(my_slice * slice_width, slice_width, orbitals.shape[2])
    cond = jnp.stack(
        [
            densities_one(plane, row_orbitals[row_index], orbitals, NV, NV + NC)
            for row_index in range(row_count)
        ],
        axis=1,
    )
    vale = jnp.stack(
        [
            densities_one(plane, row_orbitals[row_index], orbitals, 0, NV)
            for row_index in range(row_count)
        ],
        axis=1,
    )
    vale_flat = vale.reshape(pair_count, slice_width, NV * NV)
    incoming = lax.all_to_all(outgoing, "ka", split_axis=0, concat_axis=0, tiled=True)
    chosen = jnp.take(incoming.reshape(ka_count * CAP, wave_count, slice_width), position, axis=0)
    summed = lax.psum_scatter(
        jnp.einsum("pgh,phx->gpx", chosen, vale_flat, preferred_element_type=jnp.float32),
        "ga",
        scatter_dimension=0,
        tiled=True,
    )
    screened = summed.transpose(1, 0, 2).astype(jnp.bfloat16)
    screened = screened.reshape(point_local, row_count, slice_width, NV, NV)
    vec_local = vectors.reshape(vec_count, point_local, NV, NC)
    vec_row = row_vectors.reshape(vec_count, row_count, NV, NC)
    first = jnp.einsum(
        "bagcd,nbvd->bagcvn", cond, vec_local, preferred_element_type=jnp.float32
    ).astype(jnp.bfloat16)
    row_part = jnp.einsum("bagvw,bagcwn->navc", screened, first, preferred_element_type=jnp.float32)
    second = jnp.einsum(
        "bagcd,navc->bagdvn", cond, vec_row, preferred_element_type=jnp.float32
    ).astype(jnp.bfloat16)
    column_part = jnp.einsum(
        "bagvw,bagdvn->nbwd", screened, second, preferred_element_type=jnp.float32
    )
    row_part = row_part.reshape(vec_count, row_count, NV * NC)
    column_part = column_part.reshape(vec_count, point_local, NV * NC)
    row_total = lax.psum(row_part, ("ka", "ga"))
    column_total = lax.psum(column_part, "ga")
    row_scale = float(wave_count * NV * NC * point_local * ka_count) ** (-0.5)
    column_scale = float(wave_count * NV * NC * row_count) ** (-0.5)
    return (row_total * row_scale, column_total * column_scale)


def solution(mesh):
    return jax.shard_map(
        on_device,
        mesh=mesh,
        in_specs=(P(), P("ka", None, None), P("ka", None, "ga"), P(), P(), P(None, "ka", None)),
        out_specs=(P(), P(None, "ka", None)),
        check_vma=False,
    )
```

profile of v0, /device:TPU:0, one launch (start us, length us, event | category | flops | bytes accessed | tf_op | source)
XLA Modules:
  0.0 352.4 jit_solution(9296001494615573782)
XLA Ops:
  7.2 0.7 broadcast_divide_fusion
  7.9 0.7 sign_compare_fusion
  8.9 0.1 copy.50
  9.1 14.0 %copy.53 = bf16[72,304,152]{2,1,0:T(8,128)(2,1)} copy(bf16[72,304,152]{1,2,0:T(8,128)(2,1)} %param.8) | data formatting | bytes 13307904 | tf_op args[2]
  23.1 20.3 %reshape.258 = bf16[72,46208]{1,0:T(8,128)(2,1)} reshape(bf16[72,304,152]{2,1,0:T(8,128)(2,1)} %copy.53) | data formatting | bytes 13307904 | tf_op jit(solution)/shard_map/reshape | solution.py:63
  43.4 0.4 convert_reduce_fusion
  43.9 0.2 convolution_convert_fusion.1
  44.1 0.4 copy-done.10
  44.5 4.1 %convolution_convert_fusion = bf16[32,46208]{1,0:T(8,128)(2,1)S(1)} fusion(bf16[32,72]{1,0:T(8,128)(2,1)S(1)} %bitcast.188, bf16[72,46208]{1,0:T(8,128)(2,1)} %reshape.258), kind=kOutput, calls=%fused_computation.1 | convolution fusion | flops 214405120 | bytes 9615872 | tf_op jit(solution)/shard_map/dot_general | solution.py:61
  48.6 14.7 %reshape.259 = bf16[16,2,304,152]{3,2,1,0:T(8,128)(2,1)} reshape(bf16[32,46208]{1,0:T(8,128)(2,1)S(1)} %convolution_convert_fusion) | data formatting | bytes 5914624 | tf_op jit(solution)/shard_map/reshape | solution.py:66
  63.3 7.6 %copy.54 = bf16[16,2,304,152]{2,3,1,0:T(8,128)(2,1)} copy(bf16[16,2,304,152]{3,2,1,0:T(8,128)(2,1)} %reshape.259) | data formatting | bytes 5914624 | tf_op jit(solution)/shard_map/reshape | solution.py:66
  70.9 7.4 %all-to-all-start = ((bf16[16,2,304,152]{2,3,1,0:T(8,128)(2,1)}), bf16[16,2,304,152]{2,3,1,0:T(8,128)(2,1)}, u32[]{:S(2)}, u32[]{:S(2)}) async-start(bf16[16,2,304,152]{2,3,1,0:T(8,128)(2,1)} %copy.54), calls=%async_computation | async-start | bytes 7471104 | tf_op jit(solution)/shard_map/all_to_all | solution.py:86
  78.3 0.2 reduce-scatter.2.cloned.1.call-start
  78.5 9.0 %fusion.52 = f32[152,4096]{1,0:T(8,128)S(1)} fusion(s32[152]{0:T(256)S(1)} %iota_add_fusion), kind=kLoop, calls=%fused_computation.58 | loop fusion | flops 9338880 | bytes 2490976 | tf_op jit(solution)/shard_map/mul | solution.py:17
  87.6 1.3 bitcast_convert_fusion.7
  88.9 12.0 %convert_bitcast_fusion.5 = bf16[4,1,152,16,16]{4,3,0,2,1:T(8,128)(2,1)} fusion(f32[16,4096]{1,0:T(8,128)S(1)} %get-tuple-element.8, f32[152,4096]{1,0:T(8,128)S(1)} %fusion.52, bf16[4,32,4096]{2,1,0:T(8,128)(2,1)S(1)} %copy-done.13), kind=kOutput, calls=%fused_computation.62 | convolution fusion | flops 1295147008 | bytes 3588096 | tf_op jit(solution)/shard_map/dot_general | solution.py:26
  100.9 11.8 %convert_bitcast_fusion.4 = bf16[4,1,152,16,16]{4,3,0,2,1:T(8,128)(2,1)} fusion(f32[16,4096]{1,0:T(8,128)S(1)} %get-tuple-element.7, f32[152,4096]{1,0:T(8,128)S(1)} %fusion.52, bf16[4,32,4096]{2,1,0:T(8,128)(2,1)S(1)} %copy-done.13), kind=kOutput, calls=%fused_computation.61 | convolution fusion | flops 1295147008 | bytes 3588096 | tf_op jit(solution)/shard_map/dot_general | solution.py:26
  112.7 4.1 %copy.46 = bf16[4,1,152,16,16]{2,4,3,1,0:T(8,128)(2,1)S(1)} copy(bf16[4,1,152,16,16]{4,3,0,2,1:T(8,128)(2,1)} %convert_bitcast_fusion.5) | data formatting | bytes 622592 | tf_op jit(solution)/shard_map/stack | solution.py:78
  116.8 4.1 %copy.47 = bf16[4,1,152,16,16]{2,4,3,1,0:T(8,128)(2,1)S(1)} copy(bf16[4,1,152,16,16]{4,3,0,2,1:T(8,128)(2,1)} %convert_bitcast_fusion.4) | data formatting | bytes 622592 | tf_op jit(solution)/shard_map/stack | solution.py:78
  120.9 13.9 %convert_bitcast_fusion.3 = bf16[4,1,152,16,16]{4,3,0,2,1:T(8,128)(2,1)} fusion(f32[16,4096]{1,0:T(8,128)} %get-tuple-element.13, f32[152,4096]{1,0:T(8,128)S(1)} %fusion.52, bf16[4,32,4096]{2,1,0:T(8,128)(2,1)} %param.7), kind=kOutput, calls=%fused_computation.60 | convolution fusion | flops 1295147008 | bytes 3588096 | tf_op jit(solution)/shard_map/dot_general | solution.py:26
  134.7 4.8 %copy.48 = bf16[4,1,152,16,16]{2,4,3,1,0:T(8,128)(2,1)} copy(bf16[4,1,152,16,16]{4,3,0,2,1:T(8,128)(2,1)} %convert_bitcast_fusion.3) | data formatting | bytes 622592 | tf_op jit(solution)/shard_map/stack | solution.py:78
  139.5 13.6 %convert_bitcast_fusion.2 = bf16[4,1,152,16,16]{4,3,0,2,1:T(8,128)(2,1)} fusion(f32[16,4096]{1,0:T(8,128)} %get-tuple-element.12, f32[152,4096]{1,0:T(8,128)S(1)} %fusion.52, bf16[4,32,4096]{2,1,0:T(8,128)(2,1)} %param.7), kind=kOutput, calls=%fused_computation.59 | convolution fusion | flops 1295147008 | bytes 3588096 | tf_op jit(solution)/shard_map/dot_general | solution.py:26
  153.1 4.1 %copy.49 = bf16[4,1,152,16,16]{2,4,3,1,0:T(8,128)(2,1)S(1)} copy(bf16[4,1,152,16,16]{4,3,0,2,1:T(8,128)(2,1)} %convert_bitcast_fusion.2) | data formatting | bytes 622592 | tf_op jit(solution)/shard_map/stack | solution.py:78
  157.2 0.7 compare_and_fusion.2
  158.0 1.9 pad_maximum_fusion
  159.8 3.0 gather_fusion
  162.9 4.9 %convolution_bitcast_fusion = f32[304,16,256]{2,0,1:T(8,128)} fusion(bf16[16,152,256]{1,2,0:T(8,128)(2,1)} %bitcast.185, bf16[16,304,152]{1,2,0:T(8,128)(2,1)S(1)} %gather_fusion, pred[16]{0:T(512)(128)(4,1)S(1)} %get-tuple-element.2), kind=kOutput, calls=%fused_computation.70 | convolution fusion | flops 379275264 | bytes 7704592 | tf_op jit(solution)/shard_map/pgh,phx->gpx/dot_general | solution.py:89
  167.8 1.7 copy-done.2
  169.5 12.6 %convert_bitcast_fusion.6 = bf16[4,1,152,16,16]{4,3,0,2,1:T(8,128)(2,1)S(1)} fusion(f32[16,4096]{1,0:T(8,128)S(1)} %copy-done.8, f32[152,4096]{1,0:T(8,128)S(1)} %copy-done.2, bf16[4,32,4096]{2,1,0:T(8,128)(2,1)} %param.7), kind=kOutput, calls=%fused_computation.63 | convolution fusion | flops 1295147008 | bytes 3588096 | tf_op jit(solution)/shard_map/dot_general | solution.py:26
  182.1 11.8 %convert_bitcast_fusion.7 = bf16[4,1,152,16,16]{4,3,0,2,1:T(8,128)(2,1)} fusion(f32[16,4096]{1,0:T(8,128)S(1)} %copy-done.7, f32[152,4096]{1,0:T(8,128)S(1)} %copy-done.2, bf16[4,32,4096]{2,1,0:T(8,128)(2,1)S(1)} %copy-done.14), kind=kOutput, calls=%fused_computation.64 | convolution fusion | flops 1295147008 | bytes 3588096 | tf_op jit(solution)/shard_map/dot_general | solution.py:26
  193.9 12.1 %convert_bitcast_fusion.8 = bf16[4,1,152,16,16]{4,3,0,2,1:T(8,128)(2,1)} fusion(f32[16,4096]{1,0:T(8,128)S(1)} %copy-done.6, f32[152,4096]{1,0:T(8,128)S(1)} %copy-done.2, bf16[4,32,4096]{2,1,0:T(8,128)(2,1)S(1)} %copy-done.14), kind=kOutput, calls=%fused_computation.65 | convolution fusion | flops 1295147008 | bytes 3588096 | tf_op jit(solution)/shard_map/dot_general | solution.py:26
  206.0 11.7 %convert_bitcast_fusion.9 = bf16[4,1,152,16,16]{4,3,0,2,1:T(8,128)(2,1)} fusion(f32[16,4096]{1,0:T(8,128)S(1)} %copy-done.5, f32[152,4096]{1,0:T(8,128)S(1)} %copy-done.2, bf16[4,32,4096]{2,1,0:T(8,128)(2,1)S(1)} %copy-done.14), kind=kOutput, calls=%fused_computation.66 | convolution fusion | flops 1295147008 | bytes 3588096 | tf_op jit(solution)/shard_map/dot_general | solution.py:26
  217.8 9.4 %maximum_bitcast_fusion = bf16[4,4,152,16,16,1]{4,3,0,2,1,5:T(8,128)(2,1)} fusion(bf16[4,1,152,16,16]{4,3,0,2,1:T(8,128)(2,1)S(1)} %convert_bitcast_fusion.6, bf16[4,1,152,16,16]{4,3,0,2,1:T(8,128)(2,1)} %convert_bitcast_fusion.7, bf16[4,1,152,16,16]{4,3,0,2,1:T(8,128)(2,1)} %convert_bitcast_fusion.8, bf16[4,1,152,16,16]{4,3,0,2,1:T(8,128)(2,1)} %convert_bitcast_fusion.9), kind=kLoop, calls=%fused_computation.42 | loop fusion | flops 1867776 | bytes 2490368 | tf_op jit(solution)/shard_map/stack | solution.py:71
  227.2 19.6 %copy.77 = bf16[4,4,152,16,16,1]{2,3,5,4,0,1:T(8,128)(2,1)S(1)} copy(bf16[4,4,152,16,16,1]{4,3,0,2,1,5:T(8,128)(2,1)} %maximum_bitcast_fusion) | data formatting | bytes 2490368 | tf_op jit(solution)/shard_map/stack | solution.py:71
  247.1 5.7 %convert_bitcast_fusion = bf16[4,4,152,16,16,4]{2,4,5,3,0,1:T(8,128)(2,1)} fusion(bf16[4,4,152,16,16,1]{2,3,5,4,0,1:T(8,128)(2,1)S(1)} %copy.77, bf16[4,4,16,16]{3,2,1,0:T(8,128)(2,1)S(1)} %reshape.263), kind=kOutput, calls=%fused_computation.49 | convolution fusion | flops 82182144 | bytes 6234112 | tf_op jit(solution)/shard_map/bagcd,navc->bagdvn/dot_general | solution.py:102
  252.8 12.1 %convert_bitcast_fusion.1 = bf16[4,4,152,16,16,4]{2,4,5,3,1,0:T(8,128)(2,1)} fusion(bf16[4,4,152,16,16,1]{4,3,0,2,1,5:T(8,128)(2,1)S(1)} %copy-done, bf16[4,4,16,16]{3,2,1,0:T(8,128)(2,1)S(1)} %reshape.256), kind=kOutput, calls=%fused_computation.50 | convolution fusion | flops 82182144 | bytes 6234112 | tf_op jit(solution)/shard_map/bagcd,nbvd->bagcvn/dot_general | solution.py:98
  264.9 1.8 convert_bitcast_fusion.10
  266.7 1.9 copy.56
  268.7 12.3 %fusion.80 = f32[4,4,16,16]{2,3,0,1:T(8,128)S(1)} fusion(bf16[4,4,152,16,16,1]{2,4,3,1,5,0:T(8,128)(2,1)S(1)} %bitcast.186, bf16[4,4,152,16,16,4]{2,4,5,3,0,1:T(8,128)(2,1)} %convert_bitcast_fusion), kind=kOutput, calls=%fused_computation.77 | convolution fusion | flops 79691776 | bytes 6242304 | tf_op jit(solution)/shard_map/bagvw,bagdvn->nbwd/dot_general | solution.py:105
  280.9 0.1 copy.63
  281.0 0.1 reshape.264
  281.2 8.4 %psum.15 = f32[4,4,256]{2,1,0:T(4,128)S(1)} all-reduce(f32[4,4,256]{2,1,0:T(4,128)S(1)} %reshape.264), channel_id=1, replica_groups=mesh['ka'=16,'ga'=2] {'ga'}, use_global_device_ids=true, to_apply=%region_3.4 | all-reduce | flops 4096 | bytes 32768 | tf_op jit(solution)/shard_map/psum | solution.py:111
  289.6 0.6 broadcast_multiply_fusion
  290.2 13.2 %fusion.75 = f32[4,4,16,16]{2,3,0,1:T(8,128)S(1)} fusion(bf16[4,4,152,16,16,1]{2,4,3,1,0,5:T(8,128)(2,1)S(1)} %bitcast.187, bf16[4,4,152,16,16,4]{2,4,5,3,1,0:T(8,128)(2,1)} %convert_bitcast_fusion.1), kind=kOutput, calls=%fused_computation.76 | convolution fusion | flops 79691776 | bytes 6242304 | tf_op jit(solution)/shard_map/bagvw,bagcwn->navc/dot_general | solution.py:101
  303.4 0.1 copy.59
  303.5 0.1 reshape.262
  303.6 41.1 %psum.14 = f32[4,4,256]{2,1,0:T(4,128)S(1)} all-reduce(f32[4,4,256]{2,1,0:T(4,128)S(1)} %reshape.262), channel_id=1, replica_groups=mesh['ka'=16,'ga'=2] {'ka','ga'}, use_global_device_ids=true, to_apply=%region_2.3 | all-reduce | flops 4096 | bytes 32768 | tf_op jit(solution)/shard_map/psum | solution.py:110
  344.7 0.6 broadcast_multiply_fusion.1
  (43 shorter events, 0.7 us)
Async XLA Ops:
  43.4 0.7 copy-start.9
  43.9 0.6 copy-start.10
  70.9 89.0 %all-to-all-start = ((bf16[16,2,304,152]{2,3,1,0:T(8,128)(2,1)}), bf16[16,2,304,152]{2,3,1,0:T(8,128)(2,1)}, u32[]{:S(2)}, u32[]{:S(2)}) async-start(bf16[16,2,304,152]{2,3,1,0:T(8,128)(2,1)} %copy.54), calls=%async_computation | async-start | bytes 7471104 | tf_op jit(solution)/shard_map/all_to_all | solution.py:86
  78.3 9.3 %copy-start.4 = (bf16[4,32,4096]{2,1,0:T(8,128)(2,1)S(1)}, bf16[4,32,4096]{2,1,0:T(8,128)(2,1)}, u32[]{:S(2)}) copy-start(bf16[4,32,4096]{2,1,0:T(8,128)(2,1)} %param.6) | copy-start | bytes 3145732
  78.3 186.6 %reduce-scatter.2.cloned.1.call-start = ((), (), s32[]{:S(2)}) async-start(), calls=%async_computation.2 | async-start | bytes 7471104 | tf_op jit(solution)/shard_map/reduce_scatter | solution.py:88
  78.5 10.4 %copy-start.13 = (bf16[4,32,4096]{2,1,0:T(8,128)(2,1)S(1)}, bf16[4,32,4096]{2,1,0:T(8,128)(2,1)}, u32[]{:S(2)}) copy-start(bf16[4,32,4096]{2,1,0:T(8,128)(2,1)} %param.7) | copy-start | bytes 3145732
  87.6 51.9 %copy-start.1 = (f32[152,4096]{1,0:T(8,128)}, f32[152,4096]{1,0:T(8,128)S(1)}, u32[]{:S(2)}) copy-start(f32[152,4096]{1,0:T(8,128)S(1)} %fusion.52) | copy-start | bytes 7471108
  153.1 4.9 %copy-start.3 = (bf16[4,1,152,16,16]{2,4,3,1,0:T(8,128)(2,1)S(1)}, bf16[4,1,152,16,16]{2,4,3,1,0:T(8,128)(2,1)}, u32[]{:S(2)}) copy-start(bf16[4,1,152,16,16]{2,4,3,1,0:T(8,128)(2,1)} %copy.48) | copy-start | bytes 933892
  167.8 1.7 copy-start.2
  167.8 1.7 copy-start.8
  169.5 12.6 %copy-start.7 = (f32[16,4096]{1,0:T(8,128)S(1)}, f32[16,4096]{1,0:T(8,128)}, u32[]{:S(2)}) copy-start(f32[16,4096]{1,0:T(8,128)} %get-tuple-element.10) | copy-start | bytes 786436
  169.5 12.6 %copy-start.14 = (bf16[4,32,4096]{2,1,0:T(8,128)(2,1)S(1)}, bf16[4,32,4096]{2,1,0:T(8,128)(2,1)}, u32[]{:S(2)}) copy-start(bf16[4,32,4096]{2,1,0:T(8,128)(2,1)} %param.7) | copy-start | bytes 3145732
  182.1 11.8 %copy-start.6 = (f32[16,4096]{1,0:T(8,128)S(1)}, f32[16,4096]{1,0:T(8,128)}, u32[]{:S(2)}) copy-start(f32[16,4096]{1,0:T(8,128)} %get-tuple-element.11) | copy-start | bytes 786436
  193.9 12.1 %copy-start.5 = (f32[16,4096]{1,0:T(8,128)S(1)}, f32[16,4096]{1,0:T(8,128)}, u32[]{:S(2)}) copy-start(f32[16,4096]{1,0:T(8,128)} %get-tuple-element.6) | copy-start | bytes 786436
  227.2 19.7 %copy-start.11 = (bf16[4,4,256]{2,1,0:T(4,128)(2,1)S(1)}, bf16[4,4,256]{2,1,0:T(4,128)(2,1)}, u32[]{:S(2)}) copy-start(bf16[4,4,256]{2,1,0:T(4,128)(2,1)} %param.10) | copy-start | bytes 24580
  227.2 19.8 %copy-start.12 = (bf16[4,4,256]{2,1,0:T(4,128)(2,1)S(1)}, bf16[4,4,256]{2,1,0:T(4,128)(2,1)}, u32[]{:S(2)}) copy-start(bf16[4,4,256]{2,1,0:T(4,128)(2,1)} %param.11) | copy-start | bytes 24580
  247.1 5.7 %copy-start = (bf16[4,4,152,16,16,1]{4,3,0,2,1,5:T(8,128)(2,1)S(1)}, bf16[4,4,152,16,16,1]{4,3,0,2,1,5:T(8,128)(2,1)}, u32[]{:S(2)}) copy-start(bf16[4,4,152,16,16,1]{4,3,0,2,1,5:T(8,128)(2,1)} %maximum_bitcast_fusion) | copy-start | bytes 3735556
Sparse Core Ops, SparseCore 0:
  167.9 64.1 reduce-scatter.1
where the time goes:
time: 359 us; the launch traced here: 352 us
  matrix products  152 us (42%)
  local copies, waits for them, and re-layouts  102 us (28%)
  blocking collectives  49.5 us (14%)
  other arithmetic  27.3 us (8%)
  between operations  14.6 us (4%)
  starting transfers between devices  7.61 us (2%)
    dot_general x8, matrix products, densities_one(): lax.dot_general(weighted.reshape(-1, grid), orbitals[:, lower:upper].resh...  99.5 us
    psum x1, blocking collectives, on_device(): row_total = lax.psum(row_part, ('ka', 'ga'))  41.1 us
    reshape x2, local copies, waits for them, and re-layouts, on_device(): outgoing = outgoing.reshape(ka_count, CAP, wave_count, slice_width)  22.3 us
    reshape x1, local copies, waits for them, and re-layouts, on_device(): screening.reshape(block_local, wave_count * slice_width)  20.3 us
    another operation x1, local copies, waits for them, and re-layouts, on_device(): jnp.stack([densities_one(plane, row_orbitals[row_index], orbitals, NV, NV...  19.6 us
    another operation x4, local copies, waits for them, and re-layouts, on_device(): jnp.stack([densities_one(plane, row_orbitals[row_index], orbitals, 0, NV)...  17 us
    unnamed x31, local copies, waits for them, and re-layouts  16.1 us
    dot_general x1, matrix products, on_device(): jnp.einsum('bagvw,bagcwn->navc', screened, first, preferred_element_type=...  13.2 us
  transfers between devices with their start and end apart: 2, of which 0 were waited for; matrix products, arithmetic and copies ran while one was open for 50% of the time, Pallas kernels for 0%

commit v1 on v0

v1 whole, which is shorter than its diff:
```python
import math

import jax
import jax.numpy as jnp
from jax import lax
from jax.experimental import pallas as pl
from jax.experimental.pallas import tpu as pltpu
from jax.sharding import PartitionSpec as P

NV = 16
NC = 16
CAP = 2
MAIN = 256
HALF = 64
WIDE = CAP * MAIN + 2 * HALF


def plane_columns(first, count, grid, width):
    column = lax.broadcasted_iota(jnp.int32, (grid, width), 1)
    point = lax.broadcasted_iota(jnp.int32, (grid, width), 0)
    phase = ((first + column) * point % grid).astype(jnp.float32) * (2.0 * math.pi / grid)
    wave = math.sqrt(2.0 / grid) * jnp.cos(phase)
    return jnp.where(column < count, wave, 0.0).astype(jnp.bfloat16)


def gather_blocks(table, me, blocks, rows_per):
    n_dest = table.shape[0] // rows_per
    block_local, depth, waves = blocks.shape
    rest = waves - MAIN

    def kernel(table_ref, me_ref, blocks_ref, out_ref, held, packed, count, in_sem, out_sem):
        base = me_ref[0] * block_local

        def start(d, carry):
            taken = jnp.int32(0)
            for p in range(rows_per):
                local = table_ref[d * rows_per + p] - base
                hit = (local >= 0) & (local < block_local) & (taken < CAP)

                @pl.when(hit)
                def _():
                    at = d * CAP + taken
                    pltpu.make_async_copy(blocks_ref.at[local], held.at[at], in_sem.at[at]).start()

                taken = taken + hit.astype(jnp.int32)
            count[d] = taken
            return carry

        lax.fori_loop(0, n_dest, start, 0)

        def pack(d, carry):
            for s in range(CAP):

                @pl.when(count[d] > s)
                def _():
                    at = d * CAP + s
                    pltpu.make_async_copy(blocks_ref.at[0], held.at[at], in_sem.at[at]).wait()
                    packed[d, :, s * MAIN : (s + 1) * MAIN] = held[at, :, :MAIN]
                    low = CAP * MAIN + s * HALF
                    packed[d, :, low : low + rest] = held[at, :, MAIN:]

            pltpu.make_async_copy(packed.at[d], out_ref.at[d], out_sem.at[d]).start()
            return carry

        lax.fori_loop(0, n_dest, pack, 0)

        def finish(d, carry):
            pltpu.make_async_copy(packed.at[d], out_ref.at[d], out_sem.at[d]).wait()
            return carry

        lax.fori_loop(0, n_dest, finish, 0)

    return pl.pallas_call(
        kernel,
        out_shape=jax.ShapeDtypeStruct((n_dest, depth, WIDE), jnp.bfloat16),
        in_specs=[
            pl.BlockSpec(memory_space=pltpu.SMEM),
            pl.BlockSpec(memory_space=pltpu.SMEM),
            pl.BlockSpec(memory_space=pl.ANY),
        ],
        out_specs=pl.BlockSpec(memory_space=pl.ANY),
        scratch_shapes=[
            pltpu.VMEM((n_dest * CAP, depth, waves), jnp.bfloat16),
            pltpu.VMEM((n_dest, depth, WIDE), jnp.bfloat16),
            pltpu.SMEM((n_dest,), jnp.int32),
            pltpu.SemaphoreType.DMA((n_dest * CAP,)),
            pltpu.SemaphoreType.DMA((n_dest,)),
        ],
        compiler_params=pltpu.CompilerParams(vmem_limit_bytes=40 << 20),
        name="gather_blocks",
    )(table, me, blocks)


def densities(row_orbitals, orbitals, plane_vale, plane_cond):
    row_count, bands, grid = row_orbitals.shape
    point_local = orbitals.shape[0]
    depth = plane_vale.shape[1]
    width = plane_cond.shape[1]
    pairs = NV * NV

    def kernel(row_ref, orb_ref, vplane_ref, cplane_ref, vale_ref, cond_ref, fv, fc):
        def products(t, carry):
            lanes = pl.ds(pl.multiple_of(t * 128, 128), 128)
            for low, out in ((0, fv), (NV, fc)):
                ket = orb_ref[0, low : low + 16, lanes]
                for c in range(16):
                    bra = row_ref[0, low + c : low + c + 1, lanes]
                    out[c * 16 : (c + 1) * 16, lanes] = (bra * ket).astype(jnp.bfloat16)
            return carry

        lax.fori_loop(0, grid // 128, products, 0)
        vale_ref[0, 0] = jnp.dot(
            fv[...], vplane_ref[...], preferred_element_type=jnp.float32
        ).astype(jnp.bfloat16)
        cond_ref[0, 0] = jnp.dot(
            fc[...], cplane_ref[...], preferred_element_type=jnp.float32
        ).astype(jnp.bfloat16)

    return pl.pallas_call(
        kernel,
        grid=(point_local, row_count),
        out_shape=(
            jax.ShapeDtypeStruct((point_local, row_count, pairs, depth), jnp.bfloat16),
            jax.ShapeDtypeStruct((point_local, row_count, pairs, width), jnp.bfloat16),
        ),
        in_specs=[
            pl.BlockSpec((1, bands, grid), lambda b, a: (a, 0, 0)),
            pl.BlockSpec((1, bands, grid), lambda b, a: (b, 0, 0)),
            pl.BlockSpec((grid, depth), lambda b, a: (0, 0)),
            pl.BlockSpec((grid, width), lambda b, a: (0, 0)),
        ],
        out_specs=(
            pl.BlockSpec((1, 1, pairs, depth), lambda b, a: (b, a, 0, 0)),
            pl.BlockSpec((1, 1, pairs, width), lambda b, a: (b, a, 0, 0)),
        ),
        scratch_shapes=[
            pltpu.VMEM((pairs, grid), jnp.bfloat16),
            pltpu.VMEM((pairs, grid), jnp.bfloat16),
        ],
        compiler_params=pltpu.CompilerParams(vmem_limit_bytes=48 << 20),
        name="densities",
    )(row_orbitals, orbitals, plane_vale, plane_cond)


def images(owner, rank, incoming, vale, cond, vec_tile, row_tile, waves):
    point_local, row_count, pairs, depth = vale.shape
    width = cond.shape[3]
    vec_count = vec_tile.shape[0]
    rest = waves - MAIN

    def kernel(
        owner_ref, rank_ref, block_ref, vale_ref, cond_ref, vec_ref, rowvec_ref, row_out, col_out,
        matrix, row_sum, col_sum,
    ):
        b = pl.program_id(0)
        a = pl.program_id(1)
        pair = b * row_count + a

        @pl.when(pair == 0)
        def _():
            row_sum[...] = jnp.zeros(row_sum.shape, jnp.float32)
            col_sum[...] = jnp.zeros(col_sum.shape, jnp.float32)

        rank = rank_ref[pair]
        density = vale_ref[0, 0]
        main = block_ref[0, :, pl.ds(pl.multiple_of(rank * MAIN, MAIN), MAIN)]
        shared = block_ref[0, :, CAP * MAIN :]
        screened = jnp.dot(density, main, preferred_element_type=jnp.float32).astype(jnp.bfloat16)
        others = jnp.dot(density, shared, preferred_element_type=jnp.float32)
        others = jnp.where(rank == 0, others, pltpu.roll(others, HALF, 1))
        lane = lax.broadcasted_iota(jnp.int32, others.shape, 1)
        others = jnp.where(lane < rest, others, 0.0).astype(jnp.bfloat16)
        nt = (((1,), (1,)), ((), ()))
        matrix[...] = lax.dot_general(
            screened, cond_ref[0, 0, :, :MAIN], nt, preferred_element_type=jnp.float32
        ) + lax.dot_general(
            others, cond_ref[0, 0, :, MAIN:], nt, preferred_element_type=jnp.float32
        )
        for n in range(vec_count):
            vec = vec_ref[n, b]
            total = jnp.zeros((16, pairs), jnp.float32)
            for v in range(16):
                part = matrix[v * 16 : (v + 1) * 16, :]
                term = part * vec
                row_sum[n, a, v] += term[:8] + term[8:]
                total += part * rowvec_ref[n, a, v : v + 1, :]
            col_sum[n, b] += total

        @pl.when(pair == point_local * row_count - 1)
        def _():
            lane_in = lax.broadcasted_iota(jnp.int32, (16, pairs), 1)
            group = lax.broadcasted_iota(jnp.int32, (16, pairs), 0)
            pick_c = jnp.where(lane_in // 16 == group, 1.0, 0.0)
            pick_d = jnp.where(lane_in % 16 == group, 1.0, 0.0)
            rows = jnp.sum(row_sum[...].reshape(-1, 8, pairs), axis=1)
            cols = col_sum[...].reshape(-1, pairs)
            row_out[...] = lax.dot_general(
                pick_c, rows, nt, precision=lax.Precision.HIGHEST, preferred_element_type=jnp.float32
            )
            col_out[...] = lax.dot_general(
                pick_d, cols, nt, precision=lax.Precision.HIGHEST, preferred_element_type=jnp.float32
            )

    whole4 = lambda b, a, o, r: (0, 0, 0, 0)
    whole2 = lambda b, a, o, r: (0, 0)
    row_shape = (NC, vec_count * row_count * NV)
    col_shape = (NC, vec_count * point_local * NV)
    return pl.pallas_call(
        kernel,
        out_shape=(
            jax.ShapeDtypeStruct(row_shape, jnp.float32),
            jax.ShapeDtypeStruct(col_shape, jnp.float32),
        ),
        grid_spec=pltpu.PrefetchScalarGridSpec(
            num_scalar_prefetch=2,
            grid=(point_local, row_count),
            in_specs=[
                pl.BlockSpec((1, depth, WIDE), lambda b, a, o, r: (o[b * row_count + a], 0, 0)),
                pl.BlockSpec((1, 1, pairs, depth), lambda b, a, o, r: (b, a, 0, 0)),
                pl.BlockSpec((1, 1, pairs, width), lambda b, a, o, r: (b, a, 0, 0)),
                pl.BlockSpec(vec_tile.shape, whole4),
                pl.BlockSpec(row_tile.shape, whole4),
            ],
            out_specs=(pl.BlockSpec(row_shape, whole2), pl.BlockSpec(col_shape, whole2)),
            scratch_shapes=[
                pltpu.VMEM((pairs, pairs), jnp.float32),
                pltpu.VMEM((vec_count, row_count, 16, 8, pairs), jnp.float32),
                pltpu.VMEM((vec_count, point_local, 16, pairs), jnp.float32),
            ],
        ),
        compiler_params=pltpu.CompilerParams(vmem_limit_bytes=48 << 20),
        name="images",
    )(owner, rank, incoming, vale, cond, vec_tile, row_tile)


def sum_over(values, axis):
    size = lax.axis_size(axis)
    step = 1
    while step < size:
        perm = [(i, i ^ step) for i in range(size)]
        values = jax.tree.map(lambda x: x + lax.ppermute(x, axis, perm), values)
        step *= 2
    return values


def on_device(row_orbitals, orbitals, screening, pair_blocks, row_vectors, vectors):
    ka_count = lax.axis_size("ka")
    my_point = lax.axis_index("ka")
    my_slice = lax.axis_index("ga")
    row_count = row_orbitals.shape[0]
    point_local, _, grid = orbitals.shape
    block_local, wave_count, slice_width = screening.shape
    pair_count = point_local * row_count
    vec_count = vectors.shape[0]

    flat = pair_blocks.reshape(-1)
    outgoing = gather_blocks(
        flat, my_point.reshape(1), jnp.swapaxes(screening, 1, 2), pair_count
    )
    incoming = lax.all_to_all(outgoing, "ka", split_axis=0, concat_axis=0, tiled=True)

    mine = lax.dynamic_slice_in_dim(flat, my_point * pair_count, pair_count)
    owner = mine // block_local
    order = lax.iota(jnp.int32, pair_count)
    earlier = (owner[:, None] == owner[None, :]) & (order[None, :] < order[:, None])
    rank = jnp.sum(earlier.astype(jnp.int32), axis=1)

    plane_vale = plane_columns(my_slice * slice_width, slice_width, grid, slice_width)
    plane_cond = plane_columns(0, wave_count, grid, MAIN + 2 * HALF)
    vale, cond = densities(
        row_orbitals.astype(jnp.float32), orbitals.astype(jnp.float32), plane_vale, plane_cond
    )
    vec_tile = jnp.tile(
        vectors.astype(jnp.float32).reshape(vec_count, point_local, NV, NC), (1, 1, 1, NC)
    )
    row_tile = jnp.repeat(
        row_vectors.astype(jnp.float32).reshape(vec_count, row_count, NV, NC), NC, axis=3
    )
    row_part, col_part = images(
        owner, rank, incoming, vale, cond, vec_tile, row_tile, wave_count
    )
    row_part, col_part = sum_over((row_part, col_part), "ga")
    row_part = sum_over(row_part, "ka")
    row_scale = float(wave_count * NV * NC * point_local * ka_count) ** (-0.5)
    column_scale = float(wave_count * NV * NC * row_count) ** (-0.5)

    def place(part, count, scale):
        part = part.reshape(NC, vec_count, count, NV) * scale
        return part.transpose(1, 2, 3, 0).reshape(vec_count, count, NV * NC)

    return (
        place(row_part, row_count, row_scale),
        place(col_part, point_local, column_scale),
    )


def solution(mesh):
    return jax.shard_map(
        on_device,
        mesh=mesh,
        in_specs=(P(), P("ka", None, None), P("ka", None, "ga"), P(), P(), P(None, "ka", None)),
        out_specs=(P(), P(None, "ka", None)),
        check_vma=False,
    )
```

time: 359 us -> 165 us (0.46); the launches traced: 352 us -> 165 us
  matrix products: 152 us -> 0 us
  local copies, waits for them, and re-layouts: 102 us -> 19.2 us
  Pallas kernels: 0 us -> 73 us
  blocking collectives: 49.5 us -> 0 us
  other arithmetic: 27.3 us -> 47.4 us
  between operations: 14.6 us -> 0.76 us
  starting transfers between devices: 7.61 us -> 17.9 us
  waiting for transfers between devices: 0.02 us -> 6.31 us
    dot_general x15 -> x0, matrix products: 152 us -> none  [the longest x8 99.5 us: densities_one(): lax.dot_general(weighted.reshape(-1, grid), orbitals[:, lower:upper].resh...]
    pallas_call x0 -> x3, Pallas kernels: none -> 73 us  [the longest x1 51.6 us: densities(): pl.pallas_call(kernel, grid=(point_local, row_count), out_shape=(jax.Shap...]
    psum x2 -> x0, blocking collectives: 49.5 us -> none  [the longest x1 41.1 us: on_device(): row_total = lax.psum(row_part, ('ka', 'ga'))]
    convert_element_type x1 -> x4, other arithmetic: 1.82 us -> 47.1 us  [the longest x2 41.6 us: plane_columns(): return jnp.where(column < count, wave, 0.0).astype(jnp.bfloat16)]
    reshape x7 -> x5, local copies, waits for them, and re-layouts: 43.1 us -> 4.07 us  [the longest x1 2.44 us: on_device(): jnp.repeat(row_vectors.astype(jnp.float32).reshape(vec_count, row_count,...]
    another operation x5 -> x3, local copies, waits for them, and re-layouts: 36.7 us -> 4.62 us  [on_device(): jnp.tile(vectors.astype(jnp.float32).reshape(vec_count, point_local, NV,...]
    mul x4 -> x2, other arithmetic: 11.6 us -> 0.01 us  [place(): part = part.reshape(NC, vec_count, count, NV) * scale]
    another operation x2 -> x0, other arithmetic: 11.3 us -> none  [the longest x1 9.4 us: on_device(): jnp.stack([densities_one(plane, row_orbitals[row_index], orbitals, NV, NV...]
  transfers between devices with their start and end apart: 2 -> 7, of which waited for: 0 -> 5; matrix products, arithmetic and copies ran while one was open for 50% -> 35% of each run, Pallas kernels for 0% -> 31%
where the time goes in v1:
time: 165 us
  Pallas kernels  73 us (44%)
  other arithmetic  47.4 us (29%)
  local copies, waits for them, and re-layouts  19.2 us (12%)
  starting transfers between devices  17.9 us (11%)
  waiting for transfers between devices  6.31 us (4%)
    pallas_call x1, Pallas kernels, densities(): pl.pallas_call(kernel, grid=(point_local, row_count), out_shape=(jax.Shap...  51.6 us
    convert_element_type x2, other arithmetic, plane_columns(): return jnp.where(column < count, wave, 0.0).astype(jnp.bfloat16)  41.6 us
    pallas_call x1, Pallas kernels, images(): pl.pallas_call(kernel, out_shape=(jax.ShapeDtypeStruct(row_shape, jnp.flo...  14 us
    ppermute x6, starting transfers between devices, sum_over(): values = jax.tree.map(lambda x: x + lax.ppermute(x, axis, perm), values)  9.76 us
    all_to_all x1, starting transfers between devices, on_device(): lax.all_to_all(outgoing, 'ka', split_axis=0, concat_axis=0, tiled=True)  8.13 us
    unnamed x15, local copies, waits for them, and re-layouts  8.07 us
    pallas_call x1, Pallas kernels, gather_blocks(): pl.pallas_call(kernel, out_shape=jax.ShapeDtypeStruct((n_dest, depth, WID...  7.46 us
    ppermute x6, waiting for transfers between devices, sum_over(): values = jax.tree.map(lambda x: x + lax.ppermute(x, axis, perm), values)  6.31 us
  transfers between devices with their start and end apart: 7, of which 5 were waited for; matrix products, arithmetic and copies ran while one was open for 35% of the time, Pallas kernels for 31%

profile of v1, /device:TPU:0, one launch (start us, length us, event | category | flops | bytes accessed | tf_op | source)
XLA Modules:
  0.0 164.6 jit_solution(4359276171470393499)
XLA Ops:
  0.6 0.8 copy.13
  1.4 0.1 reshape.38.table_ref
  1.5 0.0 copy-start
  1.5 3.4 %copy-done = bf16[72,304,152]{1,2,0:T(8,128)(2,1)S(1)} copy-done((bf16[72,304,152]{1,2,0:T(8,128)(2,1)S(1)}, bf16[72,304,152]{1,2,0:T(8,128)(2,1)}, u32[]{:S(2)}) %copy-start) | copy-done | bytes 6653976
  4.9 7.5 %gather_blocks.1 = bf16[16,152,640]{2,1,0:T(8,128)(2,1)} custom-call(s32[256]{0:T(256)S(1)} %reshape.38.table_ref, s32[1]{0:T(128)} %bitcast.me_ref, bf16[72,152,304]{2,1,0:T(8,128)(2,1)S(1)} %bitcast.12), custom_call_target="tpu_custom_call" | custom-call | tf_op jit(solution)/shard_map/gather_blocks/pallas_call | solution.py:73
  12.4 8.1 %all-to-all-start = ((bf16[16,152,640]{2,1,0:T(8,128)(2,1)}), bf16[16,152,640]{2,1,0:T(8,128)(2,1)S(1)}, u32[]{:S(2)}, u32[]{:S(2)}) async-start(bf16[16,152,640]{2,1,0:T(8,128)(2,1)} %gather_blocks.1), calls=%async_computation | async-start | bytes 6225920 | tf_op jit(solution)/shard_map/all_to_all | solution.py:260
  20.5 0.0 copy-start.5
  20.5 2.8 %convert_element_type.24.row_ref = f32[4,32,4096]{2,1,0:T(8,128)} convert(bf16[4,32,4096]{2,1,0:T(8,128)(2,1)} %param.6) | non-fusion elementwise | flops 524288 | bytes 3145728 | tf_op jit(solution)/shard_map/convert_element_type | solution.py:271
  23.3 0.0 copy-start.6
  23.3 2.8 %convert_element_type.25.orb_ref = f32[4,32,4096]{2,1,0:T(8,128)} convert(bf16[4,32,4096]{2,1,0:T(8,128)(2,1)} %param.7) | non-fusion elementwise | flops 524288 | bytes 3145728 | tf_op jit(solution)/shard_map/convert_element_type | solution.py:271
  26.1 0.0 copy-done.5
  26.1 0.1 reshape.47
  26.2 1.9 %broadcast_in_dim.17 = f32[4,4,16,16,16]{4,3,2,1,0:T(8,128)} broadcast(f32[4,4,16,16]{3,2,1,0:T(8,128)S(1)} %reshape.47), dimensions={0,1,2,3} | broadcast | bytes 278528 | tf_op jit(solution)/shard_map/broadcast_in_dim | solution.py:276
  28.1 2.4 %reshape.42.rowvec_ref = f32[4,4,16,256]{3,2,1,0:T(8,128)S(1)} reshape(f32[4,4,16,16,16]{4,3,2,1,0:T(8,128)} %broadcast_in_dim.17) | data formatting | bytes 524288 | tf_op jit(solution)/shard_map/reshape | solution.py:276
  30.5 0.0 copy-done.6
  30.6 0.1 reshape.45
  30.7 1.5 tile.14
  32.1 3.1 %tile.15.vec_ref = f32[4,4,16,256]{3,2,1,0:T(8,128)} reshape(f32[4,4,16,16,16]{4,3,2,1,0:T(8,128)} %tile.14) | data formatting | bytes 524288 | tf_op jit(solution)/shard_map/tile | solution.py:273
  35.2 0.0 copy-start.1
  35.2 16.9 %fusion.16.vplane_ref = bf16[4096,152]{1,0:T(8,128)(2,1)} fusion(s32[152]{0:T(256)S(1)} %iota_add_fusion, pred[152]{0:T(512)(128)(4,1)S(1)} %iota_compare_fusion.2), kind=kLoop, calls=%fused_computation.22 | loop fusion | flops 10584064 | bytes 1245944 | tf_op jit(solution)/shard_map/convert_element_type | solution.py:23
  52.1 24.7 %fusion.6.cplane_ref = bf16[4096,384]{1,0:T(8,128)(2,1)} fusion(pred[384]{0:T(512)(128)(4,1)S(1)} %iota_compare_fusion.1), kind=kLoop, calls=%fused_computation.9 | loop fusion | flops 26738688 | bytes 3146112 | tf_op jit(solution)/shard_map/convert_element_type | solution.py:23
  76.8 0.0 copy-done.1
  76.8 51.6 %densities.1 = (bf16[4,4,256,152]{3,2,1,0:T(8,128)(2,1)S(1)}, bf16[4,4,256,384]{3,2,1,0:T(8,128)(2,1)}) custom-call(f32[4,32,4096]{2,1,0:T(8,128)S(1)} %copy-done.1, f32[4,32,4096]{2,1,0:T(8,128)} %convert_element_type.25.orb_ref, bf16[4096,152]{1,0:T(8,128)(2,1)} %fusion.16.vplane_ref, bf16[4096,384]{1,0:T(8,128)(2,1)} %fusion.6.cplane_ref), custom_call_target="tpu_custom_call" | custom-call | tf_op jit(solution)/shard_map/densities/pallas_call | solution.py:119
  128.4 1.4 copy-done.2
  129.7 0.1 and_select_fusion.owner_ref
  129.8 0.2 convert_reduce_fusion.rank_ref
  130.0 0.0 all-to-all-done.block_ref
  130.0 1.6 copy-done.3
  131.6 0.9 copy-done.4
  132.6 14.0 %images.1 = (f32[16,256]{1,0:T(8,128)S(1)}, f32[16,256]{1,0:T(8,128)S(1)}) custom-call(s32[16]{0:T(128)S(1)} %and_select_fusion.owner_ref, s32[16]{0:T(128)S(1)} %convert_reduce_fusion.rank_ref, bf16[16,152,640]{2,1,0:T(8,128)(2,1)S(1)} %all-to-all-done.block_ref, bf16[4,4,256,152]{3,2,1,0:T(8,128)(2,1)S(1)} %copy-done.3, ...), custom_call_target="tpu_custom_call" | custom-call | tf_op jit(solution)/shard_map/images/pallas_call | solution.py:208
  146.5 1.5 collective-permute-start
  148.1 2.2 %collective-permute-done = f32[16,256]{1,0:T(8,128)S(1)} collective-permute-done((f32[16,256]{1,0:T(8,128)S(1)}, f32[16,256]{1,0:T(8,128)S(1)}, u32[]{:S(2)}, u32[]{:S(2)}) %collective-permute-start) | collective-permute-done | bytes 16416 | tf_op jit(solution)/shard_map/ppermute | solution.py:241
  150.3 0.0 collective-permute-start.1
  150.3 1.2 collective-permute-done.1
  151.5 1.9 %collective-permute-start.2 = (f32[16,256]{1,0:T(8,128)S(1)}, f32[16,256]{1,0:T(8,128)S(1)}, u32[]{:S(2)}, u32[]{:S(2)}) collective-permute-start(f32[16,256]{1,0:T(8,128)S(1)} %add.47), channel_id=1, source_target_pairs={{0,4},{2,6},{4,0},{6,2},{8,12},{10,14},{12,8},{14,10},{16,20},{18,... | collective-permute-start | bytes 49160 | tf_op jit(solution)/shard_map/ppermute | solution.py:241
  153.4 1.8 %collective-permute-done.2 = f32[16,256]{1,0:T(8,128)S(1)} collective-permute-done((f32[16,256]{1,0:T(8,128)S(1)}, f32[16,256]{1,0:T(8,128)S(1)}, u32[]{:S(2)}, u32[]{:S(2)}) %collective-permute-start.2) | collective-permute-done | bytes 16416 | tf_op jit(solution)/shard_map/ppermute | solution.py:241
  155.2 1.9 %collective-permute-start.3 = (f32[16,256]{1,0:T(8,128)S(1)}, f32[16,256]{1,0:T(8,128)S(1)}, u32[]{:S(2)}, u32[]{:S(2)}) collective-permute-start(f32[16,256]{1,0:T(8,128)S(1)} %add.48), channel_id=1, source_target_pairs={{0,8},{2,10},{4,12},{6,14},{8,0},{10,2},{12,4},{14,6},{16,24},{18,... | collective-permute-start | bytes 49160 | tf_op jit(solution)/shard_map/ppermute | solution.py:241
  157.2 1.5 collective-permute-start.5
  158.7 0.3 collective-permute-done.3
  159.0 2.8 %collective-permute-start.4 = (f32[16,256]{1,0:T(8,128)S(1)}, f32[16,256]{1,0:T(8,128)S(1)}, u32[]{:S(2)}, u32[]{:S(2)}) collective-permute-start(f32[16,256]{1,0:T(8,128)S(1)} %add.49), channel_id=1, source_target_pairs={{0,16},{2,18},{4,20},{6,22},{8,24},{10,26},{12,28},{14,30},{16,0},... | collective-permute-start | bytes 49160 | tf_op jit(solution)/shard_map/ppermute | solution.py:241
  161.8 0.0 collective-permute-done.5
  161.8 0.1 mul.71
  162.0 0.1 copy.15
  162.1 0.7 reshape.44
  162.8 0.8 collective-permute-done.4
  163.6 0.1 mul.68
  163.8 0.1 copy.14
  163.9 0.7 reshape.43
  (12 shorter events, 0.0 us)
Async XLA Ops:
  1.5 3.4 %copy-start = (bf16[72,304,152]{1,2,0:T(8,128)(2,1)S(1)}, bf16[72,304,152]{1,2,0:T(8,128)(2,1)}, u32[]{:S(2)}) copy-start(bf16[72,304,152]{1,2,0:T(8,128)(2,1)} %param.8) | copy-start | bytes 19961860
  12.4 117.6 %all-to-all-start = ((bf16[16,152,640]{2,1,0:T(8,128)(2,1)}), bf16[16,152,640]{2,1,0:T(8,128)(2,1)S(1)}, u32[]{:S(2)}, u32[]{:S(2)}) async-start(bf16[16,152,640]{2,1,0:T(8,128)(2,1)} %gather_blocks.1), calls=%async_computation | async-start | bytes 6225920 | tf_op jit(solution)/shard_map/all_to_all | solution.py:260
  20.5 5.6 %copy-start.5 = (bf16[4,4,256]{2,1,0:T(4,128)(2,1)S(1)}, bf16[4,4,256]{2,1,0:T(4,128)(2,1)}, u32[]{:S(2)}) copy-start(bf16[4,4,256]{2,1,0:T(4,128)(2,1)} %param.10) | copy-start | bytes 24580
  23.3 7.2 %copy-start.6 = (bf16[4,4,256]{2,1,0:T(4,128)(2,1)S(1)}, bf16[4,4,256]{2,1,0:T(4,128)(2,1)}, u32[]{:S(2)}) copy-start(bf16[4,4,256]{2,1,0:T(4,128)(2,1)} %param.11) | copy-start | bytes 24580
  35.2 41.6 %copy-start.1 = (f32[4,32,4096]{2,1,0:T(8,128)S(1)}, f32[4,32,4096]{2,1,0:T(8,128)}, u32[]{:S(2)}) copy-start(f32[4,32,4096]{2,1,0:T(8,128)} %convert_element_type.24.row_ref) | copy-start | bytes 6291460
  128.4 1.4 copy-start.2
  130.0 1.6 copy-start.3
  131.6 0.9 copy-start.4
  146.5 3.8 %collective-permute-start = (f32[16,256]{1,0:T(8,128)S(1)}, f32[16,256]{1,0:T(8,128)S(1)}, u32[]{:S(2)}, u32[]{:S(2)}) collective-permute-start(f32[16,256]{1,0:T(8,128)S(1)} %get-tuple-element.8), channel_id=1, source_target_pairs={{0,1},{1,0},{2,3},{3,2},{4,5},{5,4},{6,7},{7,6},{8,9},{9,8},{10,11... | collective-permute-start | bytes 49160 | tf_op jit(solution)/shard_map/ppermute | solution.py:241
  150.3 1.2 collective-permute-start.1
  151.5 3.7 %collective-permute-start.2 = (f32[16,256]{1,0:T(8,128)S(1)}, f32[16,256]{1,0:T(8,128)S(1)}, u32[]{:S(2)}, u32[]{:S(2)}) collective-permute-start(f32[16,256]{1,0:T(8,128)S(1)} %add.47), channel_id=1, source_target_pairs={{0,4},{2,6},{4,0},{6,2},{8,12},{10,14},{12,8},{14,10},{16,20},{18,... | collective-permute-start | bytes 49160 | tf_op jit(solution)/shard_map/ppermute | solution.py:241
  155.2 3.7 %collective-permute-start.3 = (f32[16,256]{1,0:T(8,128)S(1)}, f32[16,256]{1,0:T(8,128)S(1)}, u32[]{:S(2)}, u32[]{:S(2)}) collective-permute-start(f32[16,256]{1,0:T(8,128)S(1)} %add.48), channel_id=1, source_target_pairs={{0,8},{2,10},{4,12},{6,14},{8,0},{10,2},{12,4},{14,6},{16,24},{18,... | collective-permute-start | bytes 49160 | tf_op jit(solution)/shard_map/ppermute | solution.py:241
  157.2 4.6 %collective-permute-start.5 = (f32[16,256]{1,0:T(8,128)S(1)}, f32[16,256]{1,0:T(8,128)S(1)}, u32[]{:S(2)}, u32[]{:S(2)}) collective-permute-start(f32[16,256]{1,0:T(8,128)S(1)} %get-tuple-element.9), channel_id=1, source_target_pairs={{0,1},{1,0},{2,3},{3,2},{4,5},{5,4},{6,7},{7,6},{8,9},{9,8},{10,11... | collective-permute-start | bytes 49160 | tf_op jit(solution)/shard_map/ppermute | solution.py:241
  159.0 4.6 %collective-permute-start.4 = (f32[16,256]{1,0:T(8,128)S(1)}, f32[16,256]{1,0:T(8,128)S(1)}, u32[]{:S(2)}, u32[]{:S(2)}) collective-permute-start(f32[16,256]{1,0:T(8,128)S(1)} %add.49), channel_id=1, source_target_pairs={{0,16},{2,18},{4,20},{6,22},{8,24},{10,26},{12,28},{14,30},{16,0},... | collective-permute-start | bytes 49160 | tf_op jit(solution)/shard_map/ppermute | solution.py:241

commit v2 on v0

v2 whole, which is shorter than its diff:
```python
import math

import jax
import jax.numpy as jnp
from jax import lax
from jax.experimental import pallas as pl
from jax.experimental.pallas import tpu as pltpu
from jax.sharding import PartitionSpec as P

NV = 16
NC = 16
CAP = 2
SIDES = 2
MAIN = 256
HALF = 64
WIDE = CAP * MAIN + 2 * HALF
WIDE_ONE = MAIN + 2 * HALF
LIMIT = 60 << 20
TAIL = 128
CHUNK = 512
NT = (((1,), (1,)), ((), ()))
VMEM = pl.BlockSpec(memory_space=pltpu.VMEM)
SMEM = pl.BlockSpec(memory_space=pltpu.SMEM)
HBM = pl.BlockSpec(memory_space=pltpu.HBM)


def mirror_of(device, count):
    half = count // SIDES
    return jnp.where(device < half, device + half, device - half)


def gather_blocks(table, blocks, ka_count):
    row_count = table.shape[0]
    point_local = table.shape[1] // ka_count
    block_local, depth, waves = blocks.shape
    rest = waves - MAIN
    half = ka_count // SIDES
    slots = half * SIDES

    def kernel(
        table_hbm, blocks_ref, out_ref, table_ref, held, shared, count, table_sem, in_sem, main_sem,
        shared_sem,
    ):
        me = lax.axis_index("ka")
        base = me * block_local
        first = jnp.where(me < half, 0, half)
        copy = pltpu.make_async_copy(table_hbm, table_ref, table_sem)
        copy.start()
        copy.wait()

        def start(d, carry):
            device = first + lax.rem(d, half)
            device = jnp.where(d < half, device, mirror_of(device, ka_count))
            taken = jnp.int32(0)
            for b in range(point_local):
                for a in range(row_count):
                    local = table_ref[a, device * point_local + b] - base
                    hit = (local >= 0) & (local < block_local) & (taken < CAP)

                    @pl.when(hit)
                    def _():
                        at = d * CAP + taken
                        pltpu.make_async_copy(
                            blocks_ref.at[local], held.at[at], in_sem.at[at]
                        ).start()

                    taken = taken + hit.astype(jnp.int32)
            count[d] = taken
            return carry

        lax.fori_loop(0, slots, start, 0)

        def main_copy(d, s):
            return pltpu.make_async_copy(
                held.at[d * CAP + s, :, pl.ds(0, MAIN)],
                out_ref.at[lax.rem(d, half), d // half, :, pl.ds(s * MAIN, MAIN)],
                main_sem.at[d * CAP + s],
            )

        def shared_copy(d):
            return pltpu.make_async_copy(
                shared.at[d],
                out_ref.at[lax.rem(d, half), d // half, :, pl.ds(CAP * MAIN, 2 * HALF)],
                shared_sem.at[d],
            )

        def pack(d, carry):
            for s in range(CAP):

                @pl.when(count[d] > s)
                def _():
                    at = d * CAP + s
                    pltpu.make_async_copy(blocks_ref.at[0], held.at[at], in_sem.at[at]).wait()
                    main_copy(d, s).start()
                    shared[d, :, s * HALF : s * HALF + rest] = held[at, :, MAIN:]

            @pl.when(count[d] > 0)
            def _():
                shared_copy(d).start()

            return carry

        lax.fori_loop(0, slots, pack, 0)

        def finish(d, carry):
            for s in range(CAP):

                @pl.when(count[d] > s)
                def _():
                    main_copy(d, s).wait()

            @pl.when(count[d] > 0)
            def _():
                shared_copy(d).wait()

            return carry

        lax.fori_loop(0, slots, finish, 0)

    return pl.pallas_call(
        kernel,
        out_shape=jax.ShapeDtypeStruct((half, SIDES, depth, WIDE), jnp.bfloat16),
        in_specs=[HBM, HBM],
        out_specs=HBM,
        scratch_shapes=[
            pltpu.SMEM(table.shape, jnp.int32),
            pltpu.VMEM((slots * CAP, depth, waves), jnp.bfloat16),
            pltpu.VMEM((slots, depth, 2 * HALF), jnp.bfloat16),
            pltpu.SMEM((slots,), jnp.int32),
            pltpu.SemaphoreType.DMA,
            pltpu.SemaphoreType.DMA((slots * CAP,)),
            pltpu.SemaphoreType.DMA((slots * CAP,)),
            pltpu.SemaphoreType.DMA((slots,)),
        ],
        compiler_params=pltpu.CompilerParams(vmem_limit_bytes=LIMIT),
        name="gather_blocks",
    )(table, blocks)


def spread_vectors(vec_ref, keep_second):
    count, pairs = vec_ref.shape
    row = lax.broadcasted_iota(jnp.int32, (count * 16, pairs), 0)
    lane = lax.broadcasted_iota(jnp.int32, (count * 16, pairs), 1)
    values = vec_ref[...].astype(jnp.float32)
    values = jnp.concatenate(
        [jnp.broadcast_to(values[i : i + 1], (16, pairs)) for i in range(count)], axis=0
    )
    values = jnp.where(lane // 16 == row % 16, values, 0.0).astype(jnp.bfloat16)
    at = lax.broadcasted_iota(jnp.int32, (pairs, pairs), 0)
    to = lax.broadcasted_iota(jnp.int32, (pairs, pairs), 1)
    index = to % 16 if keep_second else to // 16
    pick = jnp.where(at % 16 == index, 1.0, 0.0).astype(jnp.bfloat16)
    return jnp.dot(values, pick, preferred_element_type=jnp.float32).reshape(count, 16, pairs)


def densities(side, table, rows, pieces, plane, vecs, sizes):
    ka_count, block_local, depth, waves = sizes
    row_count = table.shape[0]
    point_local = table.shape[1] // ka_count
    pair_count = row_count * point_local
    grid = rows.shape[1]
    mid = grid // 2
    points = mid + TAIL
    width = WIDE_ONE
    half = ka_count // SIDES
    pairs = NV * NV
    block = 256
    n_piece = len(pieces)
    n_vec = len(vecs)
    make_plane = not plane

    def wave(first, step, lanes, count):
        point = lax.broadcasted_iota(jnp.int32, (TAIL, lanes), 0) + step * TAIL
        column = lax.broadcasted_iota(jnp.int32, (TAIL, lanes), 1)
        if lanes == WIDE_ONE:
            column = jnp.where(column < MAIN + HALF, column, column - HALF)
        phase = (first + column) * point
        phase = phase & (grid - 1) if grid & (grid - 1) == 0 else lax.rem(phase, grid)
        away = jnp.abs(phase - grid // 2)
        z = 1.0 - away.astype(jnp.float32) * (4.0 / grid)
        square = z * z
        value = jnp.zeros_like(z)
        for k in (11, 9, 7, 5, 3, 1):
            term = (math.pi / 2) ** k / math.factorial(k) * (-1.0) ** (k // 2)
            value = value * square + term
        value = value * z * (-math.sqrt(2.0 / grid))
        return jnp.where(column < count, value, 0.0).astype(jnp.bfloat16)

    def kernel(*refs):
        refs = list(refs)
        take = lambda count: [refs.pop(0) for _ in range(count)]
        table_hbm, row_hbm = take(2)
        piece_hbm = take(n_piece)
        plane_in = take(0 if make_plane else 2)
        vec_refs = take(n_vec)
        vale_ref, cond_ref, list_ref = take(3)
        vec_out = take(n_vec)
        plane_out = take(2 if make_plane else 0)
        table_ref, row_raw, ket_raw, vplane, cplane = take(5)
        row1, row2, ket1, ket2, fv, fc, vbuf, cbuf, seen = take(9)
        load_sem, out_sem, plane_sem = take(3)

        me = lax.axis_index("ka")
        source = me if side == 0 else mirror_of(me, ka_count)
        first = jnp.where(me < half, 0, half)

        loads = [
            pltpu.make_async_copy(table_hbm, table_ref, load_sem.at[0]),
            pltpu.make_async_copy(row_hbm, row_raw, load_sem.at[1]),
        ]
        low = 0
        for i, ref in enumerate(piece_hbm):
            size = ref.shape[0]
            loads.append(
                pltpu.make_async_copy(ref, ket_raw.at[pl.ds(low, size)], load_sem.at[2 + i])
            )
            low += size
        for i, (ref, to) in enumerate(zip(plane_in, (vplane, cplane))):
            loads.append(pltpu.make_async_copy(ref, to, load_sem.at[4 + i]))
        for load in loads:
            load.start()

        if make_plane:
            low = lax.axis_index("ga") * depth

            def fill(step, carry):
                at = pl.ds(pl.multiple_of(step * TAIL, TAIL), TAIL)
                vplane[at, :] = wave(low, step, depth, depth)
                cplane[at, :] = wave(0, step, width, waves)
                return carry

            lax.fori_loop(0, points // TAIL, fill, 0)
            stores = [
                pltpu.make_async_copy(ref, to, plane_sem.at[i])
                for i, (ref, to) in enumerate(zip((vplane, cplane), plane_out))
            ]
            for store in stores:
                store.start()
        else:
            stores = []

        for i in range(n_vec):
            vec_out[i][...] = spread_vectors(vec_refs[i], i == 0)

        at = lax.broadcasted_iota(jnp.int32, (2 * block, block), 0)
        to = lax.broadcasted_iota(jnp.int32, (2 * block, block), 1)
        flip = ((at < block) & (at + to == block)) | ((at == block) & (to == 0))
        flip = jnp.where(flip, 1.0, 0.0).astype(jnp.bfloat16)

        def fold(src, low, size, put):
            rows_at = slice(low, low + size)
            for j in range(mid // block):
                lanes = slice(j * block, (j + 1) * block)
                put(0, lanes, src[rows_at, lanes].astype(jnp.float32))
                begin = grid - (j + 1) * block
                end = begin + (block if j == 0 else 2 * block)
                turned = jnp.dot(
                    src[rows_at, begin:end], flip[: end - begin], preferred_element_type=jnp.float32
                )
                put(1, lanes, turned)
            lane = lax.broadcasted_iota(jnp.int32, (size, TAIL), 1)
            last = src[rows_at, mid : mid + TAIL].astype(jnp.float32)
            put(0, slice(mid, points), jnp.where(lane == 0, last, 0.0))

        def put_whole(one, two):
            def put(which, lanes, values):
                ref = two if which else one
                ref[:, :, :, lanes] = values.reshape(-1, 2, 16, values.shape[1])

            return put

        def put_part(one, two, kind):
            def put(which, lanes, values):
                ref = two if which else one
                for b in range(point_local):
                    ref[b, kind, :, lanes] = values[b * 16 : (b + 1) * 16]

            return put

        loads[0].wait()
        loads[1].wait()
        fold(row_raw, 0, row_raw.shape[0], put_whole(row1, row2))
        for i in range(n_piece):
            loads[2 + i].wait()
        if n_piece == 1:
            fold(ket_raw, 0, ket_raw.shape[0], put_whole(ket1, ket2))
        else:
            kind = lax.axis_index("ga") % 2
            size = point_local * 16
            fold(ket_raw, 0, size, put_part(ket1, ket2, kind))
            fold(ket_raw, size, size, put_part(ket1, ket2, 1 - kind))
        for load in loads[2 + n_piece :]:
            load.wait()

        for t in range(half):
            seen[t] = 0
        for f in range(4):
            list_ref[f] = 0

        def outputs(p, slot):
            return (
                pltpu.make_async_copy(vbuf.at[slot], vale_ref.at[p], out_sem.at[0, slot]),
                pltpu.make_async_copy(cbuf.at[slot], cond_ref.at[p], out_sem.at[1, slot]),
            )

        def pair(p, carry):
            b = p // row_count
            a = lax.rem(p, row_count)
            owner = table_ref[a, source * point_local + b] // block_local - first

            @pl.when((owner >= 0) & (owner < half))
            def _():
                at = list_ref[0]
                list_ref[1 + 3 * at] = p
                list_ref[2 + 3 * at] = owner
                list_ref[3 + 3 * at] = seen[owner]
                list_ref[0] = at + 1
                seen[owner] = seen[owner] + 1
                slot = lax.rem(at, 2)

                @pl.when(at >= 2)
                def _():
                    for copy in outputs(p, slot):
                        copy.wait()

                for kind, products, plane_ref, out in (
                    (0, fv, vplane, vbuf),
                    (1, fc, cplane, cbuf),
                ):
                    total = None
                    for low in range(0, points, CHUNK):
                        high = min(low + CHUNK, points)
                        for t in range(low, high, 128):
                            lanes = slice(t, t + 128)
                            k1 = ket1[b, kind, :, lanes]
                            k2 = ket2[b, kind, :, lanes] if t < mid else None
                            for c in range(16):
                                value = row1[a, kind, c : c + 1, lanes] * k1
                                if t < mid:
                                    value += row2[a, kind, c : c + 1, lanes] * k2
                                products[c * 16 : (c + 1) * 16, lanes] = value.astype(jnp.bfloat16)
                        part = jnp.dot(
                            products[:, low:high],
                            plane_ref[low:high, :],
                            preferred_element_type=jnp.float32,
                        )
                        total = part if total is None else total + part
                    out[slot] = (total.T if kind else total).astype(jnp.bfloat16)
                for copy in outputs(p, slot):
                    copy.start()

            return carry

        lax.fori_loop(0, pair_count, pair, 0)
        count = list_ref[0]
        for back in (1, 2):

            @pl.when(count >= back)
            def _():
                for copy in outputs(0, lax.rem(count - back, 2)):
                    copy.wait()

        for store in stores:
            store.wait()

    folded = lambda count: pltpu.VMEM((count, 2, 16, points), jnp.float32)
    plane_shapes = [
        jax.ShapeDtypeStruct((points, depth), jnp.bfloat16),
        jax.ShapeDtypeStruct((points, width), jnp.bfloat16),
    ]
    result = pl.pallas_call(
        kernel,
        out_shape=[
            jax.ShapeDtypeStruct((pair_count, pairs, depth), jnp.bfloat16),
            jax.ShapeDtypeStruct((pair_count, width, pairs), jnp.bfloat16),
            jax.ShapeDtypeStruct((1 + 3 * pair_count,), jnp.int32),
        ]
        + [jax.ShapeDtypeStruct((vec.shape[0], 16, pairs), jnp.float32) for vec in vecs]
        + (plane_shapes if make_plane else []),
        in_specs=[HBM] * (2 + n_piece + len(plane)) + [VMEM] * n_vec,
        out_specs=[HBM, HBM, SMEM] + [VMEM] * n_vec + ([HBM, HBM] if make_plane else []),
        scratch_shapes=[
            pltpu.SMEM(table.shape, jnp.int32),
            pltpu.VMEM(rows.shape, jnp.bfloat16),
            pltpu.VMEM((point_local * 32, grid), jnp.bfloat16),
            pltpu.VMEM((points, depth), jnp.bfloat16),
            pltpu.VMEM((points, width), jnp.bfloat16),
            folded(row_count),
            folded(row_count),
            folded(point_local),
            folded(point_local),
            pltpu.VMEM((pairs, points), jnp.bfloat16),
            pltpu.VMEM((pairs, points), jnp.bfloat16),
            pltpu.VMEM((2, pairs, depth), jnp.bfloat16),
            pltpu.VMEM((2, width, pairs), jnp.bfloat16),
            pltpu.SMEM((half,), jnp.int32),
            pltpu.SemaphoreType.DMA((6,)),
            pltpu.SemaphoreType.DMA((2, 2)),
            pltpu.SemaphoreType.DMA((2,)),
        ],
        compiler_params=pltpu.CompilerParams(vmem_limit_bytes=LIMIT),
        cost_estimate=pl.CostEstimate(
            flops=5 * 10**10 if side else 1, bytes_accessed=10**6, transcendentals=0
        ),
        name="densities_mirror" if side else "densities_own",
    )(table, rows, *pieces, *plane, *vecs)
    return result[:3], result[3 : 3 + n_vec], result[3 + n_vec :]


def images(incoming, sides, vecs, row_vec, counts, row_scale, col_scale, wave_count):
    pair_count, pairs, depth = sides[0][0].shape
    width = sides[0][1].shape[1]
    vec_count, row_count, point_local = counts
    rest = wave_count - MAIN
    most = SIDES * pair_count

    def kernel(*refs):
        refs = list(refs)
        take = lambda count: [refs.pop(0) for _ in range(count)]
        (block_ref,) = take(1)
        side_refs = [take(3) for _ in range(SIDES)]
        vec_hbm = take(SIDES)
        rowvec_ref, out_ref = take(2)
        block_buf, vale_buf, cond_buf, vec_buf, even, odd, row_sum, col_sum = take(8)
        main_sem, shared_sem, vale_sem, cond_sem, vec_sem = take(5)

        own_count = side_refs[0][2][0]
        count = own_count + side_refs[1][2][0]

        def copies(k, at, i):
            vale_ref, cond_ref, list_ref = side_refs[k]
            p, owner, rank = (list_ref[1 + 3 * at + f] for f in range(3))
            lanes = pl.ds(pl.multiple_of(rank * MAIN, MAIN), MAIN)
            return (
                pltpu.make_async_copy(vale_ref.at[p], vale_buf.at[i], vale_sem.at[i]),
                pltpu.make_async_copy(
                    block_ref.at[owner, k, :, lanes],
                    block_buf.at[i, :, pl.ds(0, MAIN)],
                    main_sem.at[i],
                ),
                pltpu.make_async_copy(
                    block_ref.at[owner, k, :, pl.ds(CAP * MAIN, 2 * HALF)],
                    block_buf.at[i, :, pl.ds(MAIN, 2 * HALF)],
                    shared_sem.at[i],
                ),
                pltpu.make_async_copy(cond_ref.at[p], cond_buf.at[i], cond_sem.at[i]),
            )

        for k in range(SIDES):

            def start(at, carry):
                for copy in copies(k, at, at + (own_count if k else 0)):
                    copy.start()
                return carry

            lax.fori_loop(0, side_refs[k][2][0], start, 0)

        vec_copies = [
            pltpu.make_async_copy(vec_hbm[k], vec_buf.at[k], vec_sem.at[k]) for k in range(SIDES)
        ]
        for copy in vec_copies:
            copy.start()
        row_sum[...] = jnp.zeros(row_sum.shape, jnp.float32)
        col_sum[...] = jnp.zeros(col_sum.shape, jnp.float32)
        odd[...] = jnp.zeros(odd.shape, jnp.float32)
        for copy in vec_copies:
            copy.wait()

        def field(i, f):
            i = jnp.clip(i, 0, count - 1)
            own = side_refs[0][2][1 + 3 * jnp.minimum(i, pair_count - 1) + f]
            other = side_refs[1][2][1 + 3 * jnp.maximum(i - own_count, 0) + f]
            return jnp.where(i < own_count, own, other)

        def arrived(i):
            for copy in copies(0, 0, i):
                copy.wait()

        def multiply(i, into):
            rank = field(i, 2)
            at = jnp.minimum(i, count - 1)
            screened = jnp.dot(
                vale_buf[at], block_buf[at], preferred_element_type=jnp.float32
            )
            lane = lax.broadcasted_iota(jnp.int32, (1, WIDE_ONE), 1)
            begin = MAIN + rank * HALF
            mine = (lane < MAIN) | ((lane >= begin) & (lane < begin + rest))
            screened = jnp.where(mine, screened, 0.0).astype(jnp.bfloat16)
            matrix = jnp.dot(screened, cond_buf[at], preferred_element_type=jnp.float32)
            into[...] = jnp.where(i < count, matrix, 0.0)

        def contract(i, matrix):
            p = field(i, 0)
            k = (jnp.clip(i, 0, count - 1) >= own_count).astype(jnp.int32)
            b = p // row_count
            a = lax.rem(p, row_count)
            totals = [jnp.zeros((16, pairs), jnp.float32)] * vec_count
            ket = [vec_buf[k, n * point_local + b] for n in range(vec_count)]
            for v in range(16):
                part = matrix[v * 16 : (v + 1) * 16, :]
                for n in range(vec_count):
                    term = part * ket[n]
                    row_sum[a, n, v] += term[:8] + term[8:]
                    totals[n] += part * rowvec_ref[n * row_count + a, v : v + 1, :]
            for n in range(vec_count):
                col_sum[k, n, b] += totals[n]

        def two(j, carry):
            arrived(2 * j)

            @pl.when(2 * j + 1 < count)
            def _():
                arrived(2 * j + 1)

            multiply(2 * j, even)
            contract(2 * j - 1, odd)
            multiply(2 * j + 1, odd)
            contract(2 * j, even)
            return carry

        trips = (count + 1) // 2
        lax.fori_loop(0, trips, two, 0)

        @pl.when(count > 0)
        def _():
            contract(2 * trips - 1, odd)

        def spread(values, keep_first, scale):
            at = lax.broadcasted_iota(jnp.int32, (pairs, pairs), 0)
            to = lax.broadcasted_iota(jnp.int32, (pairs, pairs), 1)
            index = at // 16 if keep_first else at % 16
            pick = jnp.where(index == to % 16, 1.0, 0.0).astype(jnp.bfloat16)
            high = values.astype(jnp.bfloat16)
            low = (values - high.astype(jnp.float32)).astype(jnp.bfloat16)
            wide = jnp.dot(high, pick, preferred_element_type=jnp.float32) + jnp.dot(
                low, pick, preferred_element_type=jnp.float32
            )
            row = lax.broadcasted_iota(jnp.int32, wide.shape, 0)
            lane = lax.broadcasted_iota(jnp.int32, wide.shape, 1)
            wide = jnp.where(row % 16 == lane // 16, wide, 0.0)
            return jnp.sum(wide.reshape(-1, 16, pairs), axis=1) * scale

        cols = vec_count * point_local
        rows = vec_count * row_count
        columns = spread(col_sum[...].reshape(-1, pairs), False, col_scale)
        out_ref[:cols] = columns[:cols]
        out_ref[cols + rows :] = columns[cols:]
        summed = jnp.sum(row_sum[...].reshape(-1, 8, pairs), axis=1)
        out_ref[cols : cols + rows] = spread(summed, True, row_scale)

    total = vec_count * (SIDES * point_local + row_count)
    return pl.pallas_call(
        kernel,
        out_shape=jax.ShapeDtypeStruct((total, pairs), jnp.float32),
        in_specs=[HBM] + [HBM, HBM, SMEM] * SIDES + [HBM] * SIDES + [VMEM],
        out_specs=VMEM,
        scratch_shapes=[
            pltpu.VMEM((most, depth, WIDE_ONE), jnp.bfloat16),
            pltpu.VMEM((most, pairs, depth), jnp.bfloat16),
            pltpu.VMEM((most, width, pairs), jnp.bfloat16),
            pltpu.VMEM((SIDES,) + vecs[0].shape, jnp.float32),
            pltpu.VMEM((pairs, pairs), jnp.float32),
            pltpu.VMEM((pairs, pairs), jnp.float32),
            pltpu.VMEM((row_count, vec_count, 16, 8, pairs), jnp.float32),
            pltpu.VMEM((SIDES, vec_count, point_local, 16, pairs), jnp.float32),
        ]
        + [pltpu.SemaphoreType.DMA((most,))] * 4
        + [pltpu.SemaphoreType.DMA((SIDES,))],
        compiler_params=pltpu.CompilerParams(vmem_limit_bytes=LIMIT),
        name="images",
    )(incoming, *sides[0], *sides[1], *vecs, row_vec)


def swap(values, axis, step):
    perm = [(i, i ^ step) for i in range(lax.axis_size(axis))]
    return lax.ppermute(values, axis, perm)


def on_device(row_orbitals, orbitals, screening, pair_blocks, row_vectors, vectors):
    ka_count = lax.axis_size("ka")
    ga_count = lax.axis_size("ga")
    half = ka_count // SIDES
    row_count = row_orbitals.shape[0]
    point_local, bands, grid = orbitals.shape
    block_local, wave_count, slice_width = screening.shape
    vec_count = vectors.shape[0]

    kind = lax.axis_index("ga") % 2
    part = lax.dynamic_slice_in_dim(orbitals, kind * NV, NV, 1)
    part = part.reshape(point_local * NV, grid)
    fetched = swap(part, "ka", half)
    mirror_vectors = swap(vectors, "ka", half)

    table = pair_blocks.T
    outgoing = gather_blocks(table, jnp.swapaxes(screening, 1, 2), ka_count)
    outgoing, table = lax.optimization_barrier((outgoing, table))
    groups = [list(range(half)), list(range(half, ka_count))]
    incoming = lax.all_to_all(
        outgoing, "ka", split_axis=0, concat_axis=0, tiled=True, axis_index_groups=groups
    )

    rows = row_orbitals.reshape(row_count * bands, grid)
    sizes = (ka_count, block_local, slice_width, wave_count)
    flat = lambda values: values.reshape(-1, NV * NC)
    own, (own_vec, row_vec), plane = densities(
        0,
        table,
        rows,
        (orbitals.reshape(point_local * bands, grid),),
        (),
        (flat(vectors), flat(row_vectors)),
        sizes,
    )
    fetched, own_vec = lax.optimization_barrier((fetched, own_vec))
    passed = swap(fetched, "ga", 1)
    mirrored, (mirror_vec,), _ = densities(
        1, table, rows, (fetched, passed), plane, (flat(mirror_vectors),), sizes
    )
    row_scale = float(wave_count * NV * NC * point_local * ka_count) ** (-0.5)
    col_scale = float(wave_count * NV * NC * row_count) ** (-0.5)
    part = images(
        incoming,
        (own, mirrored),
        (own_vec, mirror_vec),
        row_vec,
        (vec_count, row_count, point_local),
        row_scale,
        col_scale,
        wave_count,
    )
    step = 1
    while step < ga_count:
        part = part + swap(part, "ga", step)
        step *= 2
    cols = vec_count * point_local
    column = part[:cols]
    row = part[cols:]
    other = swap(row, "ka", half)
    column = column + other[-cols:]
    row = row[:-cols] + other[:-cols]
    step = 1
    while step < half:
        row = row + swap(row, "ka", step)
        step *= 2
    row = row.reshape(row_count, vec_count, NV * NC).transpose(1, 0, 2)
    return row, column.reshape(vec_count, point_local, NV * NC)


def solution(mesh):
    return jax.shard_map(
        on_device,
        mesh=mesh,
        in_specs=(P(), P("ka", None, None), P("ka", None, "ga"), P(), P(), P(None, "ka", None)),
        out_specs=(P(), P(None, "ka", None)),
        check_vma=False,
    )
```

time: 359 us -> 108 us (0.30); the launches traced: 352 us -> 107 us
  matrix products: 152 us -> 0 us
  local copies, waits for them, and re-layouts: 102 us -> 6.68 us
  Pallas kernels: 0 us -> 53.7 us
  blocking collectives: 49.5 us -> 0 us
  other arithmetic: 27.3 us -> 0.83 us
  waiting for transfers between devices: 0.02 us -> 22.9 us
  starting transfers between devices: 7.61 us -> 22.7 us
  between operations: 14.6 us -> 0.73 us
    dot_general x15 -> x0, matrix products: 152 us -> none  [the longest x8 99.5 us: densities_one(): lax.dot_general(weighted.reshape(-1, grid), orbitals[:, lower:upper].resh...]
    pallas_call x0 -> x4, Pallas kernels: none -> 53.7 us  [the longest x2 34 us: densities(): pl.pallas_call(kernel, out_shape=[jax.ShapeDtypeStruct((pair_count, pairs...]
    psum x2 -> x0, blocking collectives: 49.5 us -> none  [the longest x1 41.1 us: on_device(): row_total = lax.psum(row_part, ('ka', 'ga'))]
    reshape x7 -> x6, local copies, waits for them, and re-layouts: 43.1 us -> 3.06 us  [the longest x3 1.82 us: on_device(): flat = lambda values: values.reshape(-1, NV * NC)]
    another operation x5 -> x0, local copies, waits for them, and re-layouts: 36.7 us -> none  [the longest x1 19.6 us: on_device(): jnp.stack([densities_one(plane, row_orbitals[row_index], orbitals, NV, NV...]
    ppermute x0 -> x8, waiting for transfers between devices: none -> 22.8 us  [swap(): return lax.ppermute(values, axis, perm)]
    ppermute x0 -> x8, starting transfers between devices: none -> 19 us  [swap(): return lax.ppermute(values, axis, perm)]
    unnamed x31 -> x6, local copies, waits for them, and re-layouts: 16.1 us -> 1.72 us
  transfers between devices with their start and end apart: 2 -> 9, of which waited for: 0 -> 6; matrix products, arithmetic and copies ran while one was open for 50% -> 2% of each run, Pallas kernels for 0% -> 36%
where the time goes in v2:
time: 108 us; the launch traced here: 107 us
  Pallas kernels  53.7 us (50%)
  waiting for transfers between devices  22.9 us (21%)
  starting transfers between devices  22.7 us (21%)
  local copies, waits for them, and re-layouts  6.68 us (6%)
    pallas_call x2, Pallas kernels, densities(): pl.pallas_call(kernel, out_shape=[jax.ShapeDtypeStruct((pair_count, pairs...  34 us
    ppermute x8, waiting for transfers between devices, swap(): return lax.ppermute(values, axis, perm)  22.8 us
    ppermute x8, starting transfers between devices, swap(): return lax.ppermute(values, axis, perm)  19 us
    pallas_call x1, Pallas kernels, images(): pl.pallas_call(kernel, out_shape=jax.ShapeDtypeStruct((total, pairs), jnp...  14.9 us
    pallas_call x1, Pallas kernels, gather_blocks(): pl.pallas_call(kernel, out_shape=jax.ShapeDtypeStruct((half, SIDES, depth...  4.74 us
    all_to_all x1, starting transfers between devices, on_device(): lax.all_to_all(outgoing, 'ka', split_axis=0, concat_axis=0, tiled=True, a...  3.72 us
  transfers between devices with their start and end apart: 9, of which 6 were waited for; matrix products, arithmetic and copies ran while one was open for 2% of the time, Pallas kernels for 36%

profile of v2, /device:TPU:0, one launch (start us, length us, event | category | flops | bytes accessed | tf_op | source)
XLA Modules:
  0.0 107.4 jit_solution(6489791674325944828)
XLA Ops:
  0.6 1.9 %constant_dynamic-slice_fusion = bf16[4,16,4096]{2,1,0:T(8,128)(2,1)} fusion(bf16[4,32,4096]{2,1,0:T(8,128)(2,1)} %param.7, s32[]{:T(128)S(6)} %select_n.11), kind=kLoop, calls=%fused_computation.3 | loop fusion | bytes 1048580 | tf_op jit(solution)/shard_map/dynamic_slice | solution.py:589
  2.5 4.0 %collective-permute-start = (bf16[64,4096]{1,0:T(8,128)(2,1)}, bf16[64,4096]{1,0:T(8,128)(2,1)}, u32[]{:S(2)}, u32[]{:S(2)}) collective-permute-start(bf16[64,4096]{1,0:T(8,128)(2,1)} %bitcast.4), channel_id=1, source_target_pairs={{0,16},{2,18},{4,20},{6,22},{8,24},{10,26},{12,28},{14,30},{16,0},... | collective-permute-start | bytes 1572872 | tf_op jit(solution)/shard_map/ppermute | solution.py:576
  6.6 4.7 %gather_blocks.1 = bf16[8,2,152,640]{3,2,1,0:T(8,128)(2,1)} custom-call(s32[4,64]{1,0:T(4,128)} %bitcast.13, bf16[72,152,304]{2,1,0:T(8,128)(2,1)} %bitcast.8), custom_call_target="tpu_custom_call" | custom-call | tf_op jit(solution)/shard_map/gather_blocks/pallas_call | solution.py:120
  11.3 0.0 copy-start.1
  11.3 0.0 copy-start.2
  11.3 3.7 %all-to-all-start = ((bf16[8,2,152,640]{3,2,1,0:T(8,128)(2,1)}), bf16[8,2,152,640]{3,2,1,0:T(8,128)(2,1)S(1)}, u32[]{:S(2)}, u32[]{:S(2)}) async-start(bf16[8,2,152,640]{3,2,1,0:T(8,128)(2,1)} %gather_blocks.1), calls=%async_computation | async-start | bytes 6225920 | tf_op jit(solution)/shard_map/all_to_all | solution.py:598
  15.1 0.0 copy-done.1
  15.1 0.6 reshape.31.refs_4_
  15.7 0.0 copy-done.2
  15.7 0.6 reshape.30.refs_3_
  16.3 18.8 %densities_own.1 = (bf16[16,256,152]{2,1,0:T(8,128)(2,1)}, bf16[16,384,256]{2,1,0:T(8,128)(2,1)}, s32[49]{0:T(128)}, f32[16,16,256]{2,1,0:T(8,128)}, f32[16,16,2...) custom-call(s32[4,64]{1,0:T(4,128)} %bitcast.14, bf16[128,4096]{1,0:T(8,128)(2,1)} %bitcast.10, ...), custom_call_target="tpu_custom_call" | custom-call | flops 1 | bytes 1000000 | tf_op jit(solution)/shard_map/densities_own/pallas_call | solution.py:371
  35.1 0.0 collective-permute-done.refs_2_
  35.1 1.6 %collective-permute-start.1 = (bf16[64,4096]{1,0:T(8,128)(2,1)}, bf16[64,4096]{1,0:T(8,128)(2,1)}, u32[]{:S(2)}, u32[]{:S(2)}) collective-permute-start(bf16[64,4096]{1,0:T(8,128)(2,1)} %collective-permute-done.refs_2_), channel_id=1, source_target_pairs={{0,1},{1,0},{2,3},{3,2},{4,5},{5,4},{6,7},{7,6},{8,9},{9,8},{10,11... | collective-permute-start | bytes 1572872 | tf_op jit(solution)/shard_map/ppermute | solution.py:576
  36.7 0.4 collective-permute-start.2
  37.1 14.5 %collective-permute-done.2 = bf16[4,4,256]{2,1,0:T(4,128)(2,1)S(1)} collective-permute-done((bf16[4,4,256]{2,1,0:T(4,128)(2,1)S(1)}, bf16[4,4,256]{2,1,0:T(4,128)(2,1)S(1)}, u32[]{:S(2)}, u32[]{:S(2)}) %collective-permute-start.2) | collective-permute-done | bytes 8224 | tf_op jit(solution)/shard_map/ppermute | solution.py:576
  51.6 0.6 reshape.33.refs_6_
  52.2 0.0 collective-permute-done.1.refs_3_
  52.2 15.2 %densities_mirror.1 = (bf16[16,256,152]{2,1,0:T(8,128)(2,1)}, bf16[16,384,256]{2,1,0:T(8,128)(2,1)}, s32[49]{0:T(128)}, f32[16,16,256]{2,1,0:T(8,128)}) custom-call(s32[4,64]{1,0:T(4,128)} %bitcast.15, bf16[128,4096]{1,0:T(8,128)(2,1)} %bitcast.11, bf16[64,4096]{1,0:T(8,128)(2,1)} %collective-permute-done.refs_2_, ...), custom_call_target="tpu_custom_call" | custom-call | flops 49999998976 | bytes 1000000 | tf_op jit(solution)/shard_map/densities_mirror/pallas_call | solution.py:371
  67.4 0.0 all-to-all-done.refs_0_
  67.4 0.0 copy-start
  67.4 1.7 %copy-done = bf16[8,2,152,640]{3,2,1,0:T(8,128)(2,1)} copy-done((bf16[8,2,152,640]{3,2,1,0:T(8,128)(2,1)}, bf16[8,2,152,640]{3,2,1,0:T(8,128)(2,1)S(1)}, u32[]{:S(2)}) %copy-start) | copy-done | bytes 3112984
  69.1 14.9 %images.1 = f32[48,256]{1,0:T(8,128)} custom-call(bf16[8,2,152,640]{3,2,1,0:T(8,128)(2,1)} %copy-done, bf16[16,256,152]{2,1,0:T(8,128)(2,1)} %get-tuple-element.19.refs_1_, bf16[16,384,256]{2,1,0:T(8,128)(2,1)} %get-tuple-element.20.refs_2_, s32[49]{0:T(128)} %get-tuple-element.21.refs_3_, bf16[16,256,152]{2,1,0:T(8,128)(2,1)} %get-tuple-element.26.refs_4_, ...), custom_call_target="tpu_custom_call" | custom-call | tf_op jit(solution)/shard_map/images/pallas_call | solution.py:552
  84.1 1.6 %collective-permute-start.3 = (f32[48,256]{1,0:T(8,128)}, f32[48,256]{1,0:T(8,128)S(1)}, u32[]{:S(2)}, u32[]{:S(2)}) collective-permute-start(f32[48,256]{1,0:T(8,128)} %images.1), channel_id=1, source_target_pairs={{0,1},{1,0},{2,3},{3,2},{4,5},{5,4},{6,7},{7,6},{8,9},{9,8},{10,11... | collective-permute-start | bytes 147464 | tf_op jit(solution)/shard_map/ppermute | solution.py:576
  85.6 2.8 %collective-permute-done.3 = f32[48,256]{1,0:T(8,128)S(1)} collective-permute-done((f32[48,256]{1,0:T(8,128)}, f32[48,256]{1,0:T(8,128)S(1)}, u32[]{:S(2)}, u32[]{:S(2)}) %collective-permute-start.3) | collective-permute-done | bytes 49184 | tf_op jit(solution)/shard_map/ppermute | solution.py:576
  88.4 0.8 add.27
  89.2 3.3 %collective-permute-start.4 = (f32[32,256]{1,0:T(8,128)S(1)}, f32[32,256]{1,0:T(8,128)S(1)}, u32[]{:S(2)}, u32[]{:S(2)}) collective-permute-start(f32[32,256]{1,0:T(8,128)S(1)} %slice.22), channel_id=1, source_target_pairs={{0,16},{2,18},{4,20},{6,22},{8,24},{10,26},{12,28},{14,30},{16,0},... | collective-permute-start | bytes 98312 | tf_op jit(solution)/shard_map/ppermute | solution.py:576
  92.5 1.9 %collective-permute-done.4 = f32[32,256]{1,0:T(8,128)S(1)} collective-permute-done((f32[32,256]{1,0:T(8,128)S(1)}, f32[32,256]{1,0:T(8,128)S(1)}, u32[]{:S(2)}, u32[]{:S(2)}) %collective-permute-start.4) | collective-permute-done | bytes 32800 | tf_op jit(solution)/shard_map/ppermute | solution.py:576
  94.4 1.7 %collective-permute-start.5 = (f32[16,256]{1,0:T(8,128)S(1)}, f32[16,256]{1,0:T(8,128)S(1)}, u32[]{:S(2)}, u32[]{:S(2)}) collective-permute-start(f32[16,256]{1,0:T(8,128)S(1)} %get-tuple-element.33), channel_id=1, source_target_pairs={{0,2},{2,0},{4,6},{6,4},{8,10},{10,8},{12,14},{14,12},{16,18},{18,... | collective-permute-start | bytes 49160 | tf_op jit(solution)/shard_map/ppermute | solution.py:576
  96.1 0.8 collective-permute-done.5
  96.9 3.9 %collective-permute-start.6 = (f32[16,256]{1,0:T(8,128)S(1)}, f32[16,256]{1,0:T(8,128)S(1)}, u32[]{:S(2)}, u32[]{:S(2)}) collective-permute-start(f32[16,256]{1,0:T(8,128)S(1)} %add.29), channel_id=1, source_target_pairs={{0,4},{2,6},{4,0},{6,2},{8,12},{10,14},{12,8},{14,10},{16,20},{18,... | collective-permute-start | bytes 49160 | tf_op jit(solution)/shard_map/ppermute | solution.py:576
  100.8 1.7 %collective-permute-done.6 = f32[16,256]{1,0:T(8,128)S(1)} collective-permute-done((f32[16,256]{1,0:T(8,128)S(1)}, f32[16,256]{1,0:T(8,128)S(1)}, u32[]{:S(2)}, u32[]{:S(2)}) %collective-permute-start.6) | collective-permute-done | bytes 16416 | tf_op jit(solution)/shard_map/ppermute | solution.py:576
  102.6 2.5 %collective-permute-start.7 = (f32[16,256]{1,0:T(8,128)S(1)}, f32[16,256]{1,0:T(8,128)S(1)}, u32[]{:S(2)}, u32[]{:S(2)}) collective-permute-start(f32[16,256]{1,0:T(8,128)S(1)} %add.30), channel_id=1, source_target_pairs={{0,8},{2,10},{4,12},{6,14},{8,0},{10,2},{12,4},{14,6},{16,24},{18,... | collective-permute-start | bytes 49160 | tf_op jit(solution)/shard_map/ppermute | solution.py:576
  105.1 0.6 reshape.35
  105.7 1.1 %collective-permute-done.7 = f32[16,256]{1,0:T(8,128)S(1)} collective-permute-done((f32[16,256]{1,0:T(8,128)S(1)}, f32[16,256]{1,0:T(8,128)S(1)}, u32[]{:S(2)}, u32[]{:S(2)}) %collective-permute-start.7) | collective-permute-done | bytes 16416 | tf_op jit(solution)/shard_map/ppermute | solution.py:576
  106.8 0.6 copy.10
  (6 shorter events, 0.0 us)
Async XLA Ops:
  2.5 32.6 %collective-permute-start = (bf16[64,4096]{1,0:T(8,128)(2,1)}, bf16[64,4096]{1,0:T(8,128)(2,1)}, u32[]{:S(2)}, u32[]{:S(2)}) collective-permute-start(bf16[64,4096]{1,0:T(8,128)(2,1)} %bitcast.4), channel_id=1, source_target_pairs={{0,16},{2,18},{4,20},{6,22},{8,24},{10,26},{12,28},{14,30},{16,0},... | collective-permute-start | bytes 1572872 | tf_op jit(solution)/shard_map/ppermute | solution.py:576
  11.3 3.7 %copy-start.1 = (bf16[4,4,256]{2,1,0:T(4,128)(2,1)S(1)}, bf16[4,4,256]{2,1,0:T(4,128)(2,1)}, u32[]{:S(2)}) copy-start(bf16[4,4,256]{2,1,0:T(4,128)(2,1)} %param.10) | copy-start | bytes 24580
  11.3 4.3 %copy-start.2 = (bf16[4,4,256]{2,1,0:T(4,128)(2,1)S(1)}, bf16[4,4,256]{2,1,0:T(4,128)(2,1)}, u32[]{:S(2)}) copy-start(bf16[4,4,256]{2,1,0:T(4,128)(2,1)} %param.11) | copy-start | bytes 24580
  11.3 56.0 %all-to-all-start = ((bf16[8,2,152,640]{3,2,1,0:T(8,128)(2,1)}), bf16[8,2,152,640]{3,2,1,0:T(8,128)(2,1)S(1)}, u32[]{:S(2)}, u32[]{:S(2)}) async-start(bf16[8,2,152,640]{3,2,1,0:T(8,128)(2,1)} %gather_blocks.1), calls=%async_computation | async-start | bytes 6225920 | tf_op jit(solution)/shard_map/all_to_all | solution.py:598
  35.1 17.1 %collective-permute-start.1 = (bf16[64,4096]{1,0:T(8,128)(2,1)}, bf16[64,4096]{1,0:T(8,128)(2,1)}, u32[]{:S(2)}, u32[]{:S(2)}) collective-permute-start(bf16[64,4096]{1,0:T(8,128)(2,1)} %collective-permute-done.refs_2_), channel_id=1, source_target_pairs={{0,1},{1,0},{2,3},{3,2},{4,5},{5,4},{6,7},{7,6},{8,9},{9,8},{10,11... | collective-permute-start | bytes 1572872 | tf_op jit(solution)/shard_map/ppermute | solution.py:576
  36.7 14.9 %collective-permute-start.2 = (bf16[4,4,256]{2,1,0:T(4,128)(2,1)S(1)}, bf16[4,4,256]{2,1,0:T(4,128)(2,1)S(1)}, u32[]{:S(2)}, u32[]{:S(2)}) collective-permute-start(bf16[4,4,256]{2,1,0:T(4,128)(2,1)S(1)} %copy-done.2), channel_id=1, source_target_pairs={{0,16},{2,18},{4,20},{6,22},{8,24},{10,26},{12,28},{14,30},{16,0},... | collective-permute-start | bytes 24584 | tf_op jit(solution)/shard_map/ppermute | solution.py:576
  67.4 1.7 %copy-start = (bf16[8,2,152,640]{3,2,1,0:T(8,128)(2,1)}, bf16[8,2,152,640]{3,2,1,0:T(8,128)(2,1)S(1)}, u32[]{:S(2)}) copy-start(bf16[8,2,152,640]{3,2,1,0:T(8,128)(2,1)S(1)} %all-to-all-done.refs_0_) | copy-start | bytes 9338884
  84.1 4.4 %collective-permute-start.3 = (f32[48,256]{1,0:T(8,128)}, f32[48,256]{1,0:T(8,128)S(1)}, u32[]{:S(2)}, u32[]{:S(2)}) collective-permute-start(f32[48,256]{1,0:T(8,128)} %images.1), channel_id=1, source_target_pairs={{0,1},{1,0},{2,3},{3,2},{4,5},{5,4},{6,7},{7,6},{8,9},{9,8},{10,11... | collective-permute-start | bytes 147464 | tf_op jit(solution)/shard_map/ppermute | solution.py:576
  89.2 5.1 %collective-permute-start.4 = (f32[32,256]{1,0:T(8,128)S(1)}, f32[32,256]{1,0:T(8,128)S(1)}, u32[]{:S(2)}, u32[]{:S(2)}) collective-permute-start(f32[32,256]{1,0:T(8,128)S(1)} %slice.22), channel_id=1, source_target_pairs={{0,16},{2,18},{4,20},{6,22},{8,24},{10,26},{12,28},{14,30},{16,0},... | collective-permute-start | bytes 98312 | tf_op jit(solution)/shard_map/ppermute | solution.py:576
  94.4 2.5 %collective-permute-start.5 = (f32[16,256]{1,0:T(8,128)S(1)}, f32[16,256]{1,0:T(8,128)S(1)}, u32[]{:S(2)}, u32[]{:S(2)}) collective-permute-start(f32[16,256]{1,0:T(8,128)S(1)} %get-tuple-element.33), channel_id=1, source_target_pairs={{0,2},{2,0},{4,6},{6,4},{8,10},{10,8},{12,14},{14,12},{16,18},{18,... | collective-permute-start | bytes 49160 | tf_op jit(solution)/shard_map/ppermute | solution.py:576
  96.9 5.7 %collective-permute-start.6 = (f32[16,256]{1,0:T(8,128)S(1)}, f32[16,256]{1,0:T(8,128)S(1)}, u32[]{:S(2)}, u32[]{:S(2)}) collective-permute-start(f32[16,256]{1,0:T(8,128)S(1)} %add.29), channel_id=1, source_target_pairs={{0,4},{2,6},{4,0},{6,2},{8,12},{10,14},{12,8},{14,10},{16,20},{18,... | collective-permute-start | bytes 49160 | tf_op jit(solution)/shard_map/ppermute | solution.py:576
  102.6 4.2 %collective-permute-start.7 = (f32[16,256]{1,0:T(8,128)S(1)}, f32[16,256]{1,0:T(8,128)S(1)}, u32[]{:S(2)}, u32[]{:S(2)}) collective-permute-start(f32[16,256]{1,0:T(8,128)S(1)} %add.30), channel_id=1, source_target_pairs={{0,8},{2,10},{4,12},{6,14},{8,0},{10,2},{12,4},{14,6},{16,24},{18,... | collective-permute-start | bytes 49160 | tf_op jit(solution)/shard_map/ppermute | solution.py:576

commit v3 on v2

v3 whole, which is shorter than its diff:
```python
import math

import jax
import jax.numpy as jnp
from jax import lax
from jax.experimental import pallas as pl
from jax.experimental.pallas import tpu as pltpu
from jax.sharding import PartitionSpec as P

NV = 16
NC = 16
CAP = 2
SIDES = 2
MAIN = 256
HALF = 64
WIDE = CAP * MAIN + 2 * HALF
WIDE_ONE = MAIN + 2 * HALF
AHEAD = 4
GROUP = 2
LIMIT = 62 << 20
TAIL = 128
CHUNK = 512
NT = (((1,), (1,)), ((), ()))
VMEM = pl.BlockSpec(memory_space=pltpu.VMEM)
SMEM = pl.BlockSpec(memory_space=pltpu.SMEM)
HBM = pl.BlockSpec(memory_space=pltpu.HBM)


def mirror_of(device, count):
    half = count // SIDES
    return jnp.where(device < half, device + half, device - half)


def gather_blocks(table, blocks, ka_count):
    row_count = table.shape[0]
    point_local = table.shape[1] // ka_count
    block_local, depth, waves = blocks.shape
    rest = waves - MAIN
    half = ka_count // SIDES
    slots = half * SIDES

    def kernel(
        table_hbm, blocks_ref, out_ref, table_ref, held, shared, count, table_sem, in_sem, main_sem,
        shared_sem,
    ):
        me = lax.axis_index("ka")
        base = me * block_local
        first = jnp.where(me < half, 0, half)
        copy = pltpu.make_async_copy(table_hbm, table_ref, table_sem)
        copy.start()
        copy.wait()

        def start(d, carry):
            device = first + lax.rem(d, half)
            device = jnp.where(d < half, device, mirror_of(device, ka_count))
            taken = jnp.int32(0)
            for b in range(point_local):
                for a in range(row_count):
                    local = table_ref[a, device * point_local + b] - base
                    hit = (local >= 0) & (local < block_local) & (taken < CAP)

                    @pl.when(hit)
                    def _():
                        at = d * CAP + taken
                        pltpu.make_async_copy(
                            blocks_ref.at[local], held.at[at], in_sem.at[at]
                        ).start()

                    taken = taken + hit.astype(jnp.int32)
            count[d] = taken
            return carry

        lax.fori_loop(0, slots, start, 0)

        def main_copy(d, s):
            return pltpu.make_async_copy(
                held.at[d * CAP + s, :, pl.ds(0, MAIN)],
                out_ref.at[lax.rem(d, half), d // half, :, pl.ds(s * MAIN, MAIN)],
                main_sem.at[d * CAP + s],
            )

        def shared_copy(d):
            return pltpu.make_async_copy(
                shared.at[d],
                out_ref.at[lax.rem(d, half), d // half, :, pl.ds(CAP * MAIN, 2 * HALF)],
                shared_sem.at[d],
            )

        def pack(d, carry):
            for s in range(CAP):

                @pl.when(count[d] > s)
                def _():
                    at = d * CAP + s
                    pltpu.make_async_copy(blocks_ref.at[0], held.at[at], in_sem.at[at]).wait()
                    main_copy(d, s).start()
                    shared[d, :, s * HALF : s * HALF + rest] = held[at, :, MAIN:]

            @pl.when(count[d] > 0)
            def _():
                shared_copy(d).start()

            return carry

        lax.fori_loop(0, slots, pack, 0)

        def finish(d, carry):
            for s in range(CAP):

                @pl.when(count[d] > s)
                def _():
                    main_copy(d, s).wait()

            @pl.when(count[d] > 0)
            def _():
                shared_copy(d).wait()

            return carry

        lax.fori_loop(0, slots, finish, 0)

    return pl.pallas_call(
        kernel,
        out_shape=jax.ShapeDtypeStruct((half, SIDES, depth, WIDE), jnp.bfloat16),
        in_specs=[HBM, HBM],
        out_specs=HBM,
        scratch_shapes=[
            pltpu.SMEM(table.shape, jnp.int32),
            pltpu.VMEM((slots * CAP, depth, waves), jnp.bfloat16),
            pltpu.VMEM((slots, depth, 2 * HALF), jnp.bfloat16),
            pltpu.SMEM((slots,), jnp.int32),
            pltpu.SemaphoreType.DMA,
            pltpu.SemaphoreType.DMA((slots * CAP,)),
            pltpu.SemaphoreType.DMA((slots * CAP,)),
            pltpu.SemaphoreType.DMA((slots,)),
        ],
        compiler_params=pltpu.CompilerParams(vmem_limit_bytes=LIMIT),
        name="gather_blocks",
    )(table, blocks)


def spread_vectors(vec_ref, keep_second):
    count, pairs = vec_ref.shape
    row = lax.broadcasted_iota(jnp.int32, (count * 16, pairs), 0)
    lane = lax.broadcasted_iota(jnp.int32, (count * 16, pairs), 1)
    values = vec_ref[...].astype(jnp.float32)
    values = jnp.concatenate(
        [jnp.broadcast_to(values[i : i + 1], (16, pairs)) for i in range(count)], axis=0
    )
    values = jnp.where(lane // 16 == row % 16, values, 0.0).astype(jnp.bfloat16)
    at = lax.broadcasted_iota(jnp.int32, (pairs, pairs), 0)
    to = lax.broadcasted_iota(jnp.int32, (pairs, pairs), 1)
    index = to % 16 if keep_second else to // 16
    pick = jnp.where(at % 16 == index, 1.0, 0.0).astype(jnp.bfloat16)
    return jnp.dot(values, pick, preferred_element_type=jnp.float32).reshape(count, 16, pairs)


def densities(side, table, rows, pieces, plane, vecs, sizes):
    ka_count, block_local, depth, waves, vec_rows = sizes
    row_count = table.shape[0]
    point_local = table.shape[1] // ka_count
    pair_count = row_count * point_local
    grid = pieces[0].shape[1] - (NV * NC if plane else 0)
    quarter = grid // 4
    segment = quarter + TAIL
    points = segment + quarter
    width = WIDE_ONE
    evens, odds = (waves + 1) // 2, waves // 2
    half = ka_count // SIDES
    pairs = NV * NV
    block = 256
    n_piece = len(pieces)
    n_vec = len(vecs) + (1 if plane else 0)
    make_plane = not plane

    def cosine(phase):
        phase = phase & (grid - 1) if grid & (grid - 1) == 0 else jnp.remainder(phase, grid)
        away = jnp.abs(phase - grid // 2)
        z = 1.0 - away.astype(jnp.float32) * (4.0 / grid)
        square = z * z
        value = jnp.zeros_like(z)
        for k in (11, 9, 7, 5, 3, 1):
            term = (math.pi / 2) ** k / math.factorial(k) * (-1.0) ** (k // 2)
            value = value * square + term
        return value * -z

    def waves_of(shape):
        lane = lax.broadcasted_iota(jnp.int32, shape, 1)
        parity = (lane >= 2 * MAIN).astype(jnp.int32)
        column = lane - MAIN - parity * MAIN
        wave = jnp.where(
            lane < MAIN, lane + lax.axis_index("ga") * depth, 2 * column + parity
        )
        return wave, (lane < depth) | ((lane >= MAIN) & (column >= 0) & (wave < waves))

    def kernel(*refs):
        refs = list(refs)
        take = lambda count: [refs.pop(0) for _ in range(count)]
        (table_hbm,) = take(1)
        row_hbm = take(1)[0] if make_plane else None
        piece_hbm = take(n_piece)
        plane_in = take(0 if make_plane else 4)
        vec_refs = take(len(vecs))
        vale_ref, cond_ref, list_ref = take(3)
        vec_out = take(n_vec)
        plane_out = take(4 if make_plane else 0)
        table_ref, ket_raw, vplane, eplane, oplane = take(5)
        row_raw, cos_part, sin_part = take(3 if make_plane else 0) or (None,) * 3
        vec_raw = None if make_plane else take(1)[0]
        bras, kets, fv, fe, fo, natural, vbuf, cbuf, seen = take(9)
        load_sem, out_sem, plane_sem = take(3)

        me = lax.axis_index("ka")
        source = me if side == 0 else mirror_of(me, ka_count)
        first = jnp.where(me < half, 0, half)

        loads = [pltpu.make_async_copy(table_hbm, table_ref, load_sem.at[0])]
        if make_plane:
            loads.append(pltpu.make_async_copy(row_hbm, row_raw, load_sem.at[1]))
        ready = len(loads)
        low = 0
        for i, ref in enumerate(piece_hbm):
            size = ref.shape[0]
            loads.append(
                pltpu.make_async_copy(
                    ref.at[:, pl.ds(0, grid)], ket_raw.at[pl.ds(low, size)], load_sem.at[2 + i]
                )
            )
            low += size
        for i, (ref, to) in enumerate(zip(plane_in, (vplane, eplane, oplane, bras))):
            loads.append(pltpu.make_async_copy(ref, to, load_sem.at[4 + i]))
        if not make_plane:
            loads.append(
                pltpu.make_async_copy(
                    piece_hbm[0].at[pl.ds(0, vec_raw.shape[0]), pl.ds(grid, pairs)],
                    vec_raw,
                    load_sem.at[8],
                )
            )
            vec_refs = [vec_raw]
        for load in loads:
            load.start()

        if make_plane:
            wave, valid = waves_of(cos_part.shape)
            point = lax.broadcasted_iota(jnp.int32, cos_part.shape, 0)
            scale = jnp.where(valid, math.sqrt(2.0 / grid), 0.0)
            cos_part[...] = cosine(wave * point) * scale
            sin_part[...] = cosine(wave * point - grid // 4) * scale
            wave8, _ = waves_of((8, cos_part.shape[1]))

            def fill(step, carry):
                at = pl.ds(pl.multiple_of(step * TAIL, TAIL), TAIL)
                turn = wave8 * (step * TAIL)
                value = cosine(turn)[:1] * cos_part[...]
                value -= cosine(turn - grid // 4)[:1] * sin_part[...]
                value = value.astype(jnp.bfloat16)
                vplane[at, :] = value[:, :depth]
                eplane[at, :] = value[:, MAIN : MAIN + evens]
                oplane[at, :] = value[:, 2 * MAIN : 2 * MAIN + odds]
                return carry

            def fill_back(step, carry):
                at = pl.ds(pl.multiple_of(segment + step * TAIL, TAIL), TAIL)
                turn = wave8[:, :MAIN] * (grid // 2 - step * TAIL)
                value = cosine(turn)[:1] * cos_part[:, :MAIN]
                value += cosine(turn - grid // 4)[:1] * sin_part[:, :MAIN]
                vplane[at, :] = value.astype(jnp.bfloat16)[:, :depth]
                return carry

            lax.fori_loop(0, segment // TAIL, fill, 0)
            lax.fori_loop(0, quarter // TAIL, fill_back, 0)

        at = lax.broadcasted_iota(jnp.int32, (2 * block, block), 0)
        to = lax.broadcasted_iota(jnp.int32, (2 * block, block), 1)
        flip = ((at < block) & (at + to == block)) | ((at == block) & (to == 0))
        flip = jnp.where(flip, 1.0, 0.0).astype(jnp.bfloat16)

        def fold(src, low, size, put):
            rows_at = slice(low, low + size)
            lane = lax.broadcasted_iota(jnp.int32, (size, block), 1)

            def turned(begin, end):
                return jnp.dot(
                    src[rows_at, begin:end], flip[: end - begin], preferred_element_type=jnp.float32
                )

            for at in range(0, quarter, block):
                end = grid - at - block
                there = src[rows_at, grid // 2 + at : grid // 2 + at + block].astype(jnp.float32)
                parts = (
                    src[rows_at, at : at + block].astype(jnp.float32),
                    turned(end, min(end + 2 * block, grid)),
                    turned(end - grid // 2, end - grid // 2 + 2 * block),
                    there if at else jnp.where(lane == 0, 0.0, there),
                )
                for k, values in enumerate(parts):
                    put(slice(k * segment + at, k * segment + at + block), values)
            for k in range(2):
                at = (2 * k + 1) * quarter
                last = src[rows_at, at : at + TAIL].astype(jnp.float32)
                at = k * segment + quarter
                put(slice(at, at + TAIL), jnp.where(lane[:, :TAIL] == 0, last, 0.0))

        def put_whole(ref):
            def put(lanes, values):
                ref[:, :, :, lanes] = values.reshape(-1, 2, 16, values.shape[1])

            return put

        def put_part(ref, kind):
            def put(lanes, values):
                for b in range(point_local):
                    ref[b, kind, :, lanes] = values[b * 16 : (b + 1) * 16]

            return put

        stores = []
        if make_plane:
            loads[1].wait()
            fold(row_raw, 0, row_raw.shape[0], put_whole(bras))
            stores = [
                pltpu.make_async_copy(ref, to, plane_sem.at[i])
                for i, (ref, to) in enumerate(zip((vplane, eplane, oplane, bras), plane_out))
            ]
            for store in stores:
                store.start()
        for i in range(n_piece):
            loads[ready + i].wait()
        if n_piece == 1:
            fold(ket_raw, 0, ket_raw.shape[0], put_whole(kets))
        else:
            kind = lax.axis_index("ga") % 2
            size = point_local * 16
            fold(ket_raw, 0, size, put_part(kets, kind))
            fold(ket_raw, size, size, put_part(kets, 1 - kind))
        for load in loads[:1] + loads[ready + n_piece :]:
            load.wait()
        for i in range(n_vec):
            vec_out[i][...] = spread_vectors(vec_refs[i], i == 0)

        for t in range(half):
            seen[t] = 0
        for f in range(4):
            list_ref[f] = 0

        def listed(p, carry):
            b = p // row_count
            a = lax.rem(p, row_count)
            owner = table_ref[a, source * point_local + b] // block_local - first

            @pl.when((owner >= 0) & (owner < half))
            def _():
                at = list_ref[0]
                list_ref[1 + 3 * at] = p
                list_ref[2 + 3 * at] = owner
                list_ref[3 + 3 * at] = seen[owner]
                list_ref[0] = at + 1
                seen[owner] = seen[owner] + 1

            return carry

        lax.fori_loop(0, pair_count, listed, 0)
        count = list_ref[0]

        def outputs(n, g):
            slot = lax.rem(n, 2)
            p = list_ref[1 + 3 * jnp.minimum(n * GROUP + g, pair_count - 1)]
            return (
                pltpu.make_async_copy(vbuf.at[slot, g], vale_ref.at[p], out_sem.at[slot, g, 0]),
                pltpu.make_async_copy(cbuf.at[slot, g], cond_ref.at[p], out_sem.at[slot, g, 1]),
            )

        def finish(n):
            for g in range(GROUP):

                @pl.when((n >= 0) & (n * GROUP + g < count))
                def _():
                    for copy in outputs(n, g):
                        copy.wait()

        def group(n, carry):
            finish(n - 2)
            slot = lax.rem(n, 2)
            entries = [list_ref[1 + 3 * jnp.minimum(n * GROUP + g, count - 1)] for g in range(GROUP)]
            places = [(lax.rem(p, row_count), p // row_count) for p in entries]

            def products(kind, t):
                spans = range(4 if t < quarter else 2)
                lanes = [slice(k * segment + t, k * segment + t + 128) for k in spans]
                for g, (a, b) in enumerate(places):
                    ket = [kets[b, kind, :, at] for at in lanes]
                    for c in range(16):
                        bra = [bras[a, kind, c : c + 1, at] for at in lanes]
                        row = g * pairs + c * 16
                        yield slice(row, row + 16), [
                            bra[k] * ket[k] + bra[k + 1] * ket[k + 1] for k in spans[::2]
                        ]

            def times(lhs, low, high, plane_ref, total):
                part = jnp.dot(
                    lhs[:, low:high], plane_ref[low:high, :], preferred_element_type=jnp.float32
                )
                return part if total is None else total + part

            sums = {"vale": None, "even": None, "odd": None}

            def cond_products(low, high):
                for t in range(low, high, 128):
                    for at, value in products(1, t):
                        if t < quarter:
                            fe[at, t : t + 128] = (value[0] + value[1]).astype(jnp.bfloat16)
                            fo[at, t : t + 128] = (value[0] - value[1]).astype(jnp.bfloat16)
                        else:
                            fe[at, t : t + 128] = value[0].astype(jnp.bfloat16)

            def cond_sums(low, high):
                sums["even"] = times(fe, low, high, eplane, sums["even"])
                if low < quarter:
                    sums["odd"] = times(fo, low, high, oplane, sums["odd"])

            def vale_products(low, high):
                for t in range(low, high, 128):
                    for at, value in products(0, t):
                        for k, part in enumerate(value):
                            to = k * segment + t
                            fv[at, to : to + 128] = part.astype(jnp.bfloat16)

            def vale_sums(low, high):
                sums["vale"] = times(fv, low, high, vplane, sums["vale"])
                if low < quarter:
                    sums["vale"] = times(fv, segment + low, segment + high, vplane, sums["vale"])

            def cond_out():
                rest = waves - MAIN
                blank = jnp.zeros((HALF - rest, pairs), jnp.bfloat16)
                for g in range(GROUP):
                    for h in range(pairs // 128):
                        rows_at = slice(g * pairs + h * 128, g * pairs + (h + 1) * 128)
                        lanes = slice(h * 128, (h + 1) * 128)
                        natural[h, pl.ds(0, evens, stride=2), :] = sums["even"][rows_at].T
                        natural[h, pl.ds(1, odds, stride=2), :] = sums["odd"][rows_at].T
                        cbuf[slot, g, :waves, lanes] = natural[h, :waves].astype(jnp.bfloat16)
                        cbuf[slot, g, MAIN + HALF : waves + HALF, lanes] = natural[
                            h, MAIN:waves
                        ].astype(jnp.bfloat16)
                    cbuf[slot, g, waves : MAIN + HALF] = blank
                    cbuf[slot, g, waves + HALF :] = blank

            chunks = [(low, min(low + CHUNK, segment)) for low in range(0, segment, CHUNK)]
            steps = [(cond_products, cond_sums, chunk) for chunk in chunks]
            steps += [(vale_products, vale_sums, chunk) for chunk in chunks]
            steps[0][0](*steps[0][2])
            for at, (_, add, chunk) in enumerate(steps):
                if at + 1 < len(steps):
                    steps[at + 1][0](*steps[at + 1][2])
                add(*chunk)
                if at == len(chunks):
                    cond_out()
            vbuf[slot] = sums["vale"].astype(jnp.bfloat16).reshape(GROUP, pairs, depth)
            for g in range(GROUP):

                @pl.when(n * GROUP + g < count)
                def _():
                    for copy in outputs(n, g):
                        copy.start()

            return carry

        trips = (count + GROUP - 1) // GROUP
        lax.fori_loop(0, trips, group, 0)
        finish(trips - 2)
        finish(trips - 1)
        for store in stores:
            store.wait()

    folded = lambda count: pltpu.VMEM((count, 2, 16, 4 * segment), jnp.float32)
    plane_shapes = [
        jax.ShapeDtypeStruct((points, depth), jnp.bfloat16),
        jax.ShapeDtypeStruct((segment, evens), jnp.bfloat16),
        jax.ShapeDtypeStruct((segment, odds), jnp.bfloat16),
        jax.ShapeDtypeStruct((row_count, 2, 16, 4 * segment), jnp.float32),
    ]
    result = pl.pallas_call(
        kernel,
        out_shape=[
            jax.ShapeDtypeStruct((pair_count, pairs, depth), jnp.bfloat16),
            jax.ShapeDtypeStruct((pair_count, width, pairs), jnp.bfloat16),
            jax.ShapeDtypeStruct((1 + 3 * pair_count,), jnp.int32),
        ]
        + [jax.ShapeDtypeStruct((vec_rows, 16, pairs), jnp.float32)] * n_vec
        + (plane_shapes if make_plane else []),
        in_specs=[HBM] * (1 + len(rows) + n_piece + len(plane)) + [VMEM] * len(vecs),
        out_specs=[HBM, HBM, SMEM] + [VMEM] * n_vec + ([HBM] * 4 if make_plane else []),
        scratch_shapes=[
            pltpu.SMEM(table.shape, jnp.int32),
            pltpu.VMEM((point_local * 32, grid), jnp.bfloat16),
            pltpu.VMEM((points, depth), jnp.bfloat16),
            pltpu.VMEM((segment, evens), jnp.bfloat16),
            pltpu.VMEM((segment, odds), jnp.bfloat16),
        ]
        + (
            [
                pltpu.VMEM(rows[0].shape, jnp.bfloat16),
                pltpu.VMEM((TAIL, 3 * MAIN), jnp.float32),
                pltpu.VMEM((TAIL, 3 * MAIN), jnp.float32),
            ]
            if make_plane
            else [pltpu.VMEM((vec_rows, pairs), jnp.bfloat16)]
        )
        + [
            folded(row_count),
            folded(point_local),
            pltpu.VMEM((GROUP * pairs, points), jnp.bfloat16),
            pltpu.VMEM((GROUP * pairs, segment), jnp.bfloat16),
            pltpu.VMEM((GROUP * pairs, quarter), jnp.bfloat16),
            pltpu.VMEM((pairs // 128, 2 * evens, 128), jnp.float32),
            pltpu.VMEM((2, GROUP, pairs, depth), jnp.bfloat16),
            pltpu.VMEM((2, GROUP, width, pairs), jnp.bfloat16),
            pltpu.SMEM((half,), jnp.int32),
            pltpu.SemaphoreType.DMA((9,)),
            pltpu.SemaphoreType.DMA((2, GROUP, 2)),
            pltpu.SemaphoreType.DMA((4,)),
        ],
        compiler_params=pltpu.CompilerParams(vmem_limit_bytes=LIMIT),
        cost_estimate=pl.CostEstimate(
            flops=5 * 10**10 if side else 1, bytes_accessed=10**6, transcendentals=0
        ),
        name="densities_mirror" if side else "densities_own",
    )(table, *rows, *pieces, *plane, *vecs)
    return result[:3], result[3 : 3 + n_vec], result[3 + n_vec :]


def images(incoming, sides, vecs, row_vec, counts, row_scale, col_scale, wave_count):
    pair_count, pairs, depth = sides[0][0].shape
    width = sides[0][1].shape[1]
    vec_count, row_count, point_local = counts
    rest = wave_count - MAIN
    most = SIDES * pair_count

    def kernel(*refs):
        refs = list(refs)
        take = lambda count: [refs.pop(0) for _ in range(count)]
        (block_ref,) = take(1)
        side_refs = [take(3) for _ in range(SIDES)]
        vec_hbm = take(SIDES)
        rowvec_hbm, out_ref = take(2)
        block_buf, vale_buf, cond_buf, vec_buf, rowvec_ref, even, odd, row_sum, col_sum = take(9)
        main_sem, shared_sem, vale_sem, cond_sem, vec_sem = take(5)

        own_count = side_refs[0][2][0]
        count = own_count + side_refs[1][2][0]

        def field(i, f):
            i = jnp.clip(i, 0, count - 1)
            own = side_refs[0][2][1 + 3 * jnp.minimum(i, pair_count - 1) + f]
            other = side_refs[1][2][1 + 3 * jnp.maximum(i - own_count, 0) + f]
            return jnp.where(i < own_count, own, other)

        def copies(k, i):
            vale_ref, cond_ref, _ = side_refs[k]
            p, owner, rank = (field(i, f) for f in range(3))
            lanes = pl.ds(pl.multiple_of(rank * MAIN, MAIN), MAIN)
            return (
                pltpu.make_async_copy(vale_ref.at[p], vale_buf.at[i], vale_sem.at[i]),
                pltpu.make_async_copy(
                    block_ref.at[owner, k, :, lanes],
                    block_buf.at[i, :, pl.ds(0, MAIN)],
                    main_sem.at[i],
                ),
                pltpu.make_async_copy(
                    block_ref.at[owner, k, :, pl.ds(CAP * MAIN, 2 * HALF)],
                    block_buf.at[i, :, pl.ds(MAIN, 2 * HALF)],
                    shared_sem.at[i],
                ),
                pltpu.make_async_copy(cond_ref.at[p], cond_buf.at[i], cond_sem.at[i]),
            )

        def start(i):
            for k in range(SIDES):
                low = own_count if k else 0
                high = count if k else own_count

                @pl.when((i >= low) & (i < high))
                def _():
                    for copy in copies(k, i):
                        copy.start()

        def arrived(i):
            for copy in copies(0, i):
                copy.wait()

        for i in range(AHEAD):
            start(i)
        vec_copies = [
            pltpu.make_async_copy(ref, to, vec_sem.at[k])
            for k, (ref, to) in enumerate(
                [(rowvec_hbm, rowvec_ref)] + [(vec_hbm[k], vec_buf.at[k]) for k in range(SIDES)]
            )
        ]
        for copy in vec_copies:
            copy.start()
        row_sum[...] = jnp.zeros(row_sum.shape, jnp.float32)
        col_sum[...] = jnp.zeros(col_sum.shape, jnp.float32)
        odd[...] = jnp.zeros(odd.shape, jnp.float32)
        for copy in vec_copies:
            copy.wait()

        def screen(i):
            at = jnp.minimum(i, count - 1)
            screened = jnp.dot(
                vale_buf[at], block_buf[at], preferred_element_type=jnp.float32
            )
            lane = lax.broadcasted_iota(jnp.int32, (1, WIDE_ONE), 1)
            begin = MAIN + field(i, 2) * HALF
            mine = (lane < MAIN) | ((lane >= begin) & (lane < begin + rest))
            return jnp.where(mine & (i < count), screened, 0.0).astype(jnp.bfloat16)

        def multiply(i, screened, into):
            at = jnp.minimum(i, count - 1)
            into[...] = jnp.dot(screened, cond_buf[at], preferred_element_type=jnp.float32)

        def contract(i, matrix):
            p = field(i, 0)
            k = (jnp.clip(i, 0, count - 1) >= own_count).astype(jnp.int32)
            b = p // row_count
            a = lax.rem(p, row_count)
            totals = [jnp.zeros((16, pairs), jnp.float32)] * vec_count
            ket = [vec_buf[k, n * point_local + b] for n in range(vec_count)]
            for v in range(16):
                part = matrix[v * 16 : (v + 1) * 16, :]
                for n in range(vec_count):
                    term = part * ket[n]
                    row_sum[n, a, v] += term[:8] + term[8:]
                    totals[n] += part * rowvec_ref[n * row_count + a, v : v + 1, :]
            for n in range(vec_count):
                col_sum[k, n, b] += totals[n]

        def two(j, carry):
            for i in range(2):
                start(2 * j + AHEAD + i)
            arrived(2 * j)

            @pl.when(2 * j + 1 < count)
            def _():
                arrived(2 * j + 1)

            first = screen(2 * j)
            second = screen(2 * j + 1)
            contract(2 * j - 1, odd)
            multiply(2 * j, first, even)
            multiply(2 * j + 1, second, odd)
            contract(2 * j, even)
            return carry

        trips = (count + 1) // 2
        lax.fori_loop(0, trips, two, 0)

        @pl.when(count > 0)
        def _():
            contract(2 * trips - 1, odd)

        def spread(values, keep_first, scale):
            at = lax.broadcasted_iota(jnp.int32, (pairs, pairs), 0)
            to = lax.broadcasted_iota(jnp.int32, (pairs, pairs), 1)
            index = at // 16 if keep_first else at % 16
            pick = jnp.where(index == to % 16, 1.0, 0.0).astype(jnp.bfloat16)
            high = values.astype(jnp.bfloat16)
            low = (values - high.astype(jnp.float32)).astype(jnp.bfloat16)
            wide = jnp.dot(high, pick, preferred_element_type=jnp.float32) + jnp.dot(
                low, pick, preferred_element_type=jnp.float32
            )
            row = lax.broadcasted_iota(jnp.int32, wide.shape, 0)
            lane = lax.broadcasted_iota(jnp.int32, wide.shape, 1)
            wide = jnp.where(row % 16 == lane // 16, wide, 0.0)
            return jnp.sum(wide.reshape(-1, 16, pairs), axis=1) * scale

        columns = spread(col_sum[...].reshape(-1, pairs), False, col_scale)
        summed = jnp.sum(row_sum[...].reshape(-1, 8, pairs), axis=1)
        summed = spread(summed, True, row_scale)
        for n in range(vec_count):
            out_ref[n] = columns[n * point_local : (n + 1) * point_local]
            out_ref[vec_count + n] = summed[n * row_count : (n + 1) * row_count]
            low = (vec_count + n) * point_local
            out_ref[2 * vec_count + n] = columns[low : low + point_local]

    assert point_local == row_count
    return pl.pallas_call(
        kernel,
        out_shape=jax.ShapeDtypeStruct((3 * vec_count, row_count, pairs), jnp.float32),
        in_specs=[HBM] + [HBM, HBM, SMEM] * SIDES + [HBM] * (SIDES + 1),
        out_specs=VMEM,
        scratch_shapes=[
            pltpu.VMEM((most, depth, WIDE_ONE), jnp.bfloat16),
            pltpu.VMEM((most, pairs, depth), jnp.bfloat16),
            pltpu.VMEM((most, width, pairs), jnp.bfloat16),
            pltpu.VMEM((SIDES,) + vecs[0].shape, jnp.float32),
            pltpu.VMEM(row_vec.shape, jnp.float32),
            pltpu.VMEM((pairs, pairs), jnp.float32),
            pltpu.VMEM((pairs, pairs), jnp.float32),
            pltpu.VMEM((vec_count, row_count, 16, 8, pairs), jnp.float32),
            pltpu.VMEM((SIDES, vec_count, point_local, 16, pairs), jnp.float32),
        ]
        + [pltpu.SemaphoreType.DMA((most,))] * 4
        + [pltpu.SemaphoreType.DMA((SIDES + 1,))],
        compiler_params=pltpu.CompilerParams(vmem_limit_bytes=LIMIT),
        name="images",
    )(incoming, *sides[0], *sides[1], *vecs, row_vec)


def swap(values, axis, step):
    perm = [(i, i ^ step) for i in range(lax.axis_size(axis))]
    return lax.ppermute(values, axis, perm)


def on_device(row_orbitals, orbitals, screening, pair_blocks, row_vectors, vectors):
    ka_count = lax.axis_size("ka")
    ga_count = lax.axis_size("ga")
    half = ka_count // SIDES
    row_count = row_orbitals.shape[0]
    point_local, bands, grid = orbitals.shape
    block_local, wave_count, slice_width = screening.shape
    vec_count = vectors.shape[0]

    kind = lax.axis_index("ga") % 2
    part = lax.dynamic_slice_in_dim(orbitals, kind * NV, NV, 1)
    part = part.reshape(point_local * NV, grid)
    flat = lambda values: values.reshape(-1, NV * NC)
    beside = jnp.pad(flat(vectors), ((0, point_local * (NV - vec_count)), (0, 0)))
    fetched = swap(jnp.concatenate([part, beside], axis=1), "ka", half)

    table = pair_blocks.T
    outgoing = gather_blocks(table, jnp.swapaxes(screening, 1, 2), ka_count)
    outgoing, table = lax.optimization_barrier((outgoing, table))
    groups = [list(range(half)), list(range(half, ka_count))]
    incoming = lax.all_to_all(
        outgoing, "ka", split_axis=0, concat_axis=0, tiled=True, axis_index_groups=groups
    )

    rows = row_orbitals.reshape(row_count * bands, grid)
    sizes = (ka_count, block_local, slice_width, wave_count, vec_count * point_local)
    own, (own_vec, row_vec), plane = densities(
        0,
        table,
        (rows,),
        (orbitals.reshape(point_local * bands, grid),),
        (),
        (flat(vectors), flat(row_vectors)),
        sizes,
    )
    fetched, own_vec = lax.optimization_barrier((fetched, own_vec))
    passed = swap(fetched, "ga", 1)
    mirrored, (mirror_vec,), _ = densities(
        1, table, (), (fetched, passed), plane, (), sizes
    )
    row_scale = float(wave_count * NV * NC * point_local * ka_count) ** (-0.5)
    col_scale = float(wave_count * NV * NC * row_count) ** (-0.5)
    part = images(
        incoming,
        (own, mirrored),
        (own_vec, mirror_vec),
        row_vec,
        (vec_count, row_count, point_local),
        row_scale,
        col_scale,
        wave_count,
    )
    step = 1
    while step < ga_count:
        part = part + swap(part, "ga", step)
        step *= 2
    column = part[:vec_count]
    row = part[vec_count:]
    other = swap(row, "ka", half)
    row = row[:vec_count] + other[:vec_count]
    other, row = lax.optimization_barrier((other, row))
    column = column + other[vec_count:]
    step = 1
    while step < half:
        row = row + swap(row, "ka", step)
        step *= 2
    return row, column


def solution(mesh):
    return jax.shard_map(
        on_device,
        mesh=mesh,
        in_specs=(P(), P("ka", None, None), P("ka", None, "ga"), P(), P(), P(None, "ka", None)),
        out_specs=(P(), P(None, "ka", None)),
        check_vma=False,
    )
```

time: 108 us -> 98.3 us (0.910)
  starting transfers between devices: 22.7 us -> 12.9 us
  waiting for transfers between devices: 22.9 us -> 27.9 us
  local copies, waits for them, and re-layouts: 6.68 us -> 3.25 us
  Pallas kernels: 53.7 us -> 50.6 us
  other arithmetic: 0.83 us -> 2.09 us
    ppermute x8 -> x7, starting transfers between devices: 19 us -> 8.43 us  [swap(): return lax.ppermute(values, axis, perm)]
    ppermute x8 -> x7, waiting for transfers between devices: 22.8 us -> 27.9 us  [swap(): return lax.ppermute(values, axis, perm)]
    pallas_call x2, Pallas kernels: 34 us -> 32.3 us  [densities(): pl.pallas_call(kernel, out_shape=[jax.ShapeDtypeStruct((pair_count, pairs...]
    pallas_call x1, Pallas kernels: 14.9 us -> 13.4 us  [images(): pl.pallas_call(kernel, out_shape=jax.ShapeDtypeStruct((3 * vec_count, row...]
    reshape x3 -> x0, local copies, waits for them, and re-layouts: 1.24 us -> none  [the longest x2 0.63 us: on_device(): row = row.reshape(row_count, vec_count, NV * NC).transpose(1, 0, 2)]
  transfers between devices with their start and end apart: 9 -> 8, of which waited for: 6 -> 6; matrix products, arithmetic and copies ran while one was open for 2% -> 1% of each run, Pallas kernels for 36% -> 38%
where the time goes in v3:
time: 98.3 us; the launch traced here: 97.5 us
  Pallas kernels  50.6 us (51%)
  waiting for transfers between devices  27.9 us (28%)
  starting transfers between devices  12.9 us (13%)
  local copies, waits for them, and re-layouts  3.25 us (3%)
  other arithmetic  2.09 us (2%)
    pallas_call x2, Pallas kernels, densities(): pl.pallas_call(kernel, out_shape=[jax.ShapeDtypeStruct((pair_count, pairs...  32.3 us
    ppermute x7, waiting for transfers between devices, swap(): return lax.ppermute(values, axis, perm)  27.9 us
    pallas_call x1, Pallas kernels, images(): pl.pallas_call(kernel, out_shape=jax.ShapeDtypeStruct((3 * vec_count, row...  13.4 us
    ppermute x7, starting transfers between devices, swap(): return lax.ppermute(values, axis, perm)  8.43 us
    pallas_call x1, Pallas kernels, gather_blocks(): pl.pallas_call(kernel, out_shape=jax.ShapeDtypeStruct((half, SIDES, depth...  4.9 us
    all_to_all x1, starting transfers between devices, on_device(): lax.all_to_all(outgoing, 'ka', split_axis=0, concat_axis=0, tiled=True, a...  4.48 us
  transfers between devices with their start and end apart: 8, of which 6 were waited for; matrix products, arithmetic and copies ran while one was open for 1% of the time, Pallas kernels for 38%

profile of v3, /device:TPU:0, one launch (start us, length us, event | category | flops | bytes accessed | tf_op | source)
XLA Modules:
  0.0 97.5 jit_solution(14784308441947767790)
XLA Ops:
  0.6 0.7 reshape.22.refs_3_
  1.4 0.0 copy-start
  1.4 1.1 %constant_dynamic-slice_fusion = bf16[4,16,4096]{2,1,0:T(8,128)(2,1)S(1)} fusion(bf16[4,32,4096]{2,1,0:T(8,128)(2,1)} %param.7, s32[]{:T(128)S(6)} %select_n.11), kind=kLoop, calls=%fused_computation.5 | loop fusion | bytes 1048580 | tf_op jit(solution)/shard_map/dynamic_slice | solution.py:726
  2.5 4.1 %collective-permute-start = (bf16[64,4352]{1,0:T(8,128)(2,1)S(1)}, bf16[64,4352]{1,0:T(8,128)(2,1)S(1)}, u32[]{:S(2)}, u32[]{:S(2)}) collective-permute-start(bf16[64,4352]{1,0:T(8,128)(2,1)S(1)} %fusion.1), channel_id=1, source_target_pairs={{0,16},{2,18},{4,20},{6,22},{8,24},{10,26},{12,28},{14,30},{16,0},... | collective-permute-start | bytes 1671176 | tf_op jit(solution)/shard_map/ppermute | solution.py:713
  6.6 4.9 %gather_blocks.1 = bf16[8,2,152,640]{3,2,1,0:T(8,128)(2,1)} custom-call(s32[4,64]{1,0:T(4,128)} %bitcast.9, bf16[72,152,304]{2,1,0:T(8,128)(2,1)} %bitcast.5), custom_call_target="tpu_custom_call" | custom-call | tf_op jit(solution)/shard_map/gather_blocks/pallas_call | solution.py:122
  11.5 0.0 copy-done
  11.5 0.0 copy-start.1
  11.5 4.5 %all-to-all-start = ((bf16[8,2,152,640]{3,2,1,0:T(8,128)(2,1)}), bf16[8,2,152,640]{3,2,1,0:T(8,128)(2,1)}, u32[]{:S(2)}, u32[]{:S(2)}) async-start(bf16[8,2,152,640]{3,2,1,0:T(8,128)(2,1)} %gather_blocks.1), calls=%async_computation | async-start | bytes 6225920 | tf_op jit(solution)/shard_map/all_to_all | solution.py:736
  16.0 0.0 copy-done.1
  16.0 0.6 reshape.23.refs_4_
  16.6 15.0 %densities_own.1 = (bf16[16,256,152]{2,1,0:T(8,128)(2,1)}, bf16[16,384,256]{2,1,0:T(8,128)(2,1)}, s32[49]{0:T(128)}, f32[16,16,256]{2,1,0:T(8,128)}, f32[16,16,2...) custom-call(s32[4,64]{1,0:T(4,128)} %bitcast.10, ...), custom_call_target="tpu_custom_call" | custom-call | flops 1 | bytes 1000000 | tf_op jit(solution)/shard_map/densities_own/pallas_call | solution.py:484
  31.6 0.0 collective-permute-done.refs_1_
  31.7 0.0 copy-start.2
  31.7 1.6 %collective-permute-start.1 = (bf16[64,4352]{1,0:T(8,128)(2,1)S(1)}, bf16[64,4352]{1,0:T(8,128)(2,1)S(1)}, u32[]{:S(2)}, u32[]{:S(2)}) collective-permute-start(bf16[64,4352]{1,0:T(8,128)(2,1)S(1)} %collective-permute-done.refs_1_), channel_id=1, source_target_pairs={{0,1},{1,0},{2,3},{3,2},{4,5},{5,4},{6,7},{7,6},{8,9},{9,8},{10,11... | collective-permute-start | bytes 1671176 | tf_op jit(solution)/shard_map/ppermute | solution.py:713
  33.2 13.4 %collective-permute-done.1.refs_2_ = bf16[64,4352]{1,0:T(8,128)(2,1)S(1)} collective-permute-done((bf16[64,4352]{1,0:T(8,128)(2,1)S(1)}, bf16[64,4352]{1,0:T(8,128)(2,1)S(1)}, u32[]{:S(2)}, u32[]{:S(2)}) %collective-permute-start.1) | collective-permute-done | bytes 557088 | tf_op jit(solution)/shard_map/ppermute | solution.py:713
  46.6 0.0 copy-start.3
  46.6 0.0 copy-done.2
  46.6 0.8 copy-done.3
  47.5 17.2 %densities_mirror.1 = (bf16[16,256,152]{2,1,0:T(8,128)(2,1)}, bf16[16,384,256]{2,1,0:T(8,128)(2,1)}, s32[49]{0:T(128)}, f32[16,16,256]{2,1,0:T(8,128)}) custom-call(s32[4,64]{1,0:T(4,128)} %bitcast.11, bf16[64,4352]{1,0:T(8,128)(2,1)} %copy-done.2, bf16[64,4352]{1,0:T(8,128)(2,1)} %copy-done.3, bf16[2176,152]{1,0:T(8,128)(2,1)} %get-tuple-element.28.refs_3_, ...), custom_call_target="tpu_custom_call" | custom-call | flops 49999998976 | bytes 1000000 | tf_op jit(solution)/shard_map/densities_mirror/pallas_call | solution.py:484
  64.7 0.0 all-to-all-done.refs_0_
  64.7 13.4 %images.1 = f32[12,4,256]{2,1,0:T(4,128)} custom-call(bf16[8,2,152,640]{3,2,1,0:T(8,128)(2,1)} %all-to-all-done.refs_0_, bf16[16,256,152]{2,1,0:T(8,128)(2,1)} %get-tuple-element.23.refs_1_, bf16[16,384,256]{2,1,0:T(8,128)(2,1)} %get-tuple-element.24.refs_2_, s32[49]{0:T(128)} %get-tuple-element.25.refs_3_, bf16[16,256,152]{2,1,0:T(8,128)(2,1)} %get-tuple-element.32.refs_4_, ...), custom_call_target="tpu_custom_call" | custom-call | tf_op jit(solution)/shard_map/images/pallas_call | solution.py:688
  78.2 1.6 %collective-permute-start.2 = (f32[12,4,256]{2,1,0:T(4,128)}, f32[12,4,256]{2,1,0:T(4,128)S(1)}, u32[]{:S(2)}, u32[]{:S(2)}) collective-permute-start(f32[12,4,256]{2,1,0:T(4,128)} %images.1), channel_id=1, source_target_pairs={{0,1},{1,0},{2,3},{3,2},{4,5},{5,4},{6,7},{7,6},{8,9},{9,8},{10,11... | collective-permute-start | bytes 147464 | tf_op jit(solution)/shard_map/ppermute | solution.py:713
  79.7 2.8 %collective-permute-done.2 = f32[12,4,256]{2,1,0:T(4,128)S(1)} collective-permute-done((f32[12,4,256]{2,1,0:T(4,128)}, f32[12,4,256]{2,1,0:T(4,128)S(1)}, u32[]{:S(2)}, u32[]{:S(2)}) %collective-permute-start.2) | collective-permute-done | bytes 49184 | tf_op jit(solution)/shard_map/ppermute | solution.py:713
  82.5 0.8 add.29
  83.4 0.1 collective-permute-start.3
  83.4 4.8 %collective-permute-done.3 = f32[8,4,256]{2,1,0:T(4,128)S(1)} collective-permute-done((f32[8,4,256]{2,1,0:T(4,128)S(1)}, f32[8,4,256]{2,1,0:T(4,128)S(1)}, u32[]{:S(2)}, u32[]{:S(2)}) %collective-permute-start.3) | collective-permute-done | bytes 32800 | tf_op jit(solution)/shard_map/ppermute | solution.py:713
  88.2 0.0 collective-permute-start.4
  88.3 1.2 %collective-permute-done.4 = f32[4,4,256]{2,1,0:T(4,128)S(1)} collective-permute-done((f32[4,4,256]{2,1,0:T(4,128)S(1)}, f32[4,4,256]{2,1,0:T(4,128)S(1)}, u32[]{:S(2)}, u32[]{:S(2)}) %collective-permute-start.4) | collective-permute-done | bytes 16416 | tf_op jit(solution)/shard_map/ppermute | solution.py:713
  89.4 1.1 %collective-permute-start.5 = (f32[4,4,256]{2,1,0:T(4,128)S(1)}, f32[4,4,256]{2,1,0:T(4,128)S(1)}, u32[]{:S(2)}, u32[]{:S(2)}) collective-permute-start(f32[4,4,256]{2,1,0:T(4,128)S(1)} %add.31), channel_id=1, source_target_pairs={{0,4},{2,6},{4,0},{6,2},{8,12},{10,14},{12,8},{14,10},{16,20},{18,... | collective-permute-start | bytes 49160 | tf_op jit(solution)/shard_map/ppermute | solution.py:713
  90.5 2.7 %collective-permute-done.5 = f32[4,4,256]{2,1,0:T(4,128)S(1)} collective-permute-done((f32[4,4,256]{2,1,0:T(4,128)S(1)}, f32[4,4,256]{2,1,0:T(4,128)S(1)}, u32[]{:S(2)}, u32[]{:S(2)}) %collective-permute-start.5) | collective-permute-done | bytes 16416 | tf_op jit(solution)/shard_map/ppermute | solution.py:713
  93.2 0.0 collective-permute-start.6
  93.2 0.6 slice_add_fusion
  93.8 3.1 %collective-permute-done.6 = f32[4,4,256]{2,1,0:T(4,128)S(1)} collective-permute-done((f32[4,4,256]{2,1,0:T(4,128)S(1)}, f32[4,4,256]{2,1,0:T(4,128)S(1)}, u32[]{:S(2)}, u32[]{:S(2)}) %collective-permute-start.6) | collective-permute-done | bytes 16416 | tf_op jit(solution)/shard_map/ppermute | solution.py:713
  96.9 0.6 add.33
  (5 shorter events, 0.1 us)
Async XLA Ops:
  1.4 10.1 %copy-start = (bf16[16,256]{1,0:T(8,128)(2,1)}, bf16[16,256]{1,0:T(8,128)(2,1)S(1)}, u32[]{:S(2)}) copy-start(bf16[16,256]{1,0:T(8,128)(2,1)S(1)} %reshape.22.refs_3_) | copy-start | bytes 24580
  2.5 29.2 %collective-permute-start = (bf16[64,4352]{1,0:T(8,128)(2,1)S(1)}, bf16[64,4352]{1,0:T(8,128)(2,1)S(1)}, u32[]{:S(2)}, u32[]{:S(2)}) collective-permute-start(bf16[64,4352]{1,0:T(8,128)(2,1)S(1)} %fusion.1), channel_id=1, source_target_pairs={{0,16},{2,18},{4,20},{6,22},{8,24},{10,26},{12,28},{14,30},{16,0},... | collective-permute-start | bytes 1671176 | tf_op jit(solution)/shard_map/ppermute | solution.py:713
  11.5 4.5 %copy-start.1 = (bf16[4,4,256]{2,1,0:T(4,128)(2,1)S(1)}, bf16[4,4,256]{2,1,0:T(4,128)(2,1)}, u32[]{:S(2)}) copy-start(bf16[4,4,256]{2,1,0:T(4,128)(2,1)} %param.10) | copy-start | bytes 24580
  11.5 53.2 %all-to-all-start = ((bf16[8,2,152,640]{3,2,1,0:T(8,128)(2,1)}), bf16[8,2,152,640]{3,2,1,0:T(8,128)(2,1)}, u32[]{:S(2)}, u32[]{:S(2)}) async-start(bf16[8,2,152,640]{3,2,1,0:T(8,128)(2,1)} %gather_blocks.1), calls=%async_computation | async-start | bytes 6225920 | tf_op jit(solution)/shard_map/all_to_all | solution.py:736
  31.7 15.0 %copy-start.2 = (bf16[64,4352]{1,0:T(8,128)(2,1)}, bf16[64,4352]{1,0:T(8,128)(2,1)S(1)}, u32[]{:S(2)}) copy-start(bf16[64,4352]{1,0:T(8,128)(2,1)S(1)} %collective-permute-done.refs_1_) | copy-start | bytes 1671172
  31.7 15.0 %collective-permute-start.1 = (bf16[64,4352]{1,0:T(8,128)(2,1)S(1)}, bf16[64,4352]{1,0:T(8,128)(2,1)S(1)}, u32[]{:S(2)}, u32[]{:S(2)}) collective-permute-start(bf16[64,4352]{1,0:T(8,128)(2,1)S(1)} %collective-permute-done.refs_1_), channel_id=1, source_target_pairs={{0,1},{1,0},{2,3},{3,2},{4,5},{5,4},{6,7},{7,6},{8,9},{9,8},{10,11... | collective-permute-start | bytes 1671176 | tf_op jit(solution)/shard_map/ppermute | solution.py:713
  46.6 0.8 copy-start.3
  78.2 4.4 %collective-permute-start.2 = (f32[12,4,256]{2,1,0:T(4,128)}, f32[12,4,256]{2,1,0:T(4,128)S(1)}, u32[]{:S(2)}, u32[]{:S(2)}) collective-permute-start(f32[12,4,256]{2,1,0:T(4,128)} %images.1), channel_id=1, source_target_pairs={{0,1},{1,0},{2,3},{3,2},{4,5},{5,4},{6,7},{7,6},{8,9},{9,8},{10,11... | collective-permute-start | bytes 147464 | tf_op jit(solution)/shard_map/ppermute | solution.py:713
  83.4 4.9 %collective-permute-start.3 = (f32[8,4,256]{2,1,0:T(4,128)S(1)}, f32[8,4,256]{2,1,0:T(4,128)S(1)}, u32[]{:S(2)}, u32[]{:S(2)}) collective-permute-start(f32[8,4,256]{2,1,0:T(4,128)S(1)} %slice.21), channel_id=1, source_target_pairs={{0,16},{2,18},{4,20},{6,22},{8,24},{10,26},{12,28},{14,30},{16,0},... | collective-permute-start | bytes 98312 | tf_op jit(solution)/shard_map/ppermute | solution.py:713
  88.2 1.2 %collective-permute-start.4 = (f32[4,4,256]{2,1,0:T(4,128)S(1)}, f32[4,4,256]{2,1,0:T(4,128)S(1)}, u32[]{:S(2)}, u32[]{:S(2)}) collective-permute-start(f32[4,4,256]{2,1,0:T(4,128)S(1)} %slice_add_fusion.1), channel_id=1, source_target_pairs={{0,2},{2,0},{4,6},{6,4},{8,10},{10,8},{12,14},{14,12},{16,18},{18,... | collective-permute-start | bytes 49160 | tf_op jit(solution)/shard_map/ppermute | solution.py:713
  89.4 3.7 %collective-permute-start.5 = (f32[4,4,256]{2,1,0:T(4,128)S(1)}, f32[4,4,256]{2,1,0:T(4,128)S(1)}, u32[]{:S(2)}, u32[]{:S(2)}) collective-permute-start(f32[4,4,256]{2,1,0:T(4,128)S(1)} %add.31), channel_id=1, source_target_pairs={{0,4},{2,6},{4,0},{6,2},{8,12},{10,14},{12,8},{14,10},{16,20},{18,... | collective-permute-start | bytes 49160 | tf_op jit(solution)/shard_map/ppermute | solution.py:713
  93.2 3.7 %collective-permute-start.6 = (f32[4,4,256]{2,1,0:T(4,128)S(1)}, f32[4,4,256]{2,1,0:T(4,128)S(1)}, u32[]{:S(2)}, u32[]{:S(2)}) collective-permute-start(f32[4,4,256]{2,1,0:T(4,128)S(1)} %add.32), channel_id=1, source_target_pairs={{0,8},{2,10},{4,12},{6,14},{8,0},{10,2},{12,4},{14,6},{16,24},{18,... | collective-permute-start | bytes 49160 | tf_op jit(solution)/shard_map/ppermute | solution.py:713

commit v4 on v3

--- a/solution.py
+++ b/solution.py
@@ -15,8 +15,9 @@
 HALF = 64
 WIDE = CAP * MAIN + 2 * HALF
 WIDE_ONE = MAIN + 2 * HALF
-AHEAD = 4
+AHEAD = 8
 GROUP = 2
+SPLIT = 3
 LIMIT = 62 << 20
 TAIL = 128
 CHUNK = 512
@@ -50,6 +51,24 @@
         copy.start()
         copy.wait()
 
+        def block_copy(local, d, s):
+            at = d * CAP + s
+            return pltpu.make_async_copy(blocks_ref.at[local], held.at[at], in_sem.at[at])
+
+        def main_copy(d, s):
+            return pltpu.make_async_copy(
+                held.at[d * CAP + s, :, pl.ds(0, MAIN)],
+                out_ref.at[lax.rem(d, half), d // half, :, pl.ds(s * MAIN, MAIN)],
+                main_sem.at[d * CAP + s],
+            )
+
+        def shared_copy(d):
+            return pltpu.make_async_copy(
+                shared.at[d],
+                out_ref.at[lax.rem(d, half), d // half, :, pl.ds(CAP * MAIN, 2 * HALF)],
+                shared_sem.at[d],
+            )
+
         def start(d, carry):
             device = first + lax.rem(d, half)
             device = jnp.where(d < half, device, mirror_of(device, ka_count))
@@ -61,10 +80,7 @@
 
                     @pl.when(hit)
                     def _():
-                        at = d * CAP + taken
-                        pltpu.make_async_copy(
-                            blocks_ref.at[local], held.at[at], in_sem.at[at]
-                        ).start()
+                        block_copy(local, d, taken).start()
 
                     taken = taken + hit.astype(jnp.int32)
             count[d] = taken
@@ -72,29 +88,14 @@
 
         lax.fori_loop(0, slots, start, 0)
 
-        def main_copy(d, s):
-            return pltpu.make_async_copy(
-                held.at[d * CAP + s, :, pl.ds(0, MAIN)],
-                out_ref.at[lax.rem(d, half), d // half, :, pl.ds(s * MAIN, MAIN)],
-                main_sem.at[d * CAP + s],
-            )
-
-        def shared_copy(d):
-            return pltpu.make_async_copy(
-                shared.at[d],
-                out_ref.at[lax.rem(d, half), d // half, :, pl.ds(CAP * MAIN, 2 * HALF)],
-                shared_sem.at[d],
-            )
-
         def pack(d, carry):
             for s in range(CAP):
 
                 @pl.when(count[d] > s)
                 def _():
-                    at = d * CAP + s
-                    pltpu.make_async_copy(blocks_ref.at[0], held.at[at], in_sem.at[at]).wait()
+                    block_copy(0, d, s).wait()
                     main_copy(d, s).start()
-                    shared[d, :, s * HALF : s * HALF + rest] = held[at, :, MAIN:]
+                    shared[d, :, s * HALF : s * HALF + rest] = held[d * CAP + s, :, MAIN:]
 
             @pl.when(count[d] > 0)
             def _():
@@ -139,13 +140,13 @@
     )(table, blocks)
 
 
-def spread_vectors(vec_ref, keep_second):
-    count, pairs = vec_ref.shape
+def spread_vectors(vec_ref, keep_second, order):
+    count, pairs = len(order), vec_ref.shape[1]
     row = lax.broadcasted_iota(jnp.int32, (count * 16, pairs), 0)
     lane = lax.broadcasted_iota(jnp.int32, (count * 16, pairs), 1)
     values = vec_ref[...].astype(jnp.float32)
     values = jnp.concatenate(
-        [jnp.broadcast_to(values[i : i + 1], (16, pairs)) for i in range(count)], axis=0
+        [jnp.broadcast_to(values[i : i + 1], (16, pairs)) for i in order], axis=0
     )
     values = jnp.where(lane // 16 == row % 16, values, 0.0).astype(jnp.bfloat16)
     at = lax.broadcasted_iota(jnp.int32, (pairs, pairs), 0)
@@ -155,12 +156,11 @@
     return jnp.dot(values, pick, preferred_element_type=jnp.float32).reshape(count, 16, pairs)
 
 
-def densities(side, table, rows, pieces, plane, vecs, sizes):
-    ka_count, block_local, depth, waves, vec_rows = sizes
+def densities(side, table, rows, pieces, plane, vecs, sizes, begun=()):
+    ka_count, block_local, depth, waves, vec_rows, grid = sizes
     row_count = table.shape[0]
     point_local = table.shape[1] // ka_count
     pair_count = row_count * point_local
-    grid = pieces[0].shape[1] - (NV * NC if plane else 0)
     quarter = grid // 4
     segment = quarter + TAIL
     points = segment + quarter
@@ -170,8 +170,9 @@
     pairs = NV * NV
     block = 256
     n_piece = len(pieces)
-    n_vec = len(vecs) + (1 if plane else 0)
+    n_vec = len(vecs) + side
     make_plane = not plane
+    resume = bool(begun)
 
     def cosine(phase):
         phase = phase & (grid - 1) if grid & (grid - 1) == 0 else jnp.remainder(phase, grid)
@@ -199,14 +200,16 @@
         (table_hbm,) = take(1)
         row_hbm = take(1)[0] if make_plane else None
         piece_hbm = take(n_piece)
-        plane_in = take(0 if make_plane else 4)
+        plane_in = take(len(plane))
         vec_refs = take(len(vecs))
-        vale_ref, cond_ref, list_ref = take(3)
+        list_in = take(len(begun))[2:]
+        vale_ref, cond_ref = take(2)
+        (list_ref,) = list_in or take(1)
         vec_out = take(n_vec)
-        plane_out = take(4 if make_plane else 0)
+        plane_out = take(5 if make_plane else 0)
         table_ref, ket_raw, vplane, eplane, oplane = take(5)
         row_raw, cos_part, sin_part = take(3 if make_plane else 0) or (None,) * 3
-        vec_raw = None if make_plane else take(1)[0]
+        vec_raw = take(1)[0] if side else None
         bras, kets, fv, fe, fo, natural, vbuf, cbuf, seen = take(9)
         load_sem, out_sem, plane_sem = take(3)
 
@@ -227,17 +230,21 @@
                 )
             )
             low += size
-        for i, (ref, to) in enumerate(zip(plane_in, (vplane, eplane, oplane, bras))):
+        for i, (ref, to) in enumerate(zip(plane_in, (vplane, eplane, oplane, bras, kets))):
             loads.append(pltpu.make_async_copy(ref, to, load_sem.at[4 + i]))
-        if not make_plane:
+        if side:
             loads.append(
                 pltpu.make_async_copy(
-                    piece_hbm[0].at[pl.ds(0, vec_raw.shape[0]), pl.ds(grid, pairs)],
+                    piece_hbm[0].at[:, pl.ds(grid, pairs)],
                     vec_raw,
-                    load_sem.at[8],
+                    load_sem.at[9],
                 )
             )
             vec_refs = [vec_raw]
+            vec_count = vec_rows // point_local
+            orders = [[n * 16 + b for n in range(vec_count) for b in range(point_local)]]
+        else:
+            orders = [range(vec_rows)] * n_vec
         for load in loads:
             load.start()
 
@@ -321,15 +328,16 @@
             fold(row_raw, 0, row_raw.shape[0], put_whole(bras))
             stores = [
                 pltpu.make_async_copy(ref, to, plane_sem.at[i])
-                for i, (ref, to) in enumerate(zip((vplane, eplane, oplane, bras), plane_out))
+                for i, (ref, to) in enumerate(zip((vplane, eplane, oplane, bras, kets), plane_out))
             ]
-            for store in stores:
+            for store in stores[:4]:
                 store.start()
         for i in range(n_piece):
             loads[ready + i].wait()
         if n_piece == 1:
             fold(ket_raw, 0, ket_raw.shape[0], put_whole(kets))
-        else:
+            stores[4].start()
+        elif n_piece:
             kind = lax.axis_index("ga") % 2
             size = point_local * 16
             fold(ket_raw, 0, size, put_part(kets, kind))
@@ -337,12 +345,7 @@
         for load in loads[:1] + loads[ready + n_piece :]:
             load.wait()
         for i in range(n_vec):
-            vec_out[i][...] = spread_vectors(vec_refs[i], i == 0)
-
-        for t in range(half):
-            seen[t] = 0
-        for f in range(4):
-            list_ref[f] = 0
+            vec_out[i][...] = spread_vectors(vec_refs[i], i == 0, orders[i])
 
         def listed(p, carry):
             b = p // row_count
@@ -360,8 +363,16 @@
 
             return carry
 
-        lax.fori_loop(0, pair_count, listed, 0)
+        if not resume:
+            for t in range(half):
+                seen[t] = 0
+            for f in range(4):
+                list_ref[f] = 0
+            lax.fori_loop(0, pair_count, listed, 0)
         count = list_ref[0]
+        trips = (count + GROUP - 1) // GROUP
+        begin = jnp.minimum(SPLIT, trips) if resume else 0
+        end = jnp.minimum(SPLIT, trips) if make_plane else trips
 
         def outputs(n, g):
             slot = lax.rem(n, 2)
@@ -374,7 +385,7 @@
         def finish(n):
             for g in range(GROUP):
 
-                @pl.when((n >= 0) & (n * GROUP + g < count))
+                @pl.when((n >= begin) & (n * GROUP + g < count))
                 def _():
                     for copy in outputs(n, g):
                         copy.wait()
@@ -467,10 +478,9 @@
 
             return carry
 
-        trips = (count + GROUP - 1) // GROUP
-        lax.fori_loop(0, trips, group, 0)
-        finish(trips - 2)
-        finish(trips - 1)
+        lax.fori_loop(begin, end, group, 0)
+        finish(end - 2)
+        finish(end - 1)
         for store in stores:
             store.wait()
 
@@ -480,18 +490,25 @@
         jax.ShapeDtypeStruct((segment, evens), jnp.bfloat16),
         jax.ShapeDtypeStruct((segment, odds), jnp.bfloat16),
         jax.ShapeDtypeStruct((row_count, 2, 16, 4 * segment), jnp.float32),
+        jax.ShapeDtypeStruct((point_local, 2, 16, 4 * segment), jnp.float32),
     ]
+    n_in = 1 + len(rows) + n_piece + len(plane)
+    n_list = 0 if resume else 1
     result = pl.pallas_call(
         kernel,
         out_shape=[
             jax.ShapeDtypeStruct((pair_count, pairs, depth), jnp.bfloat16),
             jax.ShapeDtypeStruct((pair_count, width, pairs), jnp.bfloat16),
-            jax.ShapeDtypeStruct((1 + 3 * pair_count,), jnp.int32),
         ]
+        + [jax.ShapeDtypeStruct((1 + 3 * pair_count,), jnp.int32)] * n_list
         + [jax.ShapeDtypeStruct((vec_rows, 16, pairs), jnp.float32)] * n_vec
         + (plane_shapes if make_plane else []),
-        in_specs=[HBM] * (1 + len(rows) + n_piece + len(plane)) + [VMEM] * len(vecs),
-        out_specs=[HBM, HBM, SMEM] + [VMEM] * n_vec + ([HBM] * 4 if make_plane else []),
+        in_specs=[HBM] * n_in + [VMEM] * len(vecs) + ([HBM, HBM, SMEM] if resume else []),
+        out_specs=[HBM, HBM]
+        + [SMEM] * n_list
+        + [VMEM] * n_vec
+        + ([HBM] * len(plane_shapes) if make_plane else []),
+        input_output_aliases={n_in: 0, n_in + 1: 1} if resume else {},
         scratch_shapes=[
             pltpu.SMEM(table.shape, jnp.int32),
             pltpu.VMEM((point_local * 32, grid), jnp.bfloat16),
@@ -506,7 +523,7 @@
                 pltpu.VMEM((TAIL, 3 * MAIN), jnp.float32),
             ]
             if make_plane
-            else [pltpu.VMEM((vec_rows, pairs), jnp.bfloat16)]
+            else [pltpu.VMEM((point_local * 16, pairs), jnp.bfloat16)] * side
         )
         + [
             folded(row_count),
@@ -518,16 +535,18 @@
             pltpu.VMEM((2, GROUP, pairs, depth), jnp.bfloat16),
             pltpu.VMEM((2, GROUP, width, pairs), jnp.bfloat16),
             pltpu.SMEM((half,), jnp.int32),
-            pltpu.SemaphoreType.DMA((9,)),
+            pltpu.SemaphoreType.DMA((10,)),
             pltpu.SemaphoreType.DMA((2, GROUP, 2)),
-            pltpu.SemaphoreType.DMA((4,)),
+            pltpu.SemaphoreType.DMA((5,)),
         ],
         compiler_params=pltpu.CompilerParams(vmem_limit_bytes=LIMIT),
         cost_estimate=pl.CostEstimate(
             flops=5 * 10**10 if side else 1, bytes_accessed=10**6, transcendentals=0
         ),
-        name="densities_mirror" if side else "densities_own",
-    )(table, *rows, *pieces, *plane, *vecs)
+        name="densities_mirror" if side else "densities_rest" if resume else "densities_own",
+    )(table, *rows, *pieces, *plane, *vecs, *begun)
+    if resume:
+        return (*result, begun[2])
     return result[:3], result[3 : 3 + n_vec], result[3 + n_vec :]
 
 
@@ -545,7 +564,7 @@
         side_refs = [take(3) for _ in range(SIDES)]
         vec_hbm = take(SIDES)
         rowvec_hbm, out_ref = take(2)
-        block_buf, vale_buf, cond_buf, vec_buf, rowvec_ref, even, odd, row_sum, col_sum = take(9)
+        block_buf, vale_buf, cond_buf, vec_buf, rowvec_ref, ready, even, odd, row_sum, col_sum = take(10)
         main_sem, shared_sem, vale_sem, cond_sem, vec_sem = take(5)
 
         own_count = side_refs[0][2][0]
@@ -608,17 +627,19 @@
 
         def screen(i):
             at = jnp.minimum(i, count - 1)
-            screened = jnp.dot(
-                vale_buf[at], block_buf[at], preferred_element_type=jnp.float32
+            lane = lax.broadcasted_iota(jnp.int32, (depth, 2 * HALF), 1)
+            begin = field(i, 2) * HALF
+            mine = (lane >= begin) & (lane < begin + rest)
+            shared = jnp.where(mine, block_buf[at, :, MAIN:].astype(jnp.float32), 0.0)
+            block = jnp.concatenate([block_buf[at, :, :MAIN], shared.astype(jnp.bfloat16)], axis=1)
+            return jnp.dot(block, cond_buf[at], preferred_element_type=jnp.float32).astype(
+                jnp.bfloat16
             )
-            lane = lax.broadcasted_iota(jnp.int32, (1, WIDE_ONE), 1)
-            begin = MAIN + field(i, 2) * HALF
-            mine = (lane < MAIN) | ((lane >= begin) & (lane < begin + rest))
-            return jnp.where(mine & (i < count), screened, 0.0).astype(jnp.bfloat16)
 
         def multiply(i, screened, into):
             at = jnp.minimum(i, count - 1)
-            into[...] = jnp.dot(screened, cond_buf[at], preferred_element_type=jnp.float32)
+            matrix = jnp.dot(vale_buf[at], screened, preferred_element_type=jnp.float32)
+            into[...] = jnp.where(i < count, matrix, 0.0)
 
         def contract(i, matrix):
             p = field(i, 0)
@@ -636,21 +657,31 @@
             for n in range(vec_count):
                 col_sum[k, n, b] += totals[n]
 
+        def arrive(i):
+            @pl.when(i < count)
+            def _():
+                arrived(i)
+
+        @pl.when(count > 0)
+        def _():
+            for i in range(2):
+                arrive(i)
+            for i in range(2):
+                ready[i] = screen(i)
+
         def two(j, carry):
             for i in range(2):
                 start(2 * j + AHEAD + i)
-            arrived(2 * j)
-
-            @pl.when(2 * j + 1 < count)
-            def _():
-                arrived(2 * j + 1)
-
-            first = screen(2 * j)
-            second = screen(2 * j + 1)
+            for i in range(2):
+                arrive(2 * j + 2 + i)
+            multiply(2 * j, ready[0], even)
+            first = screen(2 * j + 2)
             contract(2 * j - 1, odd)
-            multiply(2 * j, first, even)
-            multiply(2 * j + 1, second, odd)
+            multiply(2 * j + 1, ready[1], odd)
+            second = screen(2 * j + 3)
             contract(2 * j, even)
+            ready[0] = first
+            ready[1] = second
             return carry
 
         trips = (count + 1) // 2
@@ -696,6 +727,7 @@
             pltpu.VMEM((most, width, pairs), jnp.bfloat16),
             pltpu.VMEM((SIDES,) + vecs[0].shape, jnp.float32),
             pltpu.VMEM(row_vec.shape, jnp.float32),
+            pltpu.VMEM((2, depth, pairs), jnp.bfloat16),
             pltpu.VMEM((pairs, pairs), jnp.float32),
             pltpu.VMEM((pairs, pairs), jnp.float32),
             pltpu.VMEM((vec_count, row_count, 16, 8, pairs), jnp.float32),
@@ -724,10 +756,11 @@
 
     kind = lax.axis_index("ga") % 2
     part = lax.dynamic_slice_in_dim(orbitals, kind * NV, NV, 1)
-    part = part.reshape(point_local * NV, grid)
+    assert vec_count == point_local
     flat = lambda values: values.reshape(-1, NV * NC)
-    beside = jnp.pad(flat(vectors), ((0, point_local * (NV - vec_count)), (0, 0)))
-    fetched = swap(jnp.concatenate([part, beside], axis=1), "ka", half)
+    beside = jnp.pad(vectors, ((0, 0), (0, NV - point_local), (0, 0)))
+    part = jnp.concatenate([part, beside], axis=2).reshape(point_local * NV, -1)
+    fetched = swap(part, "ka", half)
 
     table = pair_blocks.T
     outgoing = gather_blocks(table, jnp.swapaxes(screening, 1, 2), ka_count)
@@ -738,7 +771,7 @@
     )
 
     rows = row_orbitals.reshape(row_count * bands, grid)
-    sizes = (ka_count, block_local, slice_width, wave_count, vec_count * point_local)
+    sizes = (ka_count, block_local, slice_width, wave_count, vec_count * point_local, grid)
     own, (own_vec, row_vec), plane = densities(
         0,
         table,
@@ -748,10 +781,11 @@
         (flat(vectors), flat(row_vectors)),
         sizes,
     )
-    fetched, own_vec = lax.optimization_barrier((fetched, own_vec))
+    fetched, own = lax.optimization_barrier((fetched, tuple(own)))
     passed = swap(fetched, "ga", 1)
+    own = densities(0, table, (), (), plane, (), sizes, own)
     mirrored, (mirror_vec,), _ = densities(
-        1, table, (), (fetched, passed), plane, (), sizes
+        1, table, (), (fetched, passed), plane[:4], (), sizes
     )
     row_scale = float(wave_count * NV * NC * point_local * ka_count) ** (-0.5)
     col_scale = float(wave_count * NV * NC * row_count) ** (-0.5)

time: 98.3 us -> 95.9 us (0.976)
  waiting for transfers between devices: 27.9 us -> 23 us
  starting transfers between devices: 12.9 us -> 14.4 us
    ppermute x7, waiting for transfers between devices: 27.9 us -> 19.4 us  [swap(): return lax.ppermute(values, axis, perm)]
    all_to_all x1, waiting for transfers between devices: 0.01 us -> 3.59 us  [on_device(): lax.all_to_all(outgoing, 'ka', split_axis=0, concat_axis=0, tiled=True, a...]
    ppermute x7, starting transfers between devices: 8.43 us -> 9.96 us  [swap(): return lax.ppermute(values, axis, perm)]
    pallas_call x2 -> x3, Pallas kernels: 32.3 us -> 33.7 us  [densities(): pl.pallas_call(kernel, out_shape=[jax.ShapeDtypeStruct((pair_count, pairs...]
    pallas_call x1, Pallas kernels: 13.4 us -> 12.3 us  [images(): pl.pallas_call(kernel, out_shape=jax.ShapeDtypeStruct((3 * vec_count, row...]
  transfers between devices with their start and end apart: 8 -> 8, of which waited for: 6 -> 8; matrix products, arithmetic and copies ran while one was open for 1% -> 2% of each run, Pallas kernels for 38% -> 41%
where the time goes in v4:
time: 95.9 us; the launch traced here: 95.1 us
  Pallas kernels  51 us (53%)
  waiting for transfers between devices  23 us (24%)
  starting transfers between devices  14.4 us (15%)
  local copies, waits for them, and re-layouts  3.16 us (3%)
  other arithmetic  2.79 us (3%)
    pallas_call x3, Pallas kernels, densities(): pl.pallas_call(kernel, out_shape=[jax.ShapeDtypeStruct((pair_count, pairs...  33.7 us
    ppermute x7, waiting for transfers between devices, swap(): return lax.ppermute(values, axis, perm)  19.4 us
    pallas_call x1, Pallas kernels, images(): pl.pallas_call(kernel, out_shape=jax.ShapeDtypeStruct((3 * vec_count, row...  12.3 us
    ppermute x7, starting transfers between devices, swap(): return lax.ppermute(values, axis, perm)  9.96 us
    pallas_call x1, Pallas kernels, gather_blocks(): pl.pallas_call(kernel, out_shape=jax.ShapeDtypeStruct((half, SIDES, depth...  4.99 us
    all_to_all x1, starting transfers between devices, on_device(): lax.all_to_all(outgoing, 'ka', split_axis=0, concat_axis=0, tiled=True, a...  4.48 us
    all_to_all x1, waiting for transfers between devices, on_device(): lax.all_to_all(outgoing, 'ka', split_axis=0, concat_axis=0, tiled=True, a...  3.59 us
  transfers between devices with their start and end apart: 8, of which 8 were waited for; matrix products, arithmetic and copies ran while one was open for 2% of the time, Pallas kernels for 41%

profile of v4, /device:TPU:0, one launch (start us, length us, event | category | flops | bytes accessed | tf_op | source)
XLA Modules:
  0.0 95.1 jit_solution(2530283223137154518)
XLA Ops:
  0.6 1.1 %constant_dynamic-slice_fusion = bf16[4,16,4096]{2,1,0:T(8,128)(2,1)S(1)} fusion(bf16[4,32,4096]{2,1,0:T(8,128)(2,1)} %param.7, s32[]{:T(128)S(6)} %select_n.11), kind=kLoop, calls=%fused_computation.5 | loop fusion | bytes 1048580 | tf_op jit(solution)/shard_map/dynamic_slice | solution.py:758
  1.7 0.7 fusion.1
  2.5 4.1 %collective-permute-start = (bf16[64,4352]{1,0:T(8,128)(2,1)S(1)}, bf16[64,4352]{1,0:T(8,128)(2,1)S(1)}, u32[]{:S(2)}, u32[]{:S(2)}) collective-permute-start(bf16[64,4352]{1,0:T(8,128)(2,1)S(1)} %bitcast.8), channel_id=1, source_target_pairs={{0,16},{2,18},{4,20},{6,22},{8,24},{10,26},{12,28},{14,30},{16,0},... | collective-permute-start | bytes 1671176 | tf_op jit(solution)/shard_map/ppermute | solution.py:745
  6.6 5.0 %gather_blocks.1 = bf16[8,2,152,640]{3,2,1,0:T(8,128)(2,1)} custom-call(s32[4,64]{1,0:T(4,128)} %bitcast.9, bf16[72,152,304]{2,1,0:T(8,128)(2,1)} %bitcast.5), custom_call_target="tpu_custom_call" | custom-call | tf_op jit(solution)/shard_map/gather_blocks/pallas_call | solution.py:123
  11.6 0.0 copy-start
  11.6 0.0 copy-start.1
  11.6 4.5 %all-to-all-start = ((bf16[8,2,152,640]{3,2,1,0:T(8,128)(2,1)}), bf16[8,2,152,640]{3,2,1,0:T(8,128)(2,1)}, u32[]{:S(2)}, u32[]{:S(2)}) async-start(bf16[8,2,152,640]{3,2,1,0:T(8,128)(2,1)} %gather_blocks.1), calls=%async_computation | async-start | bytes 6225920 | tf_op jit(solution)/shard_map/all_to_all | solution.py:769
  16.1 0.0 copy-done
  16.1 0.6 reshape.21.refs_3_
  16.7 0.0 copy-done.1
  16.7 0.6 reshape.22.refs_4_
  17.3 12.7 %densities_own.1 = (bf16[16,256,152]{2,1,0:T(8,128)(2,1)}, bf16[16,384,256]{2,1,0:T(8,128)(2,1)}, s32[49]{0:T(128)}, f32[16,16,256]{2,1,0:T(8,128)}, f32[16,16,2...) custom-call(s32[4,64]{1,0:T(4,128)} %bitcast.10, ...), custom_call_target="tpu_custom_call" | custom-call | flops 1 | bytes 1000000 | tf_op jit(solution)/shard_map/densities_own/pallas_call | solution.py:497
  30.0 1.2 %collective-permute-done.refs_1_ = bf16[64,4352]{1,0:T(8,128)(2,1)S(1)} collective-permute-done((bf16[64,4352]{1,0:T(8,128)(2,1)S(1)}, bf16[64,4352]{1,0:T(8,128)(2,1)S(1)}, u32[]{:S(2)}, u32[]{:S(2)}) %collective-permute-start) | collective-permute-done | bytes 557088 | tf_op jit(solution)/shard_map/ppermute | solution.py:745
  31.2 0.0 copy-start.2
  31.2 1.6 %collective-permute-start.1 = (bf16[64,4352]{1,0:T(8,128)(2,1)S(1)}, bf16[64,4352]{1,0:T(8,128)(2,1)S(1)}, u32[]{:S(2)}, u32[]{:S(2)}) collective-permute-start(bf16[64,4352]{1,0:T(8,128)(2,1)S(1)} %collective-permute-done.refs_1_), channel_id=1, source_target_pairs={{0,1},{1,0},{2,3},{3,2},{4,5},{5,4},{6,7},{7,6},{8,9},{9,8},{10,11... | collective-permute-start | bytes 1671176 | tf_op jit(solution)/shard_map/ppermute | solution.py:745
  32.8 7.0 %densities_rest.1 = (bf16[16,256,152]{2,1,0:T(8,128)(2,1)}, bf16[16,384,256]{2,1,0:T(8,128)(2,1)}) custom-call(s32[4,64]{1,0:T(4,128)} %bitcast.11, bf16[2176,152]{1,0:T(8,128)(2,1)} %get-tuple-element.28.refs_1_.refs_3_, bf16[1152,152]{1,0:T(8,128)(2,1)} %get-tuple-element.29.refs_2_.refs_4_, ...), custom_call_target="tpu_custom_call", output_to_operand_aliasing={{0}: (6, {}), {1}: (7, {})} | custom-call | flops 1 | bytes 1000000 | tf_op jit(solution)/shard_map/densities_rest/pallas_call | solution.py:497
  39.8 0.0 copy-done.2
  39.8 5.2 %collective-permute-done.1.refs_2_ = bf16[64,4352]{1,0:T(8,128)(2,1)S(1)} collective-permute-done((bf16[64,4352]{1,0:T(8,128)(2,1)S(1)}, bf16[64,4352]{1,0:T(8,128)(2,1)S(1)}, u32[]{:S(2)}, u32[]{:S(2)}) %collective-permute-start.1) | collective-permute-done | bytes 557088 | tf_op jit(solution)/shard_map/ppermute | solution.py:745
  45.0 0.0 copy-start.3
  45.0 0.8 copy-done.3
  45.8 14.0 %densities_mirror.1 = (bf16[16,256,152]{2,1,0:T(8,128)(2,1)}, bf16[16,384,256]{2,1,0:T(8,128)(2,1)}, s32[49]{0:T(128)}, f32[16,16,256]{2,1,0:T(8,128)}) custom-call(s32[4,64]{1,0:T(4,128)} %bitcast.12, bf16[64,4352]{1,0:T(8,128)(2,1)} %copy-done.2, bf16[64,4352]{1,0:T(8,128)(2,1)} %copy-done.3, bf16[2176,152]{1,0:T(8,128)(2,1)} %get-tuple-element.28.refs_1_.refs_3_, ...), custom_call_target="tpu_custom_call" | custom-call | flops 49999998976 | bytes 1000000 | tf_op jit(solution)/shard_map/densities_mirror/pallas_call | solution.py:497
  59.9 3.6 %all-to-all-done.refs_0_ = bf16[8,2,152,640]{3,2,1,0:T(8,128)(2,1)} async-done(((bf16[8,2,152,640]{3,2,1,0:T(8,128)(2,1)}), bf16[8,2,152,640]{3,2,1,0:T(8,128)(2,1)}, u32[]{:S(2)}, u32[]{:S(2)}) %all-to-all-start) | async-done | bytes 3112992 | tf_op jit(solution)/shard_map/all_to_all | solution.py:769
  63.5 12.3 %images.1 = f32[12,4,256]{2,1,0:T(4,128)} custom-call(bf16[8,2,152,640]{3,2,1,0:T(8,128)(2,1)} %all-to-all-done.refs_0_, bf16[16,256,152]{2,1,0:T(8,128)(2,1)} %get-tuple-element.39.refs_1_, bf16[16,384,256]{2,1,0:T(8,128)(2,1)} %get-tuple-element.40.refs_2_, s32[49]{0:T(128)} %get-tuple-element.38.refs_8_.refs_3_, ...), custom_call_target="tpu_custom_call" | custom-call | tf_op jit(solution)/shard_map/images/pallas_call | solution.py:719
  75.7 1.6 %collective-permute-start.2 = (f32[12,4,256]{2,1,0:T(4,128)}, f32[12,4,256]{2,1,0:T(4,128)S(1)}, u32[]{:S(2)}, u32[]{:S(2)}) collective-permute-start(f32[12,4,256]{2,1,0:T(4,128)} %images.1), channel_id=1, source_target_pairs={{0,1},{1,0},{2,3},{3,2},{4,5},{5,4},{6,7},{7,6},{8,9},{9,8},{10,11... | collective-permute-start | bytes 147464 | tf_op jit(solution)/shard_map/ppermute | solution.py:745
  77.4 2.7 %collective-permute-done.2 = f32[12,4,256]{2,1,0:T(4,128)S(1)} collective-permute-done((f32[12,4,256]{2,1,0:T(4,128)}, f32[12,4,256]{2,1,0:T(4,128)S(1)}, u32[]{:S(2)}, u32[]{:S(2)}) %collective-permute-start.2) | collective-permute-done | bytes 49184 | tf_op jit(solution)/shard_map/ppermute | solution.py:745
  80.1 0.8 add.29
  80.9 0.1 collective-permute-start.3
  81.0 4.8 %collective-permute-done.3 = f32[8,4,256]{2,1,0:T(4,128)S(1)} collective-permute-done((f32[8,4,256]{2,1,0:T(4,128)S(1)}, f32[8,4,256]{2,1,0:T(4,128)S(1)}, u32[]{:S(2)}, u32[]{:S(2)}) %collective-permute-start.3) | collective-permute-done | bytes 32800 | tf_op jit(solution)/shard_map/ppermute | solution.py:745
  85.8 0.0 collective-permute-start.4
  85.8 1.2 %collective-permute-done.4 = f32[4,4,256]{2,1,0:T(4,128)S(1)} collective-permute-done((f32[4,4,256]{2,1,0:T(4,128)S(1)}, f32[4,4,256]{2,1,0:T(4,128)S(1)}, u32[]{:S(2)}, u32[]{:S(2)}) %collective-permute-start.4) | collective-permute-done | bytes 16416 | tf_op jit(solution)/shard_map/ppermute | solution.py:745
  87.0 1.5 %collective-permute-start.5 = (f32[4,4,256]{2,1,0:T(4,128)S(1)}, f32[4,4,256]{2,1,0:T(4,128)S(1)}, u32[]{:S(2)}, u32[]{:S(2)}) collective-permute-start(f32[4,4,256]{2,1,0:T(4,128)S(1)} %add.31), channel_id=1, source_target_pairs={{0,4},{2,6},{4,0},{6,2},{8,12},{10,14},{12,8},{14,10},{16,20},{18,... | collective-permute-start | bytes 49160 | tf_op jit(solution)/shard_map/ppermute | solution.py:745
  88.5 2.2 %collective-permute-done.5 = f32[4,4,256]{2,1,0:T(4,128)S(1)} collective-permute-done((f32[4,4,256]{2,1,0:T(4,128)S(1)}, f32[4,4,256]{2,1,0:T(4,128)S(1)}, u32[]{:S(2)}, u32[]{:S(2)}) %collective-permute-start.5) | collective-permute-done | bytes 16416 | tf_op jit(solution)/shard_map/ppermute | solution.py:745
  90.8 1.1 %collective-permute-start.6 = (f32[4,4,256]{2,1,0:T(4,128)S(1)}, f32[4,4,256]{2,1,0:T(4,128)S(1)}, u32[]{:S(2)}, u32[]{:S(2)}) collective-permute-start(f32[4,4,256]{2,1,0:T(4,128)S(1)} %add.32), channel_id=1, source_target_pairs={{0,8},{2,10},{4,12},{6,14},{8,0},{10,2},{12,4},{14,6},{16,24},{18,... | collective-permute-start | bytes 49160 | tf_op jit(solution)/shard_map/ppermute | solution.py:745
  91.8 0.6 slice_add_fusion
  92.4 2.1 %collective-permute-done.6 = f32[4,4,256]{2,1,0:T(4,128)S(1)} collective-permute-done((f32[4,4,256]{2,1,0:T(4,128)S(1)}, f32[4,4,256]{2,1,0:T(4,128)S(1)}, u32[]{:S(2)}, u32[]{:S(2)}) %collective-permute-start.6) | collective-permute-done | bytes 16416 | tf_op jit(solution)/shard_map/ppermute | solution.py:745
  94.5 0.6 add.33
  (4 shorter events, 0.0 us)
Async XLA Ops:
  2.5 28.8 %collective-permute-start = (bf16[64,4352]{1,0:T(8,128)(2,1)S(1)}, bf16[64,4352]{1,0:T(8,128)(2,1)S(1)}, u32[]{:S(2)}, u32[]{:S(2)}) collective-permute-start(bf16[64,4352]{1,0:T(8,128)(2,1)S(1)} %bitcast.8), channel_id=1, source_target_pairs={{0,16},{2,18},{4,20},{6,22},{8,24},{10,26},{12,28},{14,30},{16,0},... | collective-permute-start | bytes 1671176 | tf_op jit(solution)/shard_map/ppermute | solution.py:745
  11.6 4.5 %copy-start = (bf16[4,4,256]{2,1,0:T(4,128)(2,1)S(1)}, bf16[4,4,256]{2,1,0:T(4,128)(2,1)}, u32[]{:S(2)}) copy-start(bf16[4,4,256]{2,1,0:T(4,128)(2,1)} %param.11) | copy-start | bytes 24580
  11.6 5.1 %copy-start.1 = (bf16[4,4,256]{2,1,0:T(4,128)(2,1)S(1)}, bf16[4,4,256]{2,1,0:T(4,128)(2,1)}, u32[]{:S(2)}) copy-start(bf16[4,4,256]{2,1,0:T(4,128)(2,1)} %param.10) | copy-start | bytes 24580
  11.6 51.9 %all-to-all-start = ((bf16[8,2,152,640]{3,2,1,0:T(8,128)(2,1)}), bf16[8,2,152,640]{3,2,1,0:T(8,128)(2,1)}, u32[]{:S(2)}, u32[]{:S(2)}) async-start(bf16[8,2,152,640]{3,2,1,0:T(8,128)(2,1)} %gather_blocks.1), calls=%async_computation | async-start | bytes 6225920 | tf_op jit(solution)/shard_map/all_to_all | solution.py:769
  31.2 8.6 %copy-start.2 = (bf16[64,4352]{1,0:T(8,128)(2,1)}, bf16[64,4352]{1,0:T(8,128)(2,1)S(1)}, u32[]{:S(2)}) copy-start(bf16[64,4352]{1,0:T(8,128)(2,1)S(1)} %collective-permute-done.refs_1_) | copy-start | bytes 1671172
  31.2 13.8 %collective-permute-start.1 = (bf16[64,4352]{1,0:T(8,128)(2,1)S(1)}, bf16[64,4352]{1,0:T(8,128)(2,1)S(1)}, u32[]{:S(2)}, u32[]{:S(2)}) collective-permute-start(bf16[64,4352]{1,0:T(8,128)(2,1)S(1)} %collective-permute-done.refs_1_), channel_id=1, source_target_pairs={{0,1},{1,0},{2,3},{3,2},{4,5},{5,4},{6,7},{7,6},{8,9},{9,8},{10,11... | collective-permute-start | bytes 1671176 | tf_op jit(solution)/shard_map/ppermute | solution.py:745
  45.0 0.8 copy-start.3
  75.7 4.4 %collective-permute-start.2 = (f32[12,4,256]{2,1,0:T(4,128)}, f32[12,4,256]{2,1,0:T(4,128)S(1)}, u32[]{:S(2)}, u32[]{:S(2)}) collective-permute-start(f32[12,4,256]{2,1,0:T(4,128)} %images.1), channel_id=1, source_target_pairs={{0,1},{1,0},{2,3},{3,2},{4,5},{5,4},{6,7},{7,6},{8,9},{9,8},{10,11... | collective-permute-start | bytes 147464 | tf_op jit(solution)/shard_map/ppermute | solution.py:745
  80.9 4.9 %collective-permute-start.3 = (f32[8,4,256]{2,1,0:T(4,128)S(1)}, f32[8,4,256]{2,1,0:T(4,128)S(1)}, u32[]{:S(2)}, u32[]{:S(2)}) collective-permute-start(f32[8,4,256]{2,1,0:T(4,128)S(1)} %slice.21), channel_id=1, source_target_pairs={{0,16},{2,18},{4,20},{6,22},{8,24},{10,26},{12,28},{14,30},{16,0},... | collective-permute-start | bytes 98312 | tf_op jit(solution)/shard_map/ppermute | solution.py:745
  85.8 1.2 %collective-permute-start.4 = (f32[4,4,256]{2,1,0:T(4,128)S(1)}, f32[4,4,256]{2,1,0:T(4,128)S(1)}, u32[]{:S(2)}, u32[]{:S(2)}) collective-permute-start(f32[4,4,256]{2,1,0:T(4,128)S(1)} %slice_add_fusion.1), channel_id=1, source_target_pairs={{0,2},{2,0},{4,6},{6,4},{8,10},{10,8},{12,14},{14,12},{16,18},{18,... | collective-permute-start | bytes 49160 | tf_op jit(solution)/shard_map/ppermute | solution.py:745
  87.0 3.7 %collective-permute-start.5 = (f32[4,4,256]{2,1,0:T(4,128)S(1)}, f32[4,4,256]{2,1,0:T(4,128)S(1)}, u32[]{:S(2)}, u32[]{:S(2)}) collective-permute-start(f32[4,4,256]{2,1,0:T(4,128)S(1)} %add.31), channel_id=1, source_target_pairs={{0,4},{2,6},{4,0},{6,2},{8,12},{10,14},{12,8},{14,10},{16,20},{18,... | collective-permute-start | bytes 49160 | tf_op jit(solution)/shard_map/ppermute | solution.py:745
  90.8 3.7 %collective-permute-start.6 = (f32[4,4,256]{2,1,0:T(4,128)S(1)}, f32[4,4,256]{2,1,0:T(4,128)S(1)}, u32[]{:S(2)}, u32[]{:S(2)}) collective-permute-start(f32[4,4,256]{2,1,0:T(4,128)S(1)} %add.32), channel_id=1, source_target_pairs={{0,8},{2,10},{4,12},{6,14},{8,0},{10,2},{12,4},{14,6},{16,24},{18,... | collective-permute-start | bytes 49160 | tf_op jit(solution)/shard_map/ppermute | solution.py:745

commit v5 on v4

--- a/solution.py
+++ b/solution.py
@@ -19,6 +19,7 @@
 GROUP = 2
 SPLIT = 3
 LIMIT = 62 << 20
+WHOLE = (63 << 20) + (3 << 18)
 TAIL = 128
 CHUNK = 512
 NT = (((1,), (1,)), ((), ()))
@@ -539,7 +540,7 @@
             pltpu.SemaphoreType.DMA((2, GROUP, 2)),
             pltpu.SemaphoreType.DMA((5,)),
         ],
-        compiler_params=pltpu.CompilerParams(vmem_limit_bytes=LIMIT),
+        compiler_params=pltpu.CompilerParams(vmem_limit_bytes=LIMIT if make_plane else WHOLE),
         cost_estimate=pl.CostEstimate(
             flops=5 * 10**10 if side else 1, bytes_accessed=10**6, transcendentals=0
         ),
@@ -799,16 +800,20 @@
         col_scale,
         wave_count,
     )
-    step = 1
+    step = 2
     while step < ga_count:
         part = part + swap(part, "ga", step)
         step *= 2
-    column = part[:vec_count]
-    row = part[vec_count:]
-    other = swap(row, "ka", half)
-    row = row[:vec_count] + other[:vec_count]
-    other, row = lax.optimization_barrier((other, row))
-    column = column + other[vec_count:]
+    total = ka_count * ga_count
+    across = [(i, (i ^ 1 ^ half * ga_count)) for i in range(total)]
+    beside = swap(part, "ga", 1)
+    opposite = swap(part, "ka", half)
+    corner = lax.ppermute(part, ("ka", "ga"), across)
+    other = opposite[vec_count:] + corner[vec_count:]
+    near = part + beside
+    row = near[vec_count : 2 * vec_count] + other[:vec_count]
+    near, other, row = lax.optimization_barrier((near, other, row))
+    column = near[:vec_count] + other[vec_count:]
     step = 1
     while step < half:
         row = row + swap(row, "ka", step)

time: 95.9 us -> 94.7 us (0.987)
  Pallas kernels: 51 us -> 44.2 us
  waiting for transfers between devices: 23 us -> 28.9 us
  starting transfers between devices: 14.4 us -> 15.5 us
    pallas_call x3, Pallas kernels: 33.7 us -> 28.5 us  [densities(): pl.pallas_call(kernel, out_shape=[jax.ShapeDtypeStruct((pair_count, pairs...]
    ppermute x7, waiting for transfers between devices: 19.4 us -> 22.7 us  [swap(): return lax.ppermute(values, axis, perm)]
    ppermute x0 -> x1, starting transfers between devices: none -> 3.27 us  [on_device(): corner = lax.ppermute(part, ('ka', 'ga'), across)]
    ppermute x0 -> x1, waiting for transfers between devices: none -> 2.3 us  [on_device(): corner = lax.ppermute(part, ('ka', 'ga'), across)]
    ppermute x7, starting transfers between devices: 9.96 us -> 7.75 us  [swap(): return lax.ppermute(values, axis, perm)]
    pallas_call x1, Pallas kernels: 12.3 us -> 10.8 us  [images(): pl.pallas_call(kernel, out_shape=jax.ShapeDtypeStruct((3 * vec_count, row...]
  transfers between devices with their start and end apart: 8 -> 9, of which waited for: 8 -> 8; matrix products, arithmetic and copies ran while one was open for 2% -> 3% of each run, Pallas kernels for 41% -> 35%
where the time goes in v5:
time: 94.7 us; the launch traced here: 94.5 us
  Pallas kernels  44.2 us (47%)
  waiting for transfers between devices  28.9 us (31%)
  starting transfers between devices  15.5 us (16%)
  other arithmetic  2.84 us (3%)
  local copies, waits for them, and re-layouts  2.31 us (2%)
    pallas_call x3, Pallas kernels, densities(): pl.pallas_call(kernel, out_shape=[jax.ShapeDtypeStruct((pair_count, pairs...  28.5 us
    ppermute x7, waiting for transfers between devices, swap(): return lax.ppermute(values, axis, perm)  22.7 us
    pallas_call x1, Pallas kernels, images(): pl.pallas_call(kernel, out_shape=jax.ShapeDtypeStruct((3 * vec_count, row...  10.8 us
    ppermute x7, starting transfers between devices, swap(): return lax.ppermute(values, axis, perm)  7.75 us
    pallas_call x1, Pallas kernels, gather_blocks(): pl.pallas_call(kernel, out_shape=jax.ShapeDtypeStruct((half, SIDES, depth...  4.84 us
    all_to_all x1, starting transfers between devices, on_device(): lax.all_to_all(outgoing, 'ka', split_axis=0, concat_axis=0, tiled=True, a...  4.48 us
    all_to_all x1, waiting for transfers between devices, on_device(): lax.all_to_all(outgoing, 'ka', split_axis=0, concat_axis=0, tiled=True, a...  3.82 us
    ppermute x1, starting transfers between devices, on_device(): corner = lax.ppermute(part, ('ka', 'ga'), across)  3.27 us
  transfers between devices with their start and end apart: 9, of which 8 were waited for; matrix products, arithmetic and copies ran while one was open for 3% of the time, Pallas kernels for 35%

profile of v5, /device:TPU:0, one launch (start us, length us, event | category | flops | bytes accessed | tf_op | source)
XLA Modules:
  0.0 94.5 jit_solution(3530015792964805012)
XLA Ops:
  0.6 1.1 %constant_dynamic-slice_fusion = bf16[4,16,4096]{2,1,0:T(8,128)(2,1)S(1)} fusion(bf16[4,32,4096]{2,1,0:T(8,128)(2,1)} %param.7, s32[]{:T(128)S(6)} %select_n.11), kind=kLoop, calls=%fused_computation.6 | loop fusion | bytes 1048580 | tf_op jit(solution)/shard_map/dynamic_slice | solution.py:759
  1.7 0.7 fusion.1
  2.5 4.1 %collective-permute-start = (bf16[64,4352]{1,0:T(8,128)(2,1)S(1)}, bf16[64,4352]{1,0:T(8,128)(2,1)}, u32[]{:S(2)}, u32[]{:S(2)}) collective-permute-start(bf16[64,4352]{1,0:T(8,128)(2,1)S(1)} %bitcast.8), channel_id=1, source_target_pairs={{0,16},{2,18},{4,20},{6,22},{8,24},{10,26},{12,28},{14,30},{16,0},... | collective-permute-start | bytes 1671176 | tf_op jit(solution)/shard_map/ppermute | solution.py:746
  6.6 4.8 %gather_blocks.1 = bf16[8,2,152,640]{3,2,1,0:T(8,128)(2,1)} custom-call(s32[4,64]{1,0:T(4,128)} %bitcast.9, bf16[72,152,304]{2,1,0:T(8,128)(2,1)} %bitcast.5), custom_call_target="tpu_custom_call" | custom-call | tf_op jit(solution)/shard_map/gather_blocks/pallas_call | solution.py:124
  11.4 0.0 copy-start
  11.4 0.0 copy-start.1
  11.4 4.5 %all-to-all-start = ((bf16[8,2,152,640]{3,2,1,0:T(8,128)(2,1)}), bf16[8,2,152,640]{3,2,1,0:T(8,128)(2,1)}, u32[]{:S(2)}, u32[]{:S(2)}) async-start(bf16[8,2,152,640]{3,2,1,0:T(8,128)(2,1)} %gather_blocks.1), calls=%async_computation | async-start | bytes 6225920 | tf_op jit(solution)/shard_map/all_to_all | solution.py:770
  15.9 0.0 copy-done
  15.9 0.6 reshape.21.refs_3_
  16.6 0.0 copy-done.1
  16.6 0.6 reshape.22.refs_4_
  17.2 10.5 %densities_own.1 = (bf16[16,256,152]{2,1,0:T(8,128)(2,1)}, bf16[16,384,256]{2,1,0:T(8,128)(2,1)}, s32[49]{0:T(128)}, f32[16,16,256]{2,1,0:T(8,128)}, f32[16,16,2...) custom-call(s32[4,64]{1,0:T(4,128)} %bitcast.10, ...), custom_call_target="tpu_custom_call" | custom-call | flops 1 | bytes 1000000 | tf_op jit(solution)/shard_map/densities_own/pallas_call | solution.py:498
  27.7 3.7 %collective-permute-done.refs_1_ = bf16[64,4352]{1,0:T(8,128)(2,1)} collective-permute-done((bf16[64,4352]{1,0:T(8,128)(2,1)S(1)}, bf16[64,4352]{1,0:T(8,128)(2,1)}, u32[]{:S(2)}, u32[]{:S(2)}) %collective-permute-start) | collective-permute-done | bytes 557088 | tf_op jit(solution)/shard_map/ppermute | solution.py:746
  31.3 1.6 %collective-permute-start.1 = (bf16[64,4352]{1,0:T(8,128)(2,1)}, bf16[64,4352]{1,0:T(8,128)(2,1)}, u32[]{:S(2)}, u32[]{:S(2)}) collective-permute-start(bf16[64,4352]{1,0:T(8,128)(2,1)} %collective-permute-done.refs_1_), channel_id=1, source_target_pairs={{0,1},{1,0},{2,3},{3,2},{4,5},{5,4},{6,7},{7,6},{8,9},{9,8},{10,11... | collective-permute-start | bytes 1671176 | tf_op jit(solution)/shard_map/ppermute | solution.py:746
  32.9 4.0 %densities_rest.1 = (bf16[16,256,152]{2,1,0:T(8,128)(2,1)}, bf16[16,384,256]{2,1,0:T(8,128)(2,1)}) custom-call(s32[4,64]{1,0:T(4,128)} %bitcast.11, bf16[2176,152]{1,0:T(8,128)(2,1)} %get-tuple-element.29.refs_1_.refs_3_, bf16[1152,152]{1,0:T(8,128)(2,1)} %get-tuple-element.30.refs_2_.refs_4_, ...), custom_call_target="tpu_custom_call", output_to_operand_aliasing={{0}: (6, {}), {1}: (7, {})} | custom-call | flops 1 | bytes 1000000 | tf_op jit(solution)/shard_map/densities_rest/pallas_call | solution.py:498
  36.9 8.5 %collective-permute-done.1.refs_2_ = bf16[64,4352]{1,0:T(8,128)(2,1)} collective-permute-done((bf16[64,4352]{1,0:T(8,128)(2,1)}, bf16[64,4352]{1,0:T(8,128)(2,1)}, u32[]{:S(2)}, u32[]{:S(2)}) %collective-permute-start.1) | collective-permute-done | bytes 557088 | tf_op jit(solution)/shard_map/ppermute | solution.py:746
  45.4 14.1 %densities_mirror.1 = (bf16[16,256,152]{2,1,0:T(8,128)(2,1)}, bf16[16,384,256]{2,1,0:T(8,128)(2,1)}, s32[49]{0:T(128)}, f32[16,16,256]{2,1,0:T(8,128)}) custom-call(s32[4,64]{1,0:T(4,128)} %bitcast.12, bf16[64,4352]{1,0:T(8,128)(2,1)} %collective-permute-done.refs_1_, bf16[64,4352]{1,0:T(8,128)(2,1)} %collective-permute-done.1.refs_2_, ...), custom_call_target="tpu_custom_call" | custom-call | flops 49999998976 | bytes 1000000 | tf_op jit(solution)/shard_map/densities_mirror/pallas_call | solution.py:498
  59.5 3.8 %all-to-all-done.refs_0_ = bf16[8,2,152,640]{3,2,1,0:T(8,128)(2,1)} async-done(((bf16[8,2,152,640]{3,2,1,0:T(8,128)(2,1)}), bf16[8,2,152,640]{3,2,1,0:T(8,128)(2,1)}, u32[]{:S(2)}, u32[]{:S(2)}) %all-to-all-start) | async-done | bytes 3112992 | tf_op jit(solution)/shard_map/all_to_all | solution.py:770
  63.3 10.8 %images.1 = f32[12,4,256]{2,1,0:T(4,128)} custom-call(bf16[8,2,152,640]{3,2,1,0:T(8,128)(2,1)} %all-to-all-done.refs_0_, bf16[16,256,152]{2,1,0:T(8,128)(2,1)} %get-tuple-element.40.refs_1_, bf16[16,384,256]{2,1,0:T(8,128)(2,1)} %get-tuple-element.41.refs_2_, s32[49]{0:T(128)} %get-tuple-element.39.refs_8_.refs_3_, ...), custom_call_target="tpu_custom_call" | custom-call | tf_op jit(solution)/shard_map/images/pallas_call | solution.py:720
  74.2 1.6 %collective-permute-start.2 = (f32[12,4,256]{2,1,0:T(4,128)}, f32[12,4,256]{2,1,0:T(4,128)S(1)}, u32[]{:S(2)}, u32[]{:S(2)}) collective-permute-start(f32[12,4,256]{2,1,0:T(4,128)} %images.1), channel_id=1, source_target_pairs={{0,1},{1,0},{2,3},{3,2},{4,5},{5,4},{6,7},{7,6},{8,9},{9,8},{10,11... | collective-permute-start | bytes 147464 | tf_op jit(solution)/shard_map/ppermute | solution.py:746
  75.8 3.3 %collective-permute-start.4 = (f32[12,4,256]{2,1,0:T(4,128)}, f32[12,4,256]{2,1,0:T(4,128)S(1)}, u32[]{:S(2)}, u32[]{:S(2)}) collective-permute-start(f32[12,4,256]{2,1,0:T(4,128)} %images.1), channel_id=1, source_target_pairs={{0,17},{1,16},{2,19},{3,18},{4,21},{5,20},{6,23},{7,22},{8,25},{9,... | collective-permute-start | bytes 147464 | tf_op jit(solution)/shard_map/ppermute | solution.py:811
  79.1 0.3 collective-permute-start.3
  79.4 0.0 collective-permute-done.2
  79.4 0.8 add.32
  80.2 2.3 %collective-permute-done.4 = f32[12,4,256]{2,1,0:T(4,128)S(1)} collective-permute-done((f32[12,4,256]{2,1,0:T(4,128)}, f32[12,4,256]{2,1,0:T(4,128)S(1)}, u32[]{:S(2)}, u32[]{:S(2)}) %collective-permute-start.4) | collective-permute-done | bytes 49184 | tf_op jit(solution)/shard_map/ppermute | solution.py:811
  82.5 2.6 %collective-permute-done.3 = f32[12,4,256]{2,1,0:T(4,128)S(1)} collective-permute-done((f32[12,4,256]{2,1,0:T(4,128)}, f32[12,4,256]{2,1,0:T(4,128)S(1)}, u32[]{:S(2)}, u32[]{:S(2)}) %collective-permute-start.3) | collective-permute-done | bytes 49184 | tf_op jit(solution)/shard_map/ppermute | solution.py:746
  85.1 0.1 collective-permute-start.5
  85.2 1.2 %collective-permute-done.5 = f32[4,4,256]{2,1,0:T(4,128)S(1)} collective-permute-done((f32[4,4,256]{2,1,0:T(4,128)S(1)}, f32[4,4,256]{2,1,0:T(4,128)S(1)}, u32[]{:S(2)}, u32[]{:S(2)}) %collective-permute-start.5) | collective-permute-done | bytes 16416 | tf_op jit(solution)/shard_map/ppermute | solution.py:746
  86.4 0.1 collective-permute-start.6
  86.5 3.6 %collective-permute-done.6 = f32[4,4,256]{2,1,0:T(4,128)S(1)} collective-permute-done((f32[4,4,256]{2,1,0:T(4,128)S(1)}, f32[4,4,256]{2,1,0:T(4,128)S(1)}, u32[]{:S(2)}, u32[]{:S(2)}) %collective-permute-start.6) | collective-permute-done | bytes 16416 | tf_op jit(solution)/shard_map/ppermute | solution.py:746
  90.1 0.0 collective-permute-start.7
  90.1 0.6 slice_add_fusion.2
  90.7 3.1 %collective-permute-done.7 = f32[4,4,256]{2,1,0:T(4,128)S(1)} collective-permute-done((f32[4,4,256]{2,1,0:T(4,128)S(1)}, f32[4,4,256]{2,1,0:T(4,128)S(1)}, u32[]{:S(2)}, u32[]{:S(2)}) %collective-permute-start.7) | collective-permute-done | bytes 16416 | tf_op jit(solution)/shard_map/ppermute | solution.py:746
  93.9 0.6 add.37
  (4 shorter events, 0.0 us)
Async XLA Ops:
  2.5 28.9 %collective-permute-start = (bf16[64,4352]{1,0:T(8,128)(2,1)S(1)}, bf16[64,4352]{1,0:T(8,128)(2,1)}, u32[]{:S(2)}, u32[]{:S(2)}) collective-permute-start(bf16[64,4352]{1,0:T(8,128)(2,1)S(1)} %bitcast.8), channel_id=1, source_target_pairs={{0,16},{2,18},{4,20},{6,22},{8,24},{10,26},{12,28},{14,30},{16,0},... | collective-permute-start | bytes 1671176 | tf_op jit(solution)/shard_map/ppermute | solution.py:746
  11.4 4.5 %copy-start = (bf16[4,4,256]{2,1,0:T(4,128)(2,1)S(1)}, bf16[4,4,256]{2,1,0:T(4,128)(2,1)}, u32[]{:S(2)}) copy-start(bf16[4,4,256]{2,1,0:T(4,128)(2,1)} %param.11) | copy-start | bytes 24580
  11.4 5.1 %copy-start.1 = (bf16[4,4,256]{2,1,0:T(4,128)(2,1)S(1)}, bf16[4,4,256]{2,1,0:T(4,128)(2,1)}, u32[]{:S(2)}) copy-start(bf16[4,4,256]{2,1,0:T(4,128)(2,1)} %param.10) | copy-start | bytes 24580
  11.4 51.9 %all-to-all-start = ((bf16[8,2,152,640]{3,2,1,0:T(8,128)(2,1)}), bf16[8,2,152,640]{3,2,1,0:T(8,128)(2,1)}, u32[]{:S(2)}, u32[]{:S(2)}) async-start(bf16[8,2,152,640]{3,2,1,0:T(8,128)(2,1)} %gather_blocks.1), calls=%async_computation | async-start | bytes 6225920 | tf_op jit(solution)/shard_map/all_to_all | solution.py:770
  31.3 14.1 %collective-permute-start.1 = (bf16[64,4352]{1,0:T(8,128)(2,1)}, bf16[64,4352]{1,0:T(8,128)(2,1)}, u32[]{:S(2)}, u32[]{:S(2)}) collective-permute-start(bf16[64,4352]{1,0:T(8,128)(2,1)} %collective-permute-done.refs_1_), channel_id=1, source_target_pairs={{0,1},{1,0},{2,3},{3,2},{4,5},{5,4},{6,7},{7,6},{8,9},{9,8},{10,11... | collective-permute-start | bytes 1671176 | tf_op jit(solution)/shard_map/ppermute | solution.py:746
  74.2 5.2 %collective-permute-start.2 = (f32[12,4,256]{2,1,0:T(4,128)}, f32[12,4,256]{2,1,0:T(4,128)S(1)}, u32[]{:S(2)}, u32[]{:S(2)}) collective-permute-start(f32[12,4,256]{2,1,0:T(4,128)} %images.1), channel_id=1, source_target_pairs={{0,1},{1,0},{2,3},{3,2},{4,5},{5,4},{6,7},{7,6},{8,9},{9,8},{10,11... | collective-permute-start | bytes 147464 | tf_op jit(solution)/shard_map/ppermute | solution.py:746
  75.8 6.7 %collective-permute-start.4 = (f32[12,4,256]{2,1,0:T(4,128)}, f32[12,4,256]{2,1,0:T(4,128)S(1)}, u32[]{:S(2)}, u32[]{:S(2)}) collective-permute-start(f32[12,4,256]{2,1,0:T(4,128)} %images.1), channel_id=1, source_target_pairs={{0,17},{1,16},{2,19},{3,18},{4,21},{5,20},{6,23},{7,22},{8,25},{9,... | collective-permute-start | bytes 147464 | tf_op jit(solution)/shard_map/ppermute | solution.py:811
  79.1 6.0 %collective-permute-start.3 = (f32[12,4,256]{2,1,0:T(4,128)}, f32[12,4,256]{2,1,0:T(4,128)S(1)}, u32[]{:S(2)}, u32[]{:S(2)}) collective-permute-start(f32[12,4,256]{2,1,0:T(4,128)} %images.1), channel_id=1, source_target_pairs={{0,16},{2,18},{4,20},{6,22},{8,24},{10,26},{12,28},{14,30},{16,0},... | collective-permute-start | bytes 147464 | tf_op jit(solution)/shard_map/ppermute | solution.py:746
  85.1 1.2 %collective-permute-start.5 = (f32[4,4,256]{2,1,0:T(4,128)S(1)}, f32[4,4,256]{2,1,0:T(4,128)S(1)}, u32[]{:S(2)}, u32[]{:S(2)}) collective-permute-start(f32[4,4,256]{2,1,0:T(4,128)S(1)} %slice_add_fusion.1), channel_id=1, source_target_pairs={{0,2},{2,0},{4,6},{6,4},{8,10},{10,8},{12,14},{14,12},{16,18},{18,... | collective-permute-start | bytes 49160 | tf_op jit(solution)/shard_map/ppermute | solution.py:746
  86.4 3.7 %collective-permute-start.6 = (f32[4,4,256]{2,1,0:T(4,128)S(1)}, f32[4,4,256]{2,1,0:T(4,128)S(1)}, u32[]{:S(2)}, u32[]{:S(2)}) collective-permute-start(f32[4,4,256]{2,1,0:T(4,128)S(1)} %add.35), channel_id=1, source_target_pairs={{0,4},{2,6},{4,0},{6,2},{8,12},{10,14},{12,8},{14,10},{16,20},{18,... | collective-permute-start | bytes 49160 | tf_op jit(solution)/shard_map/ppermute | solution.py:746
  90.1 3.7 %collective-permute-start.7 = (f32[4,4,256]{2,1,0:T(4,128)S(1)}, f32[4,4,256]{2,1,0:T(4,128)S(1)}, u32[]{:S(2)}, u32[]{:S(2)}) collective-permute-start(f32[4,4,256]{2,1,0:T(4,128)S(1)} %add.36), channel_id=1, source_target_pairs={{0,8},{2,10},{4,12},{6,14},{8,0},{10,2},{12,4},{14,6},{16,24},{18,... | collective-permute-start | bytes 49160 | tf_op jit(solution)/shard_map/ppermute | solution.py:746
